TPU v7x, 32 devices: a whole 2x2x4 slice. The times are simulated.
32 devices in a mesh: groups: 2 (over y), adapter: 8 (over z, x), tensor: 2 (over core).
Axes of the slice: x: 2, y: 2, z: 4, core: 2. Of those that a mesh axis runs over, the one named last changes fastest.
Arguments:
- layer_input: bfloat16 [256, 8192], P(('groups', 'adapter')), parts along dimension 0, may hold values from -6 to 6
- input_norm_gain: float32 [8192], replicated, may hold values from 0.5 to 1.5
- query_projection: bfloat16 [8192, 512], P(None, 'tensor'), may hold values from -0.0625 to 0.0625
- key_projection: bfloat16 [8192, 128], P(None, 'tensor'), may hold values from -0.0625 to 0.0625
- value_projection: bfloat16 [8192, 128], P(None, 'tensor'), may hold values from -0.0625 to 0.0625
- output_projection: bfloat16 [512, 8192], P('tensor'), may hold values from -1 to 1
- cached_key_rows: bfloat16 [256, 32, 128], P(('groups', 'adapter')), parts along dimension 0, may hold values from -120 to 120
- cached_value_rows: bfloat16 [256, 32, 128], P(('groups', 'adapter')), parts along dimension 0, may hold values from -6 to 6
- request_adapter: int32 [256, 1], P(('groups', 'adapter')), parts along dimension 0, may hold values from 0 to 7; in each aligned block of 16 rows (0 to 15, 16 to 31, ...) at most 4 rows name the same one
- adapter_row_table: int32 [8], replicated, may hold values from 0 to 7, each once
- cached_length: int32 [256], P(('groups', 'adapter')), parts along dimension 0, may hold values from 1 to 32, as said below
- projection_adapter_down: bfloat16 [8, 8192, 192], P('adapter', 'tensor'), may hold values from -0.0625 to 0.0625
- query_adapter_up: bfloat16 [8, 64, 512], P('adapter', None, 'tensor'), may hold values from -0.75 to 0.75
- key_value_adapter_up: bfloat16 [8, 2, 64, 128], P('adapter', None, None, 'tensor'), may hold values from -0.75 to 0.75
- output_adapter_down: bfloat16 [8, 512, 64], P('adapter', 'tensor'), may hold values from -1 to 1
- output_adapter_up: bfloat16 [8, 64, 8192], P('adapter', None, 'tensor'), may hold values from -0.75 to 0.75
Outputs:
- block_out: bfloat16 [256, 8192], P(('groups', 'adapter'), 'tensor'), parts along dimension 0
There are 2 independent parts, one for each index of `groups`. A program takes and returns all parts, laid end to end along the dimension named above; an argument that names none is the same for every part. Nothing has to cross between parts.
Inputs may be any that keep to these rules, and one draw needn't show every extreme that they name: `request_adapter`: among the requests of one device (aligned blocks of 16 rows) no adapter is named more than 4 times, a bound that some block reaches. A permutation: adapter j's weights are row adapter_row_table[j] of the adapter arrays. `cached_length`: the requests of every device include one whose cache holds exactly 32 positions.
All inputs are finite; a program needn't handle non-finite values.
Results may differ from a plain program's by a relative error of at most 0.012.
The roundings to bfloat16 on the way count: a program that leaves them out, or rounds other values in their place, can miss the bound.
Values may be sent and summed in bfloat16 or wider, within the bound.
No kernel may reach another device: no remote copies, remote signals or barrier semaphores. Data moves between devices by JAX's collectives and lax.ppermute only.
A program may use at most 64 MiB of HBM per device.

v0:
```python
import math

import jax
import jax.numpy as jnp
from jax import lax
from jax.sharding import PartitionSpec as P

HEAD_SIZE = 128


EPSILON = 1e-05
THETA = 500000.0


def rotary(input_batch, positions):
    halfway = input_batch.shape[-1] // 2
    frequency = THETA ** (-jnp.arange(halfway, dtype=jnp.float32) / halfway)
    angles = positions.astype(jnp.float32)[:, None, None] * frequency[None, None, :]
    cosine = jnp.cos(angles)
    sine = jnp.sin(angles)
    leading = input_batch[..., :halfway]
    trailing = input_batch[..., halfway:]
    return jnp.concatenate(
        [leading * cosine - trailing * sine, trailing * cosine + leading * sine], axis=-1
    )


def rms_normed(layer_input, input_norm_gain):
    floats = layer_input.astype(jnp.float32)
    mean_square = jnp.mean(floats * floats, axis=1, keepdims=True)
    return (floats * lax.rsqrt(mean_square + EPSILON) * input_norm_gain[None, :]).astype(
        jnp.bfloat16
    )


def rank_terms(buffer, first):
    return jnp.einsum("sacd,adr->sacr", buffer, first, preferred_element_type=jnp.float32)


def body(
    layer_input,
    input_norm_gain,
    query_projection,
    key_projection,
    value_projection,
    output_projection,
    cached_key_rows,
    cached_value_rows,
    request_adapter,
    adapter_row_table,
    cached_length,
    projection_adapter_down,
    query_adapter_up,
    key_value_adapter_up,
    output_adapter_down,
    output_adapter_up,
):
    requests = layer_input.shape[0]
    owners = lax.axis_size("adapter")
    locally_kept = projection_adapter_down.shape[0]
    adapters = adapter_row_table.shape[0]
    capacity = max(2, 2 * ((requests + adapters - 1) // adapters))
    total_slots = owners * locally_kept * capacity
    qcols = query_projection.shape[1]
    kcols = key_projection.shape[1]
    heads_here = qcols // HEAD_SIZE
    adapter_rank_width = query_adapter_up.shape[1]
    normalized_input = rms_normed(layer_input, input_norm_gain)
    projected_q = jnp.dot(normalized_input, query_projection, preferred_element_type=jnp.float32)
    projected_k = jnp.dot(normalized_input, key_projection, preferred_element_type=jnp.float32)
    projected_v = jnp.dot(normalized_input, value_projection, preferred_element_type=jnp.float32)
    identity = jnp.arange(adapters, dtype=jnp.int32)
    adapter_slots = jnp.sum(
        jnp.where(request_adapter == identity[None, :], adapter_row_table[None, :], 0), axis=1
    )
    owner_of = adapter_slots // locally_kept
    within = adapter_slots % locally_kept
    request_order = jnp.arange(requests, dtype=jnp.int32)
    earlier = (adapter_slots[:, None] == adapter_slots[None, :]) & (
        request_order[None, :] < request_order[:, None]
    )
    standing = jnp.sum(earlier.astype(jnp.int32), axis=1)
    target = owner_of * (locally_kept * capacity) + within * capacity + standing
    slot_order = jnp.arange(total_slots, dtype=jnp.int32)
    placing = (slot_order[:, None] == target[None, :]).astype(jnp.bfloat16)
    picking = (target[:, None] == slot_order[None, :]).astype(jnp.bfloat16)

    def dispatch(input_batch):
        placed = jnp.dot(placing, input_batch, preferred_element_type=jnp.float32).astype(
            jnp.bfloat16
        )
        return placed.reshape(owners, locally_kept, capacity, input_batch.shape[1])

    def collect(returned):
        return jnp.dot(
            picking, returned.reshape(total_slots, -1), preferred_element_type=jnp.float32
        )

    complete_first_matrices = lax.all_gather(projection_adapter_down, "tensor", axis=1, tiled=True)
    sent = dispatch(normalized_input)
    rank_activations = rank_terms(
        lax.all_to_all(sent, "adapter", split_axis=0, concat_axis=0, tiled=True),
        complete_first_matrices,
    ).astype(jnp.bfloat16)
    lead = rank_activations.shape[:3]
    query_update = jnp.einsum(
        "buki,uih->bukh",
        rank_activations[..., :adapter_rank_width],
        query_adapter_up,
        preferred_element_type=jnp.float32,
    )
    key_value_rank_input = rank_activations[..., adapter_rank_width:].reshape(
        lead + (2, adapter_rank_width)
    )
    key_value_update = jnp.einsum(
        "mnoey,neyb->mnoeb",
        key_value_rank_input,
        key_value_adapter_up,
        preferred_element_type=jnp.float32,
    )
    change = jnp.concatenate(
        [
            query_update.astype(jnp.bfloat16),
            key_value_update.astype(jnp.bfloat16).reshape(lead + (2 * kcols,)),
        ],
        axis=3,
    )
    returned_qkv = lax.all_to_all(change, "adapter", split_axis=0, concat_axis=0, tiled=True)
    qkv_change = collect(returned_qkv)
    key_part = projected_k + qkv_change[:, qcols : qcols + kcols]
    value_part = projected_v + qkv_change[:, qcols + kcols :]
    key_whole, value_whole = (
        lax.all_gather(key_part, "tensor", axis=1, tiled=True),
        lax.all_gather(value_part, "tensor", axis=1, tiled=True),
    )
    queries = rotary(
        (projected_q + qkv_change[:, :qcols]).reshape(requests, heads_here, HEAD_SIZE),
        cached_length,
    ).astype(jnp.bfloat16)
    own_keys = rotary(key_whole.reshape(requests, 1, HEAD_SIZE), cached_length)[:, 0].astype(
        jnp.bfloat16
    )
    own_values = value_whole.astype(jnp.bfloat16)
    positions = cached_key_rows.shape[1]
    scores = jnp.einsum(
        "nhd,nld->nhl", queries, cached_key_rows, preferred_element_type=jnp.float32
    ) / math.sqrt(HEAD_SIZE)
    own_score = jnp.einsum(
        "nhd,nd->nh", queries, own_keys, preferred_element_type=jnp.float32
    ) / math.sqrt(HEAD_SIZE)
    visible = jnp.arange(positions, dtype=jnp.int32)[None, :] < cached_length[:, None]
    scores = jnp.where(visible[:, None, :], scores, -jnp.inf)
    highest = jnp.maximum(jnp.max(scores, axis=2), own_score)
    raised = jnp.exp(scores - highest[:, :, None])
    own_raised = jnp.exp(own_score - highest)
    total = jnp.sum(raised, axis=2) + own_raised
    weights = (raised / total[:, :, None]).astype(jnp.bfloat16)
    own_weight = (own_raised / total).astype(jnp.bfloat16)
    attention_output = jnp.einsum(
        "nhl,nld->nhd", weights, cached_value_rows, preferred_element_type=jnp.float32
    )
    attention_output = (
        attention_output
        + own_weight.astype(jnp.float32)[:, :, None] * own_values.astype(jnp.float32)[:, None, :]
    )
    attention_output = attention_output.reshape(requests, qcols).astype(jnp.bfloat16)
    summed = lax.psum(
        rank_terms(
            lax.all_to_all(
                dispatch(attention_output), "adapter", split_axis=0, concat_axis=0, tiled=True
            ),
            output_adapter_down,
        ),
        "tensor",
    )
    change = jnp.einsum(
        "sacr,ard->sacd",
        summed.astype(jnp.bfloat16),
        output_adapter_up,
        preferred_element_type=jnp.float32,
    )
    returned_out = lax.all_to_all(
        change.astype(jnp.bfloat16), "adapter", split_axis=0, concat_axis=0, tiled=True
    )
    out_change = collect(returned_out)
    head_terms = jnp.dot(attention_output, output_projection, preferred_element_type=jnp.float32)
    reduced = lax.psum_scatter(head_terms, "tensor", scatter_dimension=1, tiled=True)
    return (reduced + out_change).astype(jnp.bfloat16)


def solution(mesh):
    placed = (
        P(("groups", "adapter"), None),
        P(),
        P(None, "tensor"),
        P(None, "tensor"),
        P(None, "tensor"),
        P("tensor", None),
        P(("groups", "adapter"), None, None),
        P(("groups", "adapter"), None, None),
        P(("groups", "adapter"), None),
        P(),
        P(("groups", "adapter")),
        P("adapter", "tensor", None),
        P("adapter", None, "tensor"),
        P("adapter", None, None, "tensor"),
        P("adapter", "tensor", None),
        P("adapter", None, "tensor"),
    )
    return jax.shard_map(
        body,
        mesh=mesh,
        in_specs=placed,
        out_specs=P(("groups", "adapter"), "tensor"),
        check_vma=False,
    )
```

profile of v0, /device:TPU:0, one launch (start us, length us, event | category | flops | bytes accessed | tf_op | source)
XLA Modules:
  0.0 94.5 jit_solution(1822067422329924771)
XLA Ops:
  6.6 0.0 all-gather.4.cloned.1.call-start
  6.6 0.7 all-gather.4.cloned.1.call-update
  7.3 0.8 select_reduce_fusion
  8.0 0.2 convert_reduce_fusion
  8.2 1.1 %fusion.16 = f32[16]{0:T(128)S(1)} fusion(bf16[16,8192]{1,0:T(8,128)(2,1)} %param.16), kind=kLoop, calls=%fused_computation.26 | loop fusion | flops 393200 | bytes 262208 | tf_op jit(solution)/shard_map/reduce_sum | solution.py:30
  9.4 1.3 %convolution_convert_fusion = bf16[32,8192]{1,0:T(8,128)(2,1)S(1)} fusion(s32[16]{0:T(128)S(1)} %multiply_add_fusion, bf16[16,8192]{1,0:T(8,128)(2,1)} %param.16, f32[8192]{0:T(1024)} %param.17, f32[16]{0:T(128)S(1)} %add_rsqrt_fusion), kind=kOutput, calls=%fused_computation | convolution fusion | flops 9175552 | bytes 819328 | tf_op jit(solution)/shard_map/dot_general | solution.py:89
  10.7 1.0 %reshape.220 = bf16[8,1,4,8192]{3,2,0,1:T(4,128)(2,1)} reshape(bf16[32,8192]{1,0:T(8,128)(2,1)S(1)} %convolution_convert_fusion) | data formatting | bytes 1048576 | tf_op jit(solution)/shard_map/reshape | solution.py:92
  11.7 7.3 %all-to-all-start = ((bf16[8,1,4,8192]{3,2,1,0:T(4,128)(2,1)}), bf16[8,1,4,8192]{3,2,1,0:T(4,128)(2,1)S(1)}, u32[]{:S(2)}, u32[]{:S(2)}) async-start(bf16[8,1,4,8192]{3,2,1,0:T(4,128)(2,1)} %bitcast.1), calls=%async_computation | async-start | bytes 1048576 | tf_op jit(solution)/shard_map/all_to_all | solution.py:102
  19.0 0.1 multiply_cosine_fusion.1
  19.1 14.3 %all-to-all-done = bf16[8,1,4,8192]{3,2,1,0:T(4,128)(2,1)S(1)} async-done(((bf16[8,1,4,8192]{3,2,1,0:T(4,128)(2,1)}), bf16[8,1,4,8192]{3,2,1,0:T(4,128)(2,1)S(1)}, u32[]{:S(2)}, u32[]{:S(2)}) %all-to-all-start) | async-done | bytes 524320 | tf_op jit(solution)/shard_map/all_to_all | solution.py:102
  33.4 2.9 %fusion.7 = bf16[8,1,4,192]{3,0,2,1:T(8,128)(2,1)S(1)} fusion(bf16[1,8192,192]{1,2,0:T(8,128)(2,1)} %all-gather.4.cloned.1.call-done, bf16[8,1,4,8192]{3,2,1,0:T(4,128)(2,1)S(1)} %all-to-all-done), kind=kOutput, calls=%fused_computation.11 | convolution fusion | flops 100669440 | bytes 3682304 | tf_op jit(solution)/shard_map/sacd,adr->sacr/dot_general | solution.py:37
  36.4 0.1 slice.37
  36.5 0.1 reshape.225
  36.6 0.1 fusion.11
  36.7 0.1 reshape.227
  36.8 0.1 fusion.10
  36.9 0.6 copy.43
  37.6 3.6 %all-to-all-start.1 = ((bf16[8,1,4,384]{3,2,1,0:T(4,128)(2,1)}), bf16[8,1,4,384]{3,2,1,0:T(4,128)(2,1)S(1)}, u32[]{:S(2)}, u32[]{:S(2)}) async-start(bf16[8,1,4,384]{3,2,1,0:T(4,128)(2,1)} %copy.43), calls=%async_computation.1 | async-start | bytes 49152 | tf_op jit(solution)/shard_map/all_to_all | solution.py:128
  41.2 0.0 reduce-scatter.2.cloned.1.call-start
  41.2 0.1 iota_compare_fusion.7
  41.3 6.5 %all-to-all-done.1 = bf16[8,1,4,384]{3,2,1,0:T(4,128)(2,1)S(1)} async-done(((bf16[8,1,4,384]{3,2,1,0:T(4,128)(2,1)}), bf16[8,1,4,384]{3,2,1,0:T(4,128)(2,1)S(1)}, u32[]{:S(2)}, u32[]{:S(2)}) %all-to-all-start.1) | async-done | bytes 24608 | tf_op jit(solution)/shard_map/all_to_all | solution.py:128
  47.8 0.2 fusion.46
  48.0 0.4 fusion.15
  48.5 1.8 %all-gather = f32[2,64,16]{1,2,0:T(8,128)S(1)} all-gather(f32[1,64,16]{1,2,0:T(8,128)S(1)} %fusion.15), channel_id=1, replica_groups=mesh['groups'=2,'adapter'=8,'tensor'=2] {'tensor'}, dimensions={0}, use_global_device_ids=true | all-gather | bytes 12288 | tf_op jit(solution)/shard_map/all_gather | solution.py:133
  50.3 0.1 reshape.238
  50.4 0.1 fusion.34
  50.5 2.9 %convolution_add_fusion.2 = f32[16,256]{1,0:T(8,128)S(1)} fusion(bf16[8192,256]{1,0:T(8,128)(2,1)} %param.18, f32[16,384]{1,0:T(8,128)S(1)} %fusion.46, bf16[16,8192]{1,0:T(8,128)(2,1)S(1)} %copy-done.1, f32[8192]{0:T(1024)S(1)} %copy-done.3, f32[16]{0:T(128)S(1)} %add_rsqrt_fusion), kind=kOutput, calls=%fused_computation.18 | convolution fusion | flops 67637248 | bytes 4522048 | tf_op jit(solution)/shard_map/dot_general | solution.py:69
  53.4 0.1 maximum_bitcast_fusion
  53.5 0.1 subtract_convert_fusion
  53.6 0.2 fusion.48
  53.8 0.3 fusion.60
  54.1 0.2 fusion.32
  54.4 0.4 fusion.14
  54.8 1.8 %all-gather.1 = bf16[2,64,16]{1,2,0:T(8,128)(2,1)S(1)} all-gather(bf16[1,64,16]{1,2,0:T(8,128)(2,1)S(1)} %fusion.14), channel_id=1, replica_groups=mesh['groups'=2,'adapter'=8,'tensor'=2] {'tensor'}, dimensions={0}, use_global_device_ids=true | all-gather | bytes 6144 | tf_op jit(solution)/shard_map/all_gather | solution.py:134
  56.6 0.1 reshape.242
  56.7 0.2 fusion.13
  56.9 3.6 %fusion.38 = f32[16,8192]{1,0:T(8,128)} fusion(bf16[256,8192]{1,0:T(8,128)(2,1)} %param.21, bf16[2,8,2,128]{3,2,1,0:T(2,128)(2,1)S(1)} %bitcast.114), kind=kOutput, calls=%fused_computation.58 | convolution fusion | flops 67108864 | bytes 4726784 | tf_op jit(solution)/shard_map/dot_general | solution.py:186
  60.6 0.0 reduce-scatter.2.cloned.1.call-update
  60.6 0.1 convolution_convert_fusion.2
  60.7 8.9 %all_to_all.20 = bf16[8,1,4,256]{3,2,1,0:T(4,128)(2,1)S(1)} all-to-all(bf16[8,1,4,256]{3,2,1,0:T(4,128)(2,1)S(1)} %bitcast.113), channel_id=1, replica_groups=mesh['groups'=2,'adapter'=8,'tensor'=2] {'adapter'}, dimensions={0} | all-to-all | bytes 32768 | tf_op jit(solution)/shard_map/all_to_all | solution.py:169
  69.7 0.1 convolution_bitcast_fusion
  69.8 3.4 %psum.7 = bf16[8,1,4,64]{3,0,2,1:T(8,128)(2,1)S(1)} all-reduce(f32[8,1,4,64]{3,0,2,1:T(8,128)S(1)} %convolution_bitcast_fusion), channel_id=1, replica_groups=mesh['groups'=2,'adapter'=8,'tensor'=2] {'tensor'}, use_global_device_ids=true, to_apply=%region_6.7 | all-reduce | flops 2048 | bytes 12288 | tf_op jit(solution)/shard_map/psum | solution.py:167
  73.2 0.2 fusion
  73.4 0.2 copy.48
  73.6 12.1 %all_to_all.21 = bf16[8,1,4,4096]{3,2,1,0:T(4,128)(2,1)S(1)} all-to-all(bf16[8,1,4,4096]{3,2,1,0:T(4,128)(2,1)S(1)} %copy.48), channel_id=1, replica_groups=mesh['groups'=2,'adapter'=8,'tensor'=2] {'adapter'}, dimensions={0} | all-to-all | bytes 524288 | tf_op jit(solution)/shard_map/all_to_all | solution.py:182
  85.7 0.1 reshape.236
  85.8 0.0 reduce-scatter.2.cloned.1.call-done
  85.8 1.8 %fusion.1 = bf16[16,4096]{1,0:T(8,128)(2,1)} fusion(f32[16,4096]{1,0:T(8,128)} %reduce-scatter.2.cloned.1.call-done, bf16[32,4096]{1,0:T(8,128)(2,1)S(1)} %reshape.236, s32[16]{0:T(128)S(1)} %multiply_add_fusion), kind=kOutput, calls=%fused_computation.4 | convolution fusion | flops 4325888 | bytes 655424 | tf_op jit(solution)/shard_map/dot_general | solution.py:95
  (36 shorter events, 0.2 us)
Async XLA Ops:
  6.5 41.5 %copy-start = (bf16[8192,64]{0,1:T(8,128)(2,1)S(1)}, bf16[8192,64]{0,1:T(8,128)(2,1)}, u32[]{:S(2)}) copy-start(bf16[8192,64]{0,1:T(8,128)(2,1)} %param.19) | copy-start | bytes 3145732
  6.5 41.5 %copy-start.1 = (bf16[16,8192]{1,0:T(8,128)(2,1)S(1)}, bf16[16,8192]{1,0:T(8,128)(2,1)}, u32[]{:S(2)}) copy-start(bf16[16,8192]{1,0:T(8,128)(2,1)} %param.16) | copy-start | bytes 786436
  6.5 41.5 %copy-start.3 = (f32[8192]{0:T(1024)S(1)}, f32[8192]{0:T(1024)}, u32[]{:S(2)}) copy-start(f32[8192]{0:T(1024)} %param.17) | copy-start | bytes 98308
  6.5 12.4 %copy-start.8 = (s32[16]{0:T(128)S(1)}, s32[16]{0:T(128)}, u32[]{:S(2)}) copy-start(s32[16]{0:T(128)} %param.26) | copy-start | bytes 196
  6.5 30.0 %copy-start.6 = (bf16[1,2,64,64]{3,2,1,0:T(8,128)(2,1)S(1)}, bf16[1,2,64,64]{3,2,1,0:T(8,128)(2,1)}, u32[]{:S(2)}) copy-start(bf16[1,2,64,64]{3,2,1,0:T(8,128)(2,1)} %param.29) | copy-start | bytes 49156
  6.5 30.3 %copy-start.5 = (bf16[1,64,256]{2,1,0:T(8,128)(2,1)S(1)}, bf16[1,64,256]{2,1,0:T(8,128)(2,1)}, u32[]{:S(2)}) copy-start(bf16[1,64,256]{2,1,0:T(8,128)(2,1)} %param.28) | copy-start | bytes 98308
  6.6 26.9 %all-gather.4.cloned.1.call-start = ((), (), s32[]{:S(2)}) async-start(), calls=%async_computation.5 | async-start | bytes 4718592 | tf_op jit(solution)/shard_map/all_gather | solution.py:99
  11.7 21.7 %all-to-all-start = ((bf16[8,1,4,8192]{3,2,1,0:T(4,128)(2,1)}), bf16[8,1,4,8192]{3,2,1,0:T(4,128)(2,1)S(1)}, u32[]{:S(2)}, u32[]{:S(2)}) async-start(bf16[8,1,4,8192]{3,2,1,0:T(4,128)(2,1)} %bitcast.1), calls=%async_computation | async-start | bytes 1048576 | tf_op jit(solution)/shard_map/all_to_all | solution.py:102
  36.4 17.4 %copy-start.9 = (bf16[16,32,128]{2,1,0:T(8,128)(2,1)S(1)}, bf16[16,32,128]{2,1,0:T(8,128)(2,1)}, u32[]{:S(2)}) copy-start(bf16[16,32,128]{2,1,0:T(8,128)(2,1)} %param.22) | copy-start | bytes 393220
  36.4 18.0 %copy-start.2 = (bf16[8192,64]{0,1:T(8,128)(2,1)S(1)}, bf16[8192,64]{0,1:T(8,128)(2,1)}, u32[]{:S(2)}) copy-start(bf16[8192,64]{0,1:T(8,128)(2,1)} %param.20) | copy-start | bytes 3145732
  36.5 20.2 %copy-start.10 = (bf16[16,32,128]{2,1,0:T(8,128)(2,1)S(1)}, bf16[16,32,128]{2,1,0:T(8,128)(2,1)}, u32[]{:S(2)}) copy-start(bf16[16,32,128]{2,1,0:T(8,128)(2,1)} %param.23) | copy-start | bytes 393220
  37.6 10.3 %all-to-all-start.1 = ((bf16[8,1,4,384]{3,2,1,0:T(4,128)(2,1)}), bf16[8,1,4,384]{3,2,1,0:T(4,128)(2,1)S(1)}, u32[]{:S(2)}, u32[]{:S(2)}) async-start(bf16[8,1,4,384]{3,2,1,0:T(4,128)(2,1)} %copy.43), calls=%async_computation.1 | async-start | bytes 49152 | tf_op jit(solution)/shard_map/all_to_all | solution.py:128
  41.2 44.6 %reduce-scatter.2.cloned.1.call-start = ((), (), s32[]{:S(2)}) async-start(), calls=%async_computation.6 | async-start | bytes 786432 | tf_op jit(solution)/shard_map/reduce_scatter | solution.py:187
  53.4 16.3 %copy-start.7 = (bf16[1,256,64]{1,2,0:T(8,128)(2,1)S(1)}, bf16[1,256,64]{1,2,0:T(8,128)(2,1)}, u32[]{:S(2)}) copy-start(bf16[1,256,64]{1,2,0:T(8,128)(2,1)} %param.30) | copy-start | bytes 98308
  53.4 19.8 %copy-start.4 = (bf16[1,64,4096]{2,1,0:T(8,128)(2,1)S(1)}, bf16[1,64,4096]{2,1,0:T(8,128)(2,1)}, u32[]{:S(2)}) copy-start(bf16[1,64,4096]{2,1,0:T(8,128)(2,1)} %param.31) | copy-start | bytes 1572868
Sparse Core Ops, SparseCore 0:
  8.9 14.8 all-gather.3
  60.7 5.3 reduce-scatter.1
where the time goes:
time: 95.1 us; the launch traced here: 94.5 us
  blocking collectives  28 us (29%)
  waiting for transfers between devices  21.6 us (23%)
  matrix products  15.1 us (16%)
  between operations  13.6 us (14%)
  starting transfers between devices  11 us (12%)
  other arithmetic  2.78 us (3%)
  local copies, waits for them, and re-layouts  2.42 us (3%)
    all_to_all x1, waiting for transfers between devices, body(): lax.all_to_all(sent, 'adapter', split_axis=0, concat_axis=0, tiled=True)  14.3 us
    all_to_all x1, blocking collectives, body(): lax.all_to_all(change.astype(jnp.bfloat16), 'adapter', split_axis=0, conc...  12.1 us
    all_to_all x1, blocking collectives, body(): lax.all_to_all(dispatch(attention_output), 'adapter', split_axis=0, conca...  8.94 us
    all_to_all x1, starting transfers between devices, body(): lax.all_to_all(sent, 'adapter', split_axis=0, concat_axis=0, tiled=True)  7.25 us
    all_to_all x1, waiting for transfers between devices, body(): lax.all_to_all(change, 'adapter', split_axis=0, concat_axis=0, tiled=True)  6.51 us
    dot_general x1, matrix products, body(): jnp.dot(attention_output, output_projection, preferred_element_type=jnp.f...  3.64 us
    all_to_all x1, starting transfers between devices, body(): lax.all_to_all(change, 'adapter', split_axis=0, concat_axis=0, tiled=True)  3.64 us
    psum x1, blocking collectives, body(): lax.psum(rank_terms(lax.all_to_all(dispatch(attention_output), 'adapter',...  3.37 us
  transfers between devices with their start and end apart: 4, of which 2 were waited for; matrix products, arithmetic and copies ran while one was open for 6% of the time, Pallas kernels for 0%

commit v1 on v0

v1 whole, which is shorter than its diff:
```python
import functools
import math

import jax
import jax.numpy as jnp
from jax import lax
from jax.experimental import pallas as pl
from jax.experimental.pallas import tpu as pltpu
from jax.sharding import PartitionSpec as P

HEAD_SIZE = 128
LANES = 128
EPSILON = 1e-05
THETA = 500000.0
BF16 = jnp.bfloat16
F32 = jnp.float32
SWAP = [(0, 1), (1, 0)]
VMEM_LIMIT = 40 * 1024 * 1024


def nn(a, b):
    return lax.dot_general(a, b, (((1,), (0,)), ((), ())), preferred_element_type=F32)


def nt(a, b):
    return lax.dot_general(a, b, (((1,), (1,)), ((), ())), preferred_element_type=F32)


def iota(shape, dim):
    return lax.broadcasted_iota(jnp.int32, shape, dim)


def ones_where(condition):
    return jnp.where(condition, 1.0, 0.0).astype(BF16)


def owner_and_standing(named, table):
    requests, adapters = named.shape[1], table.shape[1]
    table_column = jnp.sum(
        jnp.where(iota((adapters, adapters), 0) == iota((adapters, adapters), 1), table, 0),
        axis=1,
        keepdims=True,
    )
    owner = jnp.sum(
        jnp.where(iota((adapters, requests), 0) == named, table_column, 0), axis=0, keepdims=True
    )
    square = (requests, requests)
    owner_column = jnp.sum(
        jnp.where(iota(square, 0) == iota(square, 1), owner, 0), axis=1, keepdims=True
    )
    earlier = (owner_column == owner) & (iota(square, 0) < iota(square, 1))
    standing = jnp.sum(jnp.where(earlier, 1, 0), axis=0, keepdims=True)
    return owner, standing


def pack_kernel(capacity, x_ref, gain_ref, k_ref, v_ref, named_ref, table_ref, length_ref, out_ref, flat_ref, spread_ref):
    core = lax.axis_index("tensor")
    requests, width = x_ref.shape
    half = width // 2
    positions = k_ref.shape[0] // requests
    per_owner = 2 * capacity
    rows = out_ref.shape[0]
    owner, standing = owner_and_standing(named_ref[...], table_ref[...])
    own_slot = standing % 2 == core
    place = owner * per_owner + standing // 2
    x_row = place + jnp.where(own_slot, 0, capacity // 2)
    k_row = jnp.where(own_slot, owner * per_owner + capacity + 2 * (standing // 2), -2)
    order = iota((rows, requests), 0)
    put_x = ones_where(order == x_row)
    put_k = ones_where(order == k_row)
    put_v = ones_where(order == k_row + 1)

    floats = x_ref[...].astype(F32)
    scale = lax.rsqrt(jnp.mean(floats * floats, axis=1, keepdims=True) + EPSILON)
    mine = pl.ds(pl.multiple_of(core * half, half), half)
    flat_ref[0:requests, :] = (x_ref[:, mine].astype(F32) * scale * gain_ref[:, mine]).astype(BF16)
    for first, source in ((requests, k_ref), (2 * requests, v_ref)):
        spread_ref[...] = source[...].astype(F32)
        for p in range(positions):
            flat_ref[first : first + requests, p * LANES : (p + 1) * LANES] = spread_ref[
                pl.ds(p, requests, stride=positions), :
            ].astype(BF16)
    put = jnp.concatenate([put_x, put_k, put_v], axis=1)
    step = 512
    for c in range(0, half, step):
        out_ref[:, c : c + step] = nn(put, flat_ref[:, c : c + step]).astype(BF16)
    square = (requests, requests)
    length_column = jnp.sum(
        jnp.where(iota(square, 0) == iota(square, 1), length_ref[...], 0), axis=1, keepdims=True
    )
    lengths = jnp.broadcast_to(length_column.astype(F32), (requests, LANES)).astype(BF16)
    out_ref[:, half:] = nn(put_x, lengths).astype(BF16)


def project_kernel(capacity, owners, buf_ref, wq_ref, wq_other_ref, kv_ref, kv_other_ref, down_ref, mine_ref, theirs_ref, sums_ref):
    core = lax.axis_index("tensor")
    half = wq_other_ref.shape[0]
    per_owner = 2 * capacity
    here = capacity // 2
    buf = buf_ref[:, :half]
    rows = pl.ds(pl.multiple_of(core * half, half), half)
    ranks = nt(buf, down_ref[...])
    spare = jnp.zeros((buf.shape[0], -ranks.shape[1] % LANES), F32)
    parts = [
        nn(buf, wq_ref[rows, :]),
        nn(buf, wq_other_ref[...]),
        nt(buf, kv_ref[:, rows]),
        nt(buf, kv_other_ref[...]),
        jnp.concatenate([ranks, spare], axis=1),
    ]
    tile = 0
    for part in parts:
        for c in range(0, part.shape[1], LANES):
            sums_ref[...] = part[:, c : c + LANES]
            columns = slice(tile * LANES, (tile + 1) * LANES)
            for i in range(here):
                to = slice(i * owners, (i + 1) * owners)
                mine_ref[to, columns] = sums_ref[pl.ds(i, owners, stride=per_owner), :]
                theirs_ref[to, columns] = sums_ref[pl.ds(here + i, owners, stride=per_owner), :]
            tile += 1


def unpack_kernel(capacity, owners, buf_ref, k_ref, v_ref, length_ref, cosine_ref, sine_ref):
    rows = buf_ref.shape[0]
    slots = owners * capacity // 2
    positions = k_ref.shape[0] // slots
    half = positions * LANES
    per_owner = 2 * capacity
    slot = iota((slots, rows), 0)
    base = (slot % owners) * per_owner
    order = iota((slots, rows), 1)
    pick_x = ones_where(order == base + slot // owners)
    pick_k = ones_where(order == base + capacity + 2 * (slot // owners))
    pick_v = ones_where(order == base + capacity + 2 * (slot // owners) + 1)
    pick = jnp.concatenate([pick_k, pick_v], axis=0)
    step = 512
    for c in range(0, half, step):
        both = nn(pick, buf_ref[:, c : c + step]).astype(BF16)
        for j in range(step // LANES):
            p = c // LANES + j
            tile = both[:, j * LANES : (j + 1) * LANES]
            k_ref[p * slots : (p + 1) * slots, :] = tile[:slots]
            v_ref[p * slots : (p + 1) * slots, :] = tile[slots:]
    length = nn(pick_x, buf_ref[:, half:])
    length_ref[...] = length
    halfway = HEAD_SIZE // 2
    lane = iota((slots, LANES), 1)
    exponent = (lane % halfway).astype(F32) * (-math.log(THETA) / halfway)
    angle = length * jnp.exp(exponent)
    cosine_ref[...] = jnp.cos(angle)
    sine = jnp.sin(angle)
    sine_ref[...] = jnp.where(lane < halfway, -sine, sine)


def attend_kernel(mine_ref, theirs_ref, up_ref, k_ref, v_ref, length_ref, cosine_ref, sine_ref, out_ref):
    core = lax.axis_index("tensor")
    slots = mine_ref.shape[0]
    ucols = up_ref.shape[1]
    kvcols = LANES
    qcols = (ucols - 2 * kvcols) // 2
    heads = 2 * qcols // HEAD_SIZE
    halfway = HEAD_SIZE // 2
    mine = mine_ref[...]
    theirs = theirs_ref[...]
    swapped = jnp.concatenate(
        [
            theirs[:, qcols : 2 * qcols],
            theirs[:, :qcols],
            theirs[:, 2 * qcols + kvcols : ucols],
            theirs[:, 2 * qcols : 2 * qcols + kvcols],
            theirs[:, ucols:],
        ],
        axis=1,
    )
    sums = mine + swapped
    ranks = sums[:, ucols : ucols + up_ref.shape[0]].astype(BF16)
    deltas = nn(ranks, up_ref[...]).astype(BF16).astype(F32)
    combined = sums[:, :ucols] + deltas
    cosine, sine = cosine_ref[...], sine_ref[...]

    def rotate(part):
        return part * cosine + pltpu.roll(part, halfway, 1) * sine

    queries = jnp.concatenate(
        [rotate(combined[:, h * HEAD_SIZE : (h + 1) * HEAD_SIZE]) for h in range(heads)], axis=0
    ).astype(BF16)
    kv_mine = combined[:, 2 * qcols : 2 * qcols + kvcols]
    kv_theirs = combined[:, 2 * qcols + kvcols :]
    leading = jnp.where(core == 0, kv_mine, kv_theirs)
    trailing = jnp.where(core == 0, kv_theirs, kv_mine)
    first = iota((slots, LANES), 1) < halfway
    own_key = rotate(jnp.where(first, leading, pltpu.roll(trailing, halfway, 1))).astype(BF16)
    own_value = jnp.where(first, pltpu.roll(leading, halfway, 1), trailing).astype(BF16)

    cached = k_ref.shape[0]
    rows = heads * slots
    shrink = math.sqrt(HEAD_SIZE)
    length = jnp.concatenate([length_ref[:, 0:1]] * heads, axis=0).astype(jnp.int32)
    column = iota((rows, cached), 1)
    visible = (column % slots == iota((rows, cached), 0) % slots) & (column // slots < length)
    own = iota((rows, slots), 1) == iota((rows, slots), 0) % slots
    scores = jnp.where(visible, nt(queries, k_ref[...]) / shrink, -jnp.inf)
    own_scores = jnp.where(own, nt(queries, own_key) / shrink, -jnp.inf)
    highest = jnp.maximum(
        jnp.max(scores, axis=1, keepdims=True), jnp.max(own_scores, axis=1, keepdims=True)
    )
    raised = jnp.exp(scores - highest)
    own_raised = jnp.exp(own_scores - highest)
    total = jnp.sum(raised, axis=1, keepdims=True) + jnp.sum(own_raised, axis=1, keepdims=True)
    weights = (raised / total).astype(BF16)
    own_weights = (own_raised / total).astype(BF16)
    attended = (nn(weights, v_ref[...]) + nn(own_weights, own_value)).astype(BF16)
    for h in range(heads):
        out_ref[:, h * HEAD_SIZE : (h + 1) * HEAD_SIZE] = attended[h * slots : (h + 1) * slots]


def output_kernel(capacity, owners, mine_ref, theirs_ref, wo_ref, wo_other_ref, down_ref, down_other_ref, up_ref, out_ref):
    core = lax.axis_index("tensor")
    slots, cols = mine_ref.shape
    hcols = cols // 2
    half = out_ref.shape[1]
    rows = owners * capacity
    theirs = theirs_ref[...]
    rows_in = jnp.concatenate(
        [mine_ref[...], jnp.concatenate([theirs[:, hcols:], theirs[:, :hcols]], axis=1)], axis=0
    )
    out_row = iota((rows, 2 * slots), 0)
    standing = out_row % capacity
    source = (
        jnp.where(standing % 2 == core, 0, slots) + (standing // 2) * owners + out_row // capacity
    )
    arrange = ones_where(iota((rows, 2 * slots), 1) == source)
    attended = nn(arrange, rows_in).astype(BF16)
    left, right = attended[:, :hcols], attended[:, hcols:]
    ranks = (nt(left, down_ref[...]) + nt(right, down_other_ref[...])).astype(BF16)
    step = 512
    for c in range(0, half, step):
        columns = pl.ds(pl.multiple_of(core * half + c, step), step)
        delta = nn(ranks, up_ref[:, c : c + step]).astype(BF16).astype(F32)
        terms = nn(left, wo_ref[:, columns]) + nn(right, wo_other_ref[:, c : c + step])
        out_ref[:, c : c + step] = (terms + delta).astype(BF16)


def pick_kernel(capacity, back_ref, named_ref, table_ref, out_ref):
    rows, half = back_ref.shape
    requests = out_ref.shape[0]
    owner, standing = owner_and_standing(named_ref[...], table_ref[...])
    place = ones_where(iota((rows, requests), 0) == owner * capacity + standing)
    step = 512
    for c in range(0, half, step):
        out_ref[:, c : c + step] = lax.dot_general(
            place,
            back_ref[:, c : c + step],
            (((0,), (0,)), ((), ())),
            preferred_element_type=F32,
        ).astype(BF16)


def call(kernel, outs, scratch=(), flops=0, moved=0):
    many = isinstance(outs, (list, tuple))
    spec = pl.BlockSpec(memory_space=pltpu.VMEM)
    return lambda *args: pl.pallas_call(
        kernel,
        out_shape=outs,
        in_specs=[spec] * len(args),
        out_specs=[spec] * len(outs) if many else spec,
        scratch_shapes=list(scratch),
        compiler_params=pltpu.CompilerParams(vmem_limit_bytes=VMEM_LIMIT),
        cost_estimate=pl.CostEstimate(flops=flops, bytes_accessed=moved, transcendentals=0),
    )(*args)


def body(
    layer_input,
    input_norm_gain,
    query_projection,
    key_projection,
    value_projection,
    output_projection,
    cached_key_rows,
    cached_value_rows,
    request_adapter,
    adapter_row_table,
    cached_length,
    projection_adapter_down,
    query_adapter_up,
    key_value_adapter_up,
    output_adapter_down,
    output_adapter_up,
):
    requests, width = layer_input.shape
    owners = lax.axis_size("adapter")
    adapters = adapter_row_table.shape[0]
    positions = cached_key_rows.shape[1]
    half = width // 2
    capacity = max(2, 2 * ((requests + adapters - 1) // adapters))
    rows = owners * 2 * capacity
    slots = owners * capacity // 2
    core = lax.axis_index("tensor")
    named = request_adapter.reshape(1, requests)
    table = adapter_row_table.reshape(1, adapters)
    shape = jax.ShapeDtypeStruct

    packed = call(
        functools.partial(pack_kernel, capacity),
        shape((rows, half + LANES), BF16),
        [pltpu.VMEM((3 * requests, half), BF16), pltpu.VMEM((positions * requests, LANES), F32)],
    )(
        layer_input,
        input_norm_gain.reshape(1, width),
        cached_key_rows.reshape(requests * positions, HEAD_SIZE),
        cached_value_rows.reshape(requests * positions, HEAD_SIZE),
        named,
        table,
        cached_length.reshape(1, requests),
    )
    arrived = lax.all_to_all(
        packed.reshape(owners, 2 * capacity, half + LANES),
        "adapter",
        split_axis=0,
        concat_axis=0,
        tiled=True,
    ).reshape(rows, half + LANES)

    other = (1 - core) * half
    qcols = query_projection.shape[1]
    kv = jnp.concatenate([key_projection.T, value_projection.T], axis=0)
    kvcols = kv.shape[0]
    wq_other = lax.ppermute(
        lax.dynamic_slice(query_projection, (other, 0), (half, qcols)), "tensor", SWAP
    )
    kv_other = lax.ppermute(lax.dynamic_slice(kv, (0, other), (kvcols, half)), "tensor", SWAP)
    wo_other = lax.ppermute(
        lax.dynamic_slice(output_projection, (0, other), (output_projection.shape[0], half)),
        "tensor",
        SWAP,
    )
    query_up = query_adapter_up[0]
    rank = query_up.shape[0]
    kv_up = key_value_adapter_up[0]
    hcols = kv_up.shape[2]
    out_down = output_adapter_down[0].T
    small = jnp.concatenate([query_up, kv_up[0], kv_up[1], out_down], axis=1)
    small_other = lax.ppermute(small, "tensor", SWAP)
    out_down_other = small_other[:, qcols + 2 * hcols :]

    def zeros(columns):
        return jnp.zeros((rank, columns), BF16)

    def kv_rows(which):
        blocks = []
        for source in (small, small_other):
            for one in range(2):
                first = qcols + one * hcols
                blocks.append(source[:, first : first + hcols] if one == which else zeros(hcols))
        return jnp.concatenate([zeros(2 * qcols)] + blocks, axis=1)

    up = jnp.concatenate(
        [
            jnp.concatenate(
                [small[:, :qcols], small_other[:, :qcols], zeros(4 * hcols)], axis=1
            ),
            kv_rows(0),
            kv_rows(1),
        ],
        axis=0,
    )
    down = projection_adapter_down[0].T
    ucols = 2 * qcols + 2 * kvcols
    pcols = ucols + (down.shape[0] + LANES - 1) // LANES * LANES

    mine, theirs = call(
        functools.partial(project_kernel, capacity, owners),
        [shape((slots, pcols), F32), shape((slots, pcols), F32)],
        [pltpu.VMEM((rows, LANES), F32)],
    )(arrived, query_projection, wq_other, kv, kv_other, down)
    theirs = lax.ppermute(theirs, "tensor", SWAP)
    keys, values, lengths, cosine, sine = call(
        functools.partial(unpack_kernel, capacity, owners),
        [shape((slots * positions, HEAD_SIZE), BF16)] * 2 + [shape((slots, LANES), F32)] * 3,
    )(arrived)
    attended = call(attend_kernel, shape((slots, 2 * qcols), BF16))(
        mine, theirs, up, keys, values, lengths, cosine, sine
    )
    attended_other = lax.ppermute(attended, "tensor", SWAP)
    finished = call(
        functools.partial(output_kernel, capacity, owners),
        shape((owners * capacity, half), BF16),
    )(
        attended,
        attended_other,
        output_projection,
        wo_other,
        out_down,
        out_down_other,
        output_adapter_up[0],
    )
    back = lax.all_to_all(
        finished.reshape(owners, capacity, half), "adapter", split_axis=0, concat_axis=0, tiled=True
    ).reshape(owners * capacity, half)
    return call(functools.partial(pick_kernel, capacity), shape((requests, half), BF16))(
        back, named, table
    )


def solution(mesh):
    placed = (
        P(("groups", "adapter"), None),
        P(),
        P(None, "tensor"),
        P(None, "tensor"),
        P(None, "tensor"),
        P("tensor", None),
        P(("groups", "adapter"), None, None),
        P(("groups", "adapter"), None, None),
        P(("groups", "adapter"), None),
        P(),
        P(("groups", "adapter")),
        P("adapter", "tensor", None),
        P("adapter", None, "tensor"),
        P("adapter", None, None, "tensor"),
        P("adapter", "tensor", None),
        P("adapter", None, "tensor"),
    )
    return jax.shard_map(
        body,
        mesh=mesh,
        in_specs=placed,
        out_specs=P(("groups", "adapter"), "tensor"),
        check_vma=False,
    )
```

time: 95.1 us -> 59 us (0.62)
  blocking collectives: 28 us -> 12.7 us
  matrix products: 15.1 us -> 0 us
  between operations: 13.6 us -> 0.2 us
  Pallas kernels: 0 us -> 10.3 us
  waiting for transfers between devices: 21.6 us -> 15 us
  local copies, waits for them, and re-layouts: 2.42 us -> 8.85 us
  starting transfers between devices: 11 us -> 8.76 us
    dot_general x16 -> x0, matrix products: 15.1 us -> none  [the longest x1 3.64 us: body(): jnp.dot(attention_output, output_projection, preferred_element_type=jnp.f...]
    pallas_call x0 -> x6, Pallas kernels: none -> 10.3 us  [call(): pl.pallas_call(kernel, out_shape=outs, in_specs=[spec] * len(args), out_s...]
    all_to_all x2 -> x1, blocking collectives: 21.1 us -> 12.7 us  [body(): lax.all_to_all(finished.reshape(owners, capacity, half), 'adapter', split...]
    all_to_all x2 -> x1, waiting for transfers between devices: 20.8 us -> 13 us  [body(): lax.all_to_all(packed.reshape(owners, 2 * capacity, half + LANES), 'adapt...]
    dynamic_slice x0 -> x2, local copies, waits for them, and re-layouts: none -> 4.71 us  [the longest x1 3.24 us: body(): lax.dynamic_slice(query_projection, (other, 0), (half, qcols))]
    all_to_all x2 -> x1, starting transfers between devices: 10.9 us -> 7.25 us  [body(): lax.all_to_all(packed.reshape(owners, 2 * capacity, half + LANES), 'adapt...]
    all_gather x2 -> x0, blocking collectives: 3.62 us -> none  [the longest x1 1.82 us: body(): lax.all_gather(key_part, 'tensor', axis=1, tiled=True)]
    unnamed x23 -> x34, local copies, waits for them, and re-layouts: 0.13 us -> 3.66 us
  transfers between devices with their start and end apart: 4 -> 7, of which waited for: 2 -> 3; matrix products, arithmetic and copies ran while one was open for 6% -> 8% of each run, Pallas kernels for 0% -> 11%
where the time goes in v1:
time: 59 us; the launch traced here: 58.6 us
  waiting for transfers between devices  15 us (25%)
  blocking collectives  12.7 us (22%)
  Pallas kernels  10.3 us (17%)
  local copies, waits for them, and re-layouts  8.85 us (15%)
  starting transfers between devices  8.76 us (15%)
  other arithmetic  2.86 us (5%)
    all_to_all x1, waiting for transfers between devices, body(): lax.all_to_all(packed.reshape(owners, 2 * capacity, half + LANES), 'adapt...  13 us
    all_to_all x1, blocking collectives, body(): lax.all_to_all(finished.reshape(owners, capacity, half), 'adapter', split...  12.7 us
    pallas_call x6, Pallas kernels, call(): pl.pallas_call(kernel, out_shape=outs, in_specs=[spec] * len(args), out_s...  10.3 us
    all_to_all x1, starting transfers between devices, body(): lax.all_to_all(packed.reshape(owners, 2 * capacity, half + LANES), 'adapt...  7.25 us
    unnamed x34, local copies, waits for them, and re-layouts  3.66 us
    dynamic_slice x1, local copies, waits for them, and re-layouts, body(): lax.dynamic_slice(query_projection, (other, 0), (half, qcols))  3.24 us
    concatenate x2, other arithmetic, body(): kv = jnp.concatenate([key_projection.T, value_projection.T], axis=0)  2.75 us
    dynamic_slice x1, local copies, waits for them, and re-layouts, body(): lax.dynamic_slice(output_projection, (0, other), (output_projection.shape...  1.47 us
  transfers between devices with their start and end apart: 7, of which 3 were waited for; matrix products, arithmetic and copies ran while one was open for 8% of the time, Pallas kernels for 11%

profile of v1, /device:TPU:0, one launch (start us, length us, event | category | flops | bytes accessed | tf_op | source)
XLA Modules:
  0.0 58.6 jit_solution(5629948770787590781)
XLA Ops:
  0.0 3.2 %constant_dynamic-slice_fusion.1 = bf16[4096,256]{1,0:T(8,128)(2,1)} fusion(bf16[8192,256]{1,0:T(8,128)(2,1)} %wq_ref.1, s32[]{:T(128)S(6)} %select_n.2), kind=kLoop, calls=%fused_computation.9 | loop fusion | bytes 4194308 | tf_op jit(solution)/shard_map/dynamic_slice | solution.py:330
  3.3 0.0 copy-start.14
  3.3 0.5 collective-permute-start
  3.8 0.0 copy-done
  3.8 1.5 %constant_dynamic-slice_fusion = bf16[256,4096]{1,0:T(8,128)(2,1)} fusion(bf16[256,8192]{1,0:T(8,128)(2,1)S(1)} %copy-done, s32[]{:T(128)S(6)} %select_n.2), kind=kLoop, calls=%fused_computation.8 | loop fusion | bytes 4194308 | tf_op jit(solution)/shard_map/dynamic_slice | solution.py:334
  5.3 0.0 copy-start.10
  5.3 0.0 copy-start.11
  5.3 0.0 copy-start.12
  5.3 0.1 collective-permute-start.5
  5.4 0.0 copy-done.16
  5.4 0.0 copy-done.6
  5.4 0.0 copy-done.15
  5.5 0.1 pad_maximum_fusion.2
  5.5 0.5 collective-permute-start.3
  6.1 0.0 copy-done.13
  6.1 0.0 copy-done.14
  6.1 1.1 %fusion = bf16[128,4096]{1,0:T(8,128)(2,1)} fusion(s32[]{:T(128)S(6)} %select_n.2, bf16[64,8192]{1,0:T(8,128)(2,1)S(1)} %bitcast.39, bf16[64,8192]{1,0:T(8,128)(2,1)S(1)} %bitcast.37), kind=kLoop, calls=%fused_computation.3 | loop fusion | flops 2097152 | bytes 3145732 | tf_op jit(solution)/shard_map/concatenate | solution.py:327
  7.1 0.1 collective-permute-start.1
  7.2 0.0 copy-done.5
  7.2 0.0 copy-done.7
  7.2 0.0 copy-done.8
  7.2 0.0 copy-done.9
  7.2 1.6 %shard_map.154 = bf16[64,4224]{1,0:T(8,128)(2,1)} custom-call(bf16[16,8192]{1,0:T(8,128)(2,1)S(1)} %copy-done.5, f32[1,8192]{1,0:T(1,128)S(1)} %bitcast.30, bf16[512,128]{1,0:T(8,128)(2,1)S(1)} %bitcast.28, bf16[512,128]{1,0:T(8,128)(2,1)S(1)} %bitcast.29, s32[1,16]{1,0:T(1,128)S(1)} %bitcast.31, s32[1,8]{1,0:T(1,128)S(1)} %bitcast.33, s32[1,16]{1,0:T(1,128)S(1)} %bitcast.35), custom_call_target="tpu_custom_call" | custom-call | tf_op jit(solution)/shard_map/pallas_call | solution.py:262
  8.8 7.3 %all-to-all-start = ((bf16[8,8,4224]{2,1,0:T(8,128)(2,1)}), bf16[8,8,4224]{2,1,0:T(8,128)(2,1)S(1)}, u32[]{:S(2)}, u32[]{:S(2)}) async-start(bf16[8,8,4224]{2,1,0:T(8,128)(2,1)} %bitcast.6), calls=%async_computation | async-start | bytes 1081344 | tf_op jit(solution)/shard_map/all_to_all | solution.py:317
  16.1 1.7 %pad_maximum_fusion.kv_ref = bf16[128,8192]{1,0:T(8,128)(2,1)S(1)} fusion(bf16[64,8192]{1,0:T(8,128)(2,1)} %bitcast.36, bf16[64,8192]{1,0:T(8,128)(2,1)} %bitcast.38), kind=kLoop, calls=%fused_computation.1 | loop fusion | flops 4194304 | bytes 4194304 | tf_op jit(solution)/shard_map/concatenate | solution.py:327
  17.8 0.0 collective-permute-done.3
  17.8 0.1 fusion.2
  17.9 0.1 concatenate.21
  18.0 0.1 concatenate.22
  18.1 13.0 %all-to-all-done = bf16[8,8,4224]{2,1,0:T(8,128)(2,1)S(1)} async-done(((bf16[8,8,4224]{2,1,0:T(8,128)(2,1)}), bf16[8,8,4224]{2,1,0:T(8,128)(2,1)S(1)}, u32[]{:S(2)}, u32[]{:S(2)}) %all-to-all-start) | async-done | bytes 540704 | tf_op jit(solution)/shard_map/all_to_all | solution.py:317
  31.1 0.0 collective-permute-done.1.kv_other_ref
  31.1 0.0 collective-permute-done.wq_other_ref
  31.1 2.2 %copy-done.2 = bf16[8192,256]{1,0:T(8,128)(2,1)S(1)} copy-done((bf16[8192,256]{1,0:T(8,128)(2,1)S(1)}, bf16[8192,256]{1,0:T(8,128)(2,1)}, u32[]{:S(2)}) %copy-start.2) | copy-done | bytes 4194328
  33.3 1.4 %copy-done.3 = bf16[1,4096,192]{1,2,0:T(8,128)(2,1)S(1)} copy-done((bf16[1,4096,192]{1,2,0:T(8,128)(2,1)S(1)}, bf16[1,4096,192]{1,2,0:T(8,128)(2,1)}, u32[]{:S(2)}) %copy-start.3) | copy-done | bytes 1572888
  34.7 4.0 %shard_map.155 = (f32[16,1024]{1,0:T(8,128)S(1)}, f32[16,1024]{1,0:T(8,128)S(1)}) custom-call(bf16[64,4224]{1,0:T(8,128)(2,1)S(1)} %bitcast.22, bf16[8192,256]{1,0:T(8,128)(2,1)S(1)} %copy-done.2, bf16[4096,256]{1,0:T(8,128)(2,1)} %collective-permute-done.wq_other_ref, bf16[128,8192]{1,0:T(8,128)(2,1)S(1)} %pad_maximum_fusion.kv_ref, ...), custom_call_target="tpu_custom_call" | custom-call | tf_op jit(solution)/shard_map/pallas_call | solution.py:262
  38.7 0.0 copy-start.4
  38.7 0.1 collective-permute-start.2
  38.9 0.3 shard_map.156
  39.1 0.9 %collective-permute-done.2.theirs_ref = f32[16,1024]{1,0:T(8,128)S(1)} collective-permute-done((f32[16,1024]{1,0:T(8,128)S(1)}, f32[16,1024]{1,0:T(8,128)S(1)}, u32[]{:S(2)}, u32[]{:S(2)}) %collective-permute-start.2) | collective-permute-done | bytes 65568 | tf_op jit(solution)/shard_map/ppermute | solution.py:377
  40.1 0.8 %shard_map.157.mine_ref = bf16[16,512]{1,0:T(8,128)(2,1)S(1)} custom-call(f32[16,1024]{1,0:T(8,128)S(1)} %get-tuple-element.12.mine_ref, f32[16,1024]{1,0:T(8,128)S(1)} %collective-permute-done.2.theirs_ref, bf16[192,768]{1,0:T(8,128)(2,1)S(1)} %pad_maximum_fusion.1.up_ref, bf16[512,128]{1,0:T(8,128)(2,1)S(1)} %get-tuple-element.14.k_ref, ...), custom_call_target="tpu_custom_call" | custom-call | tf_op jit(solution)/shard_map/pallas_call | solution.py:262
  40.8 0.2 collective-permute-start.4
  41.1 0.0 collective-permute-done.5.wo_other_ref
  41.1 1.0 %collective-permute-done.4.theirs_ref = bf16[16,512]{1,0:T(8,128)(2,1)S(1)} collective-permute-done((bf16[16,512]{1,0:T(8,128)(2,1)S(1)}, bf16[16,512]{1,0:T(8,128)(2,1)S(1)}, u32[]{:S(2)}, u32[]{:S(2)}) %collective-permute-start.4) | collective-permute-done | bytes 16416 | tf_op jit(solution)/shard_map/ppermute | solution.py:385
  42.1 2.6 %shard_map.158 = bf16[32,4096]{1,0:T(8,128)(2,1)S(1)} custom-call(bf16[16,512]{1,0:T(8,128)(2,1)S(1)} %shard_map.157.mine_ref, bf16[16,512]{1,0:T(8,128)(2,1)S(1)} %collective-permute-done.4.theirs_ref, bf16[256,8192]{1,0:T(8,128)(2,1)S(1)} %copy-done.1, bf16[256,4096]{1,0:T(8,128)(2,1)} %collective-permute-done.5.wo_other_ref, ...), custom_call_target="tpu_custom_call" | custom-call | tf_op jit(solution)/shard_map/pallas_call | solution.py:262
  44.7 0.1 reshape.42
  44.8 12.7 %all_to_all.10 = bf16[8,4,4096]{2,1,0:T(4,128)(2,1)S(1)} all-to-all(bf16[8,4,4096]{2,1,0:T(4,128)(2,1)S(1)} %reshape.42), channel_id=1, replica_groups=mesh['groups'=2,'adapter'=8,'tensor'=2] {'adapter'}, dimensions={0} | all-to-all | bytes 524288 | tf_op jit(solution)/shard_map/all_to_all | solution.py:398
  57.5 0.1 reshape.43.back_ref
  57.6 1.1 %shard_map.159 = bf16[16,4096]{1,0:T(8,128)(2,1)} custom-call(bf16[32,4096]{1,0:T(8,128)(2,1)S(1)} %reshape.43.back_ref, s32[1,16]{1,0:T(1,128)S(1)} %bitcast.32, s32[1,8]{1,0:T(1,128)S(1)} %bitcast.34), custom_call_target="tpu_custom_call" | custom-call | tf_op jit(solution)/shard_map/pallas_call | solution.py:262
  (23 shorter events, 0.1 us)
Async XLA Ops:
  0.0 3.8 %copy-start = (bf16[256,8192]{1,0:T(8,128)(2,1)S(1)}, bf16[256,8192]{1,0:T(8,128)(2,1)}, u32[]{:S(2)}) copy-start(bf16[256,8192]{1,0:T(8,128)(2,1)} %wo_ref.1) | copy-start | bytes 12582916
  3.2 2.2 %copy-start.16 = (bf16[1,2,64,64]{3,2,1,0:T(8,128)(2,1)S(1)}, bf16[1,2,64,64]{3,2,1,0:T(8,128)(2,1)}, u32[]{:S(2)}) copy-start(bf16[1,2,64,64]{3,2,1,0:T(8,128)(2,1)} %param.29) | copy-start | bytes 49156
  3.2 2.2 %copy-start.6 = (bf16[1,256,64]{1,2,0:T(8,128)(2,1)S(1)}, bf16[1,256,64]{1,2,0:T(8,128)(2,1)}, u32[]{:S(2)}) copy-start(bf16[1,256,64]{1,2,0:T(8,128)(2,1)} %param.30) | copy-start | bytes 98308
  3.2 2.2 %copy-start.15 = (bf16[1,64,256]{2,1,0:T(8,128)(2,1)S(1)}, bf16[1,64,256]{2,1,0:T(8,128)(2,1)}, u32[]{:S(2)}) copy-start(bf16[1,64,256]{2,1,0:T(8,128)(2,1)} %param.28) | copy-start | bytes 98308
  3.2 2.8 %copy-start.13 = (bf16[8192,64]{0,1:T(8,128)(2,1)S(1)}, bf16[8192,64]{0,1:T(8,128)(2,1)}, u32[]{:S(2)}) copy-start(bf16[8192,64]{0,1:T(8,128)(2,1)} %param.20) | copy-start | bytes 3145732
  3.3 2.8 %copy-start.14 = (bf16[8192,64]{0,1:T(8,128)(2,1)S(1)}, bf16[8192,64]{0,1:T(8,128)(2,1)}, u32[]{:S(2)}) copy-start(bf16[8192,64]{0,1:T(8,128)(2,1)} %param.19) | copy-start | bytes 3145732
  3.3 27.8 %collective-permute-start = (bf16[4096,256]{1,0:T(8,128)(2,1)}, bf16[4096,256]{1,0:T(8,128)(2,1)}, u32[]{:S(2)}, u32[]{:S(2)}) collective-permute-start(bf16[4096,256]{1,0:T(8,128)(2,1)} %constant_dynamic-slice_fusion.1), channel_id=1, source_target_pairs={{0,1},{1,0},{2,3},{3,2},{4,5},{5,4},{6,7},{7,6},{8,9},{9,8},{10,11... | collective-permute-start | bytes 6291464 | tf_op jit(solution)/shard_map/ppermute | solution.py:329
  5.3 1.9 %copy-start.5 = (bf16[16,8192]{1,0:T(8,128)(2,1)S(1)}, bf16[16,8192]{1,0:T(8,128)(2,1)}, u32[]{:S(2)}) copy-start(bf16[16,8192]{1,0:T(8,128)(2,1)} %x_ref.1) | copy-start | bytes 786436
  5.3 1.9 %copy-start.7 = (bf16[16,32,128]{2,1,0:T(8,128)(2,1)S(1)}, bf16[16,32,128]{2,1,0:T(8,128)(2,1)}, u32[]{:S(2)}) copy-start(bf16[16,32,128]{2,1,0:T(8,128)(2,1)} %param.22) | copy-start | bytes 393220
  5.3 1.9 %copy-start.8 = (bf16[16,32,128]{2,1,0:T(8,128)(2,1)S(1)}, bf16[16,32,128]{2,1,0:T(8,128)(2,1)}, u32[]{:S(2)}) copy-start(bf16[16,32,128]{2,1,0:T(8,128)(2,1)} %param.23) | copy-start | bytes 393220
  5.3 1.9 %copy-start.9 = (f32[8192]{0:T(1024)S(1)}, f32[8192]{0:T(1024)}, u32[]{:S(2)}) copy-start(f32[8192]{0:T(1024)} %param.17) | copy-start | bytes 98308
  5.3 1.9 %copy-start.10 = (s32[16,1]{0,1:T(1,128)S(1)}, s32[16,1]{0,1:T(1,128)}, u32[]{:S(2)}) copy-start(s32[16,1]{0,1:T(1,128)} %param.24) | copy-start | bytes 196
  5.3 1.9 %copy-start.11 = (s32[8]{0:T(128)S(1)}, s32[8]{0:T(128)}, u32[]{:S(2)}) copy-start(s32[8]{0:T(128)} %param.25) | copy-start | bytes 100
  5.3 1.9 %copy-start.12 = (s32[16]{0:T(128)S(1)}, s32[16]{0:T(128)}, u32[]{:S(2)}) copy-start(s32[16]{0:T(128)} %param.26) | copy-start | bytes 196
  5.3 35.8 %collective-permute-start.5 = (bf16[256,4096]{1,0:T(8,128)(2,1)}, bf16[256,4096]{1,0:T(8,128)(2,1)}, u32[]{:S(2)}, u32[]{:S(2)}) collective-permute-start(bf16[256,4096]{1,0:T(8,128)(2,1)} %constant_dynamic-slice_fusion), channel_id=1, source_target_pairs={{0,1},{1,0},{2,3},{3,2},{4,5},{5,4},{6,7},{7,6},{8,9},{9,8},{10,11... | collective-permute-start | bytes 6291464 | tf_op jit(solution)/shard_map/ppermute | solution.py:333
  5.5 12.2 %collective-permute-start.3 = (bf16[64,640]{1,0:T(8,128)(2,1)S(1)}, bf16[64,640]{1,0:T(8,128)(2,1)S(1)}, u32[]{:S(2)}, u32[]{:S(2)}) collective-permute-start(bf16[64,640]{1,0:T(8,128)(2,1)S(1)} %pad_maximum_fusion.2), channel_id=1, source_target_pairs={{0,1},{1,0},{2,3},{3,2},{4,5},{5,4},{6,7},{7,6},{8,9},{9,8},{10,11... | collective-permute-start | bytes 245768 | tf_op jit(solution)/shard_map/ppermute | solution.py:344
  7.1 24.0 %collective-permute-start.1 = (bf16[128,4096]{1,0:T(8,128)(2,1)}, bf16[128,4096]{1,0:T(8,128)(2,1)}, u32[]{:S(2)}, u32[]{:S(2)}) collective-permute-start(bf16[128,4096]{1,0:T(8,128)(2,1)} %fusion), channel_id=1, source_target_pairs={{0,1},{1,0},{2,3},{3,2},{4,5},{5,4},{6,7},{7,6},{8,9},{9,8},{10,11... | collective-permute-start | bytes 3145736 | tf_op jit(solution)/shard_map/ppermute | solution.py:332
  8.8 22.3 %all-to-all-start = ((bf16[8,8,4224]{2,1,0:T(8,128)(2,1)}), bf16[8,8,4224]{2,1,0:T(8,128)(2,1)S(1)}, u32[]{:S(2)}, u32[]{:S(2)}) async-start(bf16[8,8,4224]{2,1,0:T(8,128)(2,1)} %bitcast.6), calls=%async_computation | async-start | bytes 1081344 | tf_op jit(solution)/shard_map/all_to_all | solution.py:317
  31.1 2.2 %copy-start.2 = (bf16[8192,256]{1,0:T(8,128)(2,1)S(1)}, bf16[8192,256]{1,0:T(8,128)(2,1)}, u32[]{:S(2)}) copy-start(bf16[8192,256]{1,0:T(8,128)(2,1)} %wq_ref.1) | copy-start | bytes 12582916
  33.3 1.4 %copy-start.3 = (bf16[1,4096,192]{1,2,0:T(8,128)(2,1)S(1)}, bf16[1,4096,192]{1,2,0:T(8,128)(2,1)}, u32[]{:S(2)}) copy-start(bf16[1,4096,192]{1,2,0:T(8,128)(2,1)} %param.27) | copy-start | bytes 4718596
  34.7 7.4 %copy-start.1 = (bf16[256,8192]{1,0:T(8,128)(2,1)S(1)}, bf16[256,8192]{1,0:T(8,128)(2,1)}, u32[]{:S(2)}) copy-start(bf16[256,8192]{1,0:T(8,128)(2,1)} %wo_ref.1) | copy-start | bytes 12582916
  38.7 3.4 %copy-start.4 = (bf16[1,64,4096]{2,1,0:T(8,128)(2,1)S(1)}, bf16[1,64,4096]{2,1,0:T(8,128)(2,1)}, u32[]{:S(2)}) copy-start(bf16[1,64,4096]{2,1,0:T(8,128)(2,1)} %param.31) | copy-start | bytes 1572868
  38.7 1.3 %collective-permute-start.2 = (f32[16,1024]{1,0:T(8,128)S(1)}, f32[16,1024]{1,0:T(8,128)S(1)}, u32[]{:S(2)}, u32[]{:S(2)}) collective-permute-start(f32[16,1024]{1,0:T(8,128)S(1)} %get-tuple-element.13), channel_id=1, source_target_pairs={{0,1},{1,0},{2,3},{3,2},{4,5},{5,4},{6,7},{7,6},{8,9},{9,8},{10,11... | collective-permute-start | bytes 196616 | tf_op jit(solution)/shard_map/ppermute | solution.py:377
  40.8 1.2 %collective-permute-start.4 = (bf16[16,512]{1,0:T(8,128)(2,1)S(1)}, bf16[16,512]{1,0:T(8,128)(2,1)S(1)}, u32[]{:S(2)}, u32[]{:S(2)}) collective-permute-start(bf16[16,512]{1,0:T(8,128)(2,1)S(1)} %shard_map.157.mine_ref), channel_id=1, source_target_pairs={{0,1},{1,0},{2,3},{3,2},{4,5},{5,4},{6,7},{7,6},{8,9},{9,8},{10,11... | collective-permute-start | bytes 49160 | tf_op jit(solution)/shard_map/ppermute | solution.py:385

commit v2 on v1

--- a/solution.py
+++ b/solution.py
@@ -15,7 +15,8 @@
 BF16 = jnp.bfloat16
 F32 = jnp.float32
 SWAP = [(0, 1), (1, 0)]
-VMEM_LIMIT = 40 * 1024 * 1024
+STEPS = 4
+MIB = 1024 * 1024
 
 
 def nn(a, b):
@@ -53,8 +54,30 @@
     return owner, standing
 
 
-def pack_kernel(capacity, x_ref, gain_ref, k_ref, v_ref, named_ref, table_ref, length_ref, out_ref, flat_ref, spread_ref):
+def copy_all(pairs, sems):
+    copies = [pltpu.make_async_copy(a, b, sems.at[i]) for i, (a, b) in enumerate(pairs)]
+    for copy in copies:
+        copy.start()
+    return copies
+
+
+def pack_kernel(capacity, x_hbm, gain_hbm, k_hbm, v_hbm, named_hbm, table_hbm, length_hbm, out_ref, x_ref, gain_ref, k_ref, v_ref, named_ref, table_ref, length_ref, flat_ref, spread_ref, sems):
     core = lax.axis_index("tensor")
+    named_copy, table_copy, length_copy, x_copy, gain_copy, k_copy, v_copy = copy_all(
+        [
+            (named_hbm, named_ref),
+            (table_hbm, table_ref),
+            (length_hbm, length_ref),
+            (x_hbm, x_ref),
+            (gain_hbm, gain_ref),
+            (k_hbm, k_ref),
+            (v_hbm, v_ref),
+        ],
+        sems,
+    )
+    named_copy.wait()
+    table_copy.wait()
+    length_copy.wait()
     requests, width = x_ref.shape
     half = width // 2
     positions = k_ref.shape[0] // requests
@@ -70,11 +93,14 @@
     put_k = ones_where(order == k_row)
     put_v = ones_where(order == k_row + 1)
 
+    x_copy.wait()
+    gain_copy.wait()
     floats = x_ref[...].astype(F32)
     scale = lax.rsqrt(jnp.mean(floats * floats, axis=1, keepdims=True) + EPSILON)
     mine = pl.ds(pl.multiple_of(core * half, half), half)
     flat_ref[0:requests, :] = (x_ref[:, mine].astype(F32) * scale * gain_ref[:, mine]).astype(BF16)
-    for first, source in ((requests, k_ref), (2 * requests, v_ref)):
+    for first, source, copy in ((requests, k_ref, k_copy), (2 * requests, v_ref, v_copy)):
+        copy.wait()
         spread_ref[...] = source[...].astype(F32)
         for p in range(positions):
             flat_ref[first : first + requests, p * LANES : (p + 1) * LANES] = spread_ref[
@@ -92,35 +118,58 @@
     out_ref[:, half:] = nn(put_x, lengths).astype(BF16)
 
 
-def project_kernel(capacity, owners, buf_ref, wq_ref, wq_other_ref, kv_ref, kv_other_ref, down_ref, mine_ref, theirs_ref, sums_ref):
-    core = lax.axis_index("tensor")
-    half = wq_other_ref.shape[0]
+def project_kernel(capacity, owners, buf_ref, wq_hbm, wk_hbm, wv_hbm, down_hbm, *rest):
+    wq_other_hbm, kv_other_hbm = rest[:STEPS], rest[STEPS : 2 * STEPS]
+    mine_ref, theirs_ref, q_ref, narrow_ref, sums_ref, sems = rest[2 * STEPS :]
+    half, qcols = q_ref.shape[0], wq_hbm.shape[1]
+    hcols = wk_hbm.shape[0]
+    kvcols = 2 * hcols
     per_owner = 2 * capacity
     here = capacity // 2
-    buf = buf_ref[:, :half]
-    rows = pl.ds(pl.multiple_of(core * half, half), half)
-    ranks = nt(buf, down_ref[...])
-    spare = jnp.zeros((buf.shape[0], -ranks.shape[1] % LANES), F32)
-    parts = [
-        nn(buf, wq_ref[rows, :]),
-        nn(buf, wq_other_ref[...]),
-        nt(buf, kv_ref[:, rows]),
-        nt(buf, kv_other_ref[...]),
-        jnp.concatenate([ranks, spare], axis=1),
-    ]
+    rows = buf_ref.shape[0]
+    start = lax.axis_index("tensor") * half
+    step = half // STEPS
+    waiting = []
+    for n in range(STEPS):
+        part = pl.ds(n * step, step)
+        span = pl.ds(pl.multiple_of(start + n * step, step), step)
+        pairs = [
+            (wq_hbm.at[span, :], q_ref.at[part, 0:qcols]),
+            (wq_other_hbm[n], q_ref.at[part, qcols : 2 * qcols]),
+            (wk_hbm.at[:, span], narrow_ref.at[0:hcols, part]),
+            (wv_hbm.at[:, span], narrow_ref.at[hcols:kvcols, part]),
+            (kv_other_hbm[n], narrow_ref.at[kvcols : 2 * kvcols, part]),
+            (down_hbm.at[:, part], narrow_ref.at[2 * kvcols :, part]),
+        ]
+        waiting.append(copy_all(pairs, sems.at[n]))
+    wide = jnp.zeros((rows, 2 * qcols), F32)
+    narrow = jnp.zeros((rows, narrow_ref.shape[0]), F32)
+    for n in range(STEPS):
+        for copy in waiting[n]:
+            copy.wait()
+        part = slice(n * step, (n + 1) * step)
+        buf = buf_ref[:, part]
+        wide += nn(buf, q_ref[part, :])
+        narrow += nt(buf, narrow_ref[:, part])
+    spare = jnp.zeros((rows, -narrow.shape[1] % LANES), F32)
     tile = 0
-    for part in parts:
+    for part in (wide, jnp.concatenate([narrow, spare], axis=1)):
         for c in range(0, part.shape[1], LANES):
-            sums_ref[...] = part[:, c : c + LANES]
+            sums_ref[tile] = part[:, c : c + LANES]
             columns = slice(tile * LANES, (tile + 1) * LANES)
             for i in range(here):
                 to = slice(i * owners, (i + 1) * owners)
-                mine_ref[to, columns] = sums_ref[pl.ds(i, owners, stride=per_owner), :]
-                theirs_ref[to, columns] = sums_ref[pl.ds(here + i, owners, stride=per_owner), :]
+                mine_ref[to, columns] = sums_ref[tile, pl.ds(i, owners, stride=per_owner), :]
+                theirs_ref[to, columns] = sums_ref[
+                    tile, pl.ds(here + i, owners, stride=per_owner), :
+                ]
             tile += 1
 
 
-def unpack_kernel(capacity, owners, buf_ref, k_ref, v_ref, length_ref, cosine_ref, sine_ref):
+def unpack_kernel(capacity, owners, buf_ref, wo_hbm, k_ref, v_ref, length_ref, cosine_ref, sine_ref, wo_ref, sems):
+    columns = wo_ref.shape[1]
+    span = pl.ds(pl.multiple_of(lax.axis_index("tensor") * columns, columns), columns)
+    copies = copy_all([(wo_hbm.at[:, span], wo_ref)], sems)
     rows = buf_ref.shape[0]
     slots = owners * capacity // 2
     positions = k_ref.shape[0] // slots
@@ -150,9 +199,21 @@
     cosine_ref[...] = jnp.cos(angle)
     sine = jnp.sin(angle)
     sine_ref[...] = jnp.where(lane < halfway, -sine, sine)
-
-
-def attend_kernel(mine_ref, theirs_ref, up_ref, k_ref, v_ref, length_ref, cosine_ref, sine_ref, out_ref):
+    for copy in copies:
+        copy.wait()
+
+
+def attend_kernel(mine_ref, theirs_ref, up_ref, k_ref, v_ref, length_ref, cosine_ref, sine_ref, out_up_hbm, *rest):
+    wo_other_hbm = rest[:STEPS]
+    out_ref, wo_other_ref, out_up_ref, sems = rest[STEPS:]
+    step = wo_other_ref.shape[1] // STEPS
+    copies = copy_all(
+        [(out_up_hbm, out_up_ref)]
+        + [
+            (wo_other_hbm[n], wo_other_ref.at[:, n * step : (n + 1) * step]) for n in range(STEPS)
+        ],
+        sems,
+    )
     core = lax.axis_index("tensor")
     slots = mine_ref.shape[0]
     ucols = up_ref.shape[1]
@@ -212,6 +273,8 @@
     attended = (nn(weights, v_ref[...]) + nn(own_weights, own_value)).astype(BF16)
     for h in range(heads):
         out_ref[:, h * HEAD_SIZE : (h + 1) * HEAD_SIZE] = attended[h * slots : (h + 1) * slots]
+    for copy in copies:
+        copy.wait()
 
 
 def output_kernel(capacity, owners, mine_ref, theirs_ref, wo_ref, wo_other_ref, down_ref, down_other_ref, up_ref, out_ref):
@@ -235,9 +298,8 @@
     ranks = (nt(left, down_ref[...]) + nt(right, down_other_ref[...])).astype(BF16)
     step = 512
     for c in range(0, half, step):
-        columns = pl.ds(pl.multiple_of(core * half + c, step), step)
         delta = nn(ranks, up_ref[:, c : c + step]).astype(BF16).astype(F32)
-        terms = nn(left, wo_ref[:, columns]) + nn(right, wo_other_ref[:, c : c + step])
+        terms = nn(left, wo_ref[:, c : c + step]) + nn(right, wo_other_ref[:, c : c + step])
         out_ref[:, c : c + step] = (terms + delta).astype(BF16)
 
 
@@ -256,18 +318,26 @@
         ).astype(BF16)
 
 
-def call(kernel, outs, scratch=(), flops=0, moved=0):
+OUTSIDE = pl.BlockSpec(memory_space=pltpu.HBM)
+INSIDE = pl.BlockSpec(memory_space=pltpu.VMEM)
+
+
+def call(kernel, outs, scratch=(), vmem=8, outside=(), out_spec=INSIDE, moved=0):
     many = isinstance(outs, (list, tuple))
-    spec = pl.BlockSpec(memory_space=pltpu.VMEM)
     return lambda *args: pl.pallas_call(
         kernel,
         out_shape=outs,
-        in_specs=[spec] * len(args),
-        out_specs=[spec] * len(outs) if many else spec,
+        in_specs=[OUTSIDE if i in outside else INSIDE for i in range(len(args))],
+        out_specs=[out_spec] * len(outs) if many else out_spec,
         scratch_shapes=list(scratch),
-        compiler_params=pltpu.CompilerParams(vmem_limit_bytes=VMEM_LIMIT),
-        cost_estimate=pl.CostEstimate(flops=flops, bytes_accessed=moved, transcendentals=0),
-    )(*args)
+        compiler_params=pltpu.CompilerParams(vmem_limit_bytes=vmem * MIB),
+        cost_estimate=pl.CostEstimate(flops=0, bytes_accessed=moved, transcendentals=0),
+    )(
+        *[
+            pltpu.with_memory_space_constraint(arg, pltpu.HBM) if i in outside else arg
+            for i, arg in enumerate(args)
+        ]
+    )
 
 
 def body(
@@ -296,7 +366,6 @@
     capacity = max(2, 2 * ((requests + adapters - 1) // adapters))
     rows = owners * 2 * capacity
     slots = owners * capacity // 2
-    core = lax.axis_index("tensor")
     named = request_adapter.reshape(1, requests)
     table = adapter_row_table.reshape(1, adapters)
     shape = jax.ShapeDtypeStruct
@@ -304,7 +373,19 @@
     packed = call(
         functools.partial(pack_kernel, capacity),
         shape((rows, half + LANES), BF16),
-        [pltpu.VMEM((3 * requests, half), BF16), pltpu.VMEM((positions * requests, LANES), F32)],
+        [
+            pltpu.VMEM((requests, width), BF16),
+            pltpu.VMEM((1, width), F32),
+            pltpu.VMEM((positions * requests, LANES), BF16),
+            pltpu.VMEM((positions * requests, LANES), BF16),
+            pltpu.VMEM((1, requests), jnp.int32),
+            pltpu.VMEM((1, adapters), jnp.int32),
+            pltpu.VMEM((1, requests), jnp.int32),
+            pltpu.VMEM((3 * requests, half), BF16),
+            pltpu.VMEM((positions * requests, LANES), F32),
+            pltpu.SemaphoreType.DMA((7,)),
+        ],
+        outside=range(7),
     )(
         layer_input,
         input_norm_gain.reshape(1, width),
@@ -314,6 +395,27 @@
         table,
         cached_length.reshape(1, requests),
     )
+    (
+        packed,
+        query_projection,
+        key_projection,
+        value_projection,
+        output_projection,
+        query_adapter_up,
+        key_value_adapter_up,
+        output_adapter_down,
+    ) = lax.optimization_barrier(
+        (
+            packed,
+            query_projection,
+            key_projection,
+            value_projection,
+            output_projection,
+            query_adapter_up,
+            key_value_adapter_up,
+            output_adapter_down,
+        )
+    )
     arrived = lax.all_to_all(
         packed.reshape(owners, 2 * capacity, half + LANES),
         "adapter",
@@ -322,19 +424,40 @@
         tiled=True,
     ).reshape(rows, half + LANES)
 
-    other = (1 - core) * half
     qcols = query_projection.shape[1]
-    kv = jnp.concatenate([key_projection.T, value_projection.T], axis=0)
-    kvcols = kv.shape[0]
-    wq_other = lax.ppermute(
-        lax.dynamic_slice(query_projection, (other, 0), (half, qcols)), "tensor", SWAP
-    )
-    kv_other = lax.ppermute(lax.dynamic_slice(kv, (0, other), (kvcols, half)), "tensor", SWAP)
-    wo_other = lax.ppermute(
-        lax.dynamic_slice(output_projection, (0, other), (output_projection.shape[0], half)),
-        "tensor",
-        SWAP,
-    )
+    wk, wv = key_projection.T, value_projection.T
+    kvcols = 2 * wk.shape[0]
+    other = (1 - lax.axis_index("tensor")) * half
+    hrows = output_projection.shape[0]
+    step = half // STEPS
+    wq_other = [
+        lax.ppermute(
+            lax.dynamic_slice(query_projection, (other + n * step, 0), (step, qcols)), "tensor", SWAP
+        )
+        for n in range(STEPS)
+    ]
+    kv_other = [
+        lax.ppermute(
+            jnp.concatenate(
+                [
+                    lax.dynamic_slice(w, (0, other + n * step), (kvcols // 2, step))
+                    for w in (wk, wv)
+                ],
+                axis=0,
+            ),
+            "tensor",
+            SWAP,
+        )
+        for n in range(STEPS)
+    ]
+    wo_other = [
+        lax.ppermute(
+            lax.dynamic_slice(output_projection, (0, other + n * step), (hrows, step)),
+            "tensor",
+            SWAP,
+        )
+        for n in range(STEPS)
+    ]
     query_up = query_adapter_up[0]
     rank = query_up.shape[0]
     kv_up = key_value_adapter_up[0]
@@ -369,31 +492,52 @@
     ucols = 2 * qcols + 2 * kvcols
     pcols = ucols + (down.shape[0] + LANES - 1) // LANES * LANES
 
+    narrow_rows = 2 * kvcols + down.shape[0]
     mine, theirs = call(
         functools.partial(project_kernel, capacity, owners),
         [shape((slots, pcols), F32), shape((slots, pcols), F32)],
-        [pltpu.VMEM((rows, LANES), F32)],
-    )(arrived, query_projection, wq_other, kv, kv_other, down)
+        [
+            pltpu.VMEM((half, 2 * qcols), BF16),
+            pltpu.VMEM((narrow_rows, half), BF16),
+            pltpu.VMEM((pcols // LANES, rows, LANES), F32),
+            pltpu.SemaphoreType.DMA((STEPS, 6)),
+        ],
+        vmem=24,
+        outside=range(1, 5 + 2 * STEPS),
+    )(arrived, query_projection, wk, wv, down, *wq_other, *kv_other)
     theirs = lax.ppermute(theirs, "tensor", SWAP)
-    keys, values, lengths, cosine, sine = call(
+    keys, values, lengths, cosine, sine, wo_mine = call(
         functools.partial(unpack_kernel, capacity, owners),
-        [shape((slots * positions, HEAD_SIZE), BF16)] * 2 + [shape((slots, LANES), F32)] * 3,
-    )(arrived)
-    attended = call(attend_kernel, shape((slots, 2 * qcols), BF16))(
-        mine, theirs, up, keys, values, lengths, cosine, sine
-    )
+        [shape((slots * positions, HEAD_SIZE), BF16)] * 2
+        + [shape((slots, LANES), F32)] * 3
+        + [shape((hrows, half), BF16)],
+        [pltpu.SemaphoreType.DMA((1,))],
+        outside=(1,),
+    )(arrived, output_projection)
+    attended, wo_other, out_up = call(
+        attend_kernel,
+        [
+            shape((slots, 2 * qcols), BF16),
+            shape((hrows, half), BF16),
+            shape((rank, half), BF16),
+        ],
+        [pltpu.SemaphoreType.DMA((1 + STEPS,))],
+        vmem=16,
+        outside=range(8, 9 + STEPS),
+    )(mine, theirs, up, keys, values, lengths, cosine, sine, output_adapter_up[0], *wo_other)
     attended_other = lax.ppermute(attended, "tensor", SWAP)
     finished = call(
         functools.partial(output_kernel, capacity, owners),
         shape((owners * capacity, half), BF16),
+        vmem=16,
     )(
         attended,
         attended_other,
-        output_projection,
+        wo_mine,
         wo_other,
         out_down,
         out_down_other,
-        output_adapter_up[0],
+        out_up,
     )
     back = lax.all_to_all(
         finished.reshape(owners, capacity, half), "adapter", split_axis=0, concat_axis=0, tiled=True

time: 59 us -> 52 us (0.88)
  waiting for transfers between devices: 15 us -> 4.48 us
  starting transfers between devices: 8.76 us -> 11.6 us
  Pallas kernels: 10.3 us -> 12.7 us
  other arithmetic: 2.86 us -> 0.95 us
  local copies, waits for them, and re-layouts: 8.85 us -> 7.58 us
  blocking collectives: 12.7 us -> 13.9 us
    all_to_all x1, waiting for transfers between devices: 13 us -> 1.43 us  [body(): lax.all_to_all(packed.reshape(owners, 2 * capacity, half + LANES), 'adapt...]
    ppermute x3 -> x12, starting transfers between devices: 0.7 us -> 3.65 us  [the longest x4 1.35 us: body(): lax.ppermute(lax.dynamic_slice(query_projection, (other + n * step, 0), (...]
    concatenate x2 -> x4, other arithmetic: 2.75 us -> 0.07 us  [body(): jnp.concatenate([lax.dynamic_slice(w, (0, other + n * step), (kvcols // 2...]
    unnamed x34 -> x28, local copies, waits for them, and re-layouts: 3.66 us -> 1.01 us
    pallas_call x6, Pallas kernels: 10.3 us -> 12.7 us  [call(): pl.pallas_call(kernel, out_shape=outs, in_specs=[OUTSIDE if i in outside...]
    ppermute x3 -> x12, waiting for transfers between devices: 0.01 us -> 2.2 us  [the longest x4 2.18 us: body(): lax.ppermute(jnp.concatenate([lax.dynamic_slice(w, (0, other + n * step),...]
    all_to_all x1, blocking collectives: 12.7 us -> 13.9 us  [body(): lax.all_to_all(finished.reshape(owners, capacity, half), 'adapter', split...]
    ppermute x1, waiting for transfers between devices: 0.92 us -> 0.01 us  [body(): theirs = lax.ppermute(theirs, 'tensor', SWAP)]
  transfers between devices with their start and end apart: 7 -> 16, of which waited for: 3 -> 3; matrix products, arithmetic and copies ran while one was open for 8% -> 14% of each run, Pallas kernels for 11% -> 12%
where the time goes in v2:
time: 52 us; the launch traced here: 51.6 us
  blocking collectives  13.9 us (27%)
  Pallas kernels  12.7 us (24%)
  starting transfers between devices  11.6 us (22%)
  local copies, waits for them, and re-layouts  7.58 us (15%)
  waiting for transfers between devices  4.48 us (9%)
  other arithmetic  0.95 us (2%)
    all_to_all x1, blocking collectives, body(): lax.all_to_all(finished.reshape(owners, capacity, half), 'adapter', split...  13.9 us
    pallas_call x6, Pallas kernels, call(): pl.pallas_call(kernel, out_shape=outs, in_specs=[OUTSIDE if i in outside...  12.7 us
    all_to_all x1, starting transfers between devices, body(): lax.all_to_all(packed.reshape(owners, 2 * capacity, half + LANES), 'adapt...  7.27 us
    dynamic_slice x1, local copies, waits for them, and re-layouts, body(): lax.dynamic_slice(query_projection, (other + n * step, 0), (step, qcols))  2.44 us
    ppermute x4, waiting for transfers between devices, body(): lax.ppermute(jnp.concatenate([lax.dynamic_slice(w, (0, other + n * step),...  2.18 us
    dynamic_slice x1, local copies, waits for them, and re-layouts, body(): lax.dynamic_slice(w, (0, other + n * step), (kvcols // 2, step))  1.52 us
    all_to_all x1, waiting for transfers between devices, body(): lax.all_to_all(packed.reshape(owners, 2 * capacity, half + LANES), 'adapt...  1.43 us
    dynamic_slice x1, local copies, waits for them, and re-layouts, body(): lax.dynamic_slice(output_projection, (0, other + n * step), (hrows, step))  1.4 us
  transfers between devices with their start and end apart: 16, of which 3 were waited for; matrix products, arithmetic and copies ran while one was open for 14% of the time, Pallas kernels for 12%

profile of v2, /device:TPU:0, one launch (start us, length us, event | category | flops | bytes accessed | tf_op | source)
XLA Modules:
  0.0 51.6 jit_solution(12156536997235714970)
XLA Ops:
  0.0 2.6 %shard_map.154 = bf16[64,4224]{1,0:T(8,128)(2,1)} custom-call(bf16[16,8192]{1,0:T(8,128)(2,1)} %x_hbm.1, f32[1,8192]{1,0:T(1,128)} %bitcast.54, bf16[512,128]{1,0:T(8,128)(2,1)} %bitcast.50, bf16[512,128]{1,0:T(8,128)(2,1)} %bitcast.51, s32[1,16]{1,0:T(1,128)} %bitcast.42, s32[1,8]{1,0:T(1,128)} %bitcast.44, s32[1,16]{1,0:T(1,128)} %bitcast.55), custom_call_target="tpu_custom_call" | custom-call | tf_op jit(solution)/shard_map/pallas_call | solution.py:327
  2.6 7.3 %all-to-all-start = ((bf16[8,8,4224]{2,1,0:T(8,128)(2,1)}), bf16[8,8,4224]{2,1,0:T(8,128)(2,1)S(1)}, u32[]{:S(2)}, u32[]{:S(2)}) async-start(bf16[8,8,4224]{2,1,0:T(8,128)(2,1)} %bitcast.6), calls=%async_computation | async-start | bytes 1081344 | tf_op jit(solution)/shard_map/all_to_all | solution.py:419
  9.9 0.7 %slice_bitcast_fusion.1 = (bf16[64,64]{1,0:T(8,128)(2,1)S(1)}, bf16[64,64]{1,0:T(8,128)(2,1)S(1)}) fusion(bf16[1,2,64,64]{3,2,1,0:T(8,128)(2,1)} %param.29), kind=kLoop, calls=%fused_computation.15 | loop fusion | bytes 32768 | tf_op jit(solution)/shard_map/squeeze | solution.py:466
  10.6 0.9 %pad_maximum_fusion.5 = bf16[64,640]{1,0:T(8,128)(2,1)S(1)} fusion(bf16[64,256]{1,0:T(8,128)(2,1)} %bitcast.40, bf16[64,64]{1,0:T(8,128)(2,1)S(1)} %get-tuple-element.64, bf16[64,64]{1,0:T(8,128)(2,1)S(1)} %get-tuple-element.63, bf16[64,256]{1,0:T(8,128)(2,1)} %bitcast.52), kind=kLoop, calls=%fused_computation.13 | loop fusion | flops 327680 | bytes 163840 | tf_op jit(solution)/shard_map/concatenate | solution.py:466
  11.5 0.1 collective-permute-start.9
  11.5 0.0 copy-start.3
  11.6 1.5 %dynamic-slice_bitcast_fusion = (bf16[64,1024]{1,0:T(8,128)(2,1)S(1)}, bf16[64,1024]{1,0:T(8,128)(2,1)S(1)}, bf16[64,1024]{1,0:T(8,128)(2,1)S(1)}, bf16[64,1024]...) fusion(bf16[8192,64]{0,1:T(8,128)(2,1)} %param.20, ...), kind=kLoop, calls=%fused_computation.5 | loop fusion | bytes 2097168 | tf_op jit(solution)/shard_map/dynamic_slice | solution.py:443
  13.1 0.5 %collective-permute-start.4 = (bf16[128,1024]{1,0:T(8,128)(2,1)S(1)}, bf16[128,1024]{1,0:T(8,128)(2,1)S(1)}, u32[]{:S(2)}, u32[]{:S(2)}) collective-permute-start(bf16[128,1024]{1,0:T(8,128)(2,1)S(1)} %pad_maximum_fusion.1), channel_id=1, source_target_pairs={{0,1},{1,0},{2,3},{3,2},{4,5},{5,4},{6,7},{7,6},{8,9},{9,8},{10,11... | collective-permute-start | bytes 786440 | tf_op jit(solution)/shard_map/ppermute | solution.py:440
  13.7 0.1 collective-permute-start.5
  13.8 2.4 %constant_dynamic-slice_fusion.4 = (bf16[1024,256]{1,0:T(8,128)(2,1)S(1)}, bf16[1024,256]{1,0:T(8,128)(2,1)S(1)}, bf16[1024,256]{1,0:T(8,128)(2,1)S(1)}, bf16[1024,256]{1,0:T(8,128)(2,1)}) fusion(bf16[8192,256]{1,0:T(8,128)(2,1)} %wq_hbm, s32[]{:T(128)S(6)} %select_n.11, s32[]{:T(128)S(6)} %select_n.10, s32[]{:T(128)S(6)} %select_n.9, s32[]{:T(128)S(6)} %select_n.8), kind=kLoop, calls=%fused_computation.20 | loop fusion | bytes 4194320 | tf_op jit(solution)/shard_map/dynamic_slice | solution.py:435
  16.2 0.5 collective-permute-start.3
  16.7 0.0 collective-permute-start.2
  16.7 0.0 collective-permute-done.9
  16.7 0.5 collective-permute-start.1
  17.2 0.0 collective-permute-done.4.rest_4_
  17.2 0.1 collective-permute-start.6
  17.4 0.0 collective-permute-done.5.rest_5_
  17.4 0.5 %collective-permute-start.7 = (bf16[128,1024]{1,0:T(8,128)(2,1)S(1)}, bf16[128,1024]{1,0:T(8,128)(2,1)S(1)}, u32[]{:S(2)}, u32[]{:S(2)}) collective-permute-start(bf16[128,1024]{1,0:T(8,128)(2,1)S(1)} %pad_maximum_fusion.4), channel_id=1, source_target_pairs={{0,1},{1,0},{2,3},{3,2},{4,5},{5,4},{6,7},{7,6},{8,9},{9,8},{10,11... | collective-permute-start | bytes 786440 | tf_op jit(solution)/shard_map/ppermute | solution.py:440
  17.9 2.2 %collective-permute-done.6.rest_6_ = bf16[128,1024]{1,0:T(8,128)(2,1)S(1)} collective-permute-done((bf16[128,1024]{1,0:T(8,128)(2,1)S(1)}, bf16[128,1024]{1,0:T(8,128)(2,1)S(1)}, u32[]{:S(2)}, u32[]{:S(2)}) %collective-permute-start.6) | collective-permute-done | bytes 262176 | tf_op jit(solution)/shard_map/ppermute | solution.py:440
  20.1 0.4 collective-permute-start
  20.5 1.4 %constant_dynamic-slice_fusion = (bf16[256,1024]{1,0:T(8,128)(2,1)}, bf16[256,1024]{1,0:T(8,128)(2,1)}, bf16[256,1024]{1,0:T(8,128)(2,1)}, bf16[256,1024]{1,0:T(8,128)(2,1)}) fusion(bf16[256,8192]{1,0:T(8,128)(2,1)S(1)} %copy-done.3, s32[]{:T(128)S(6)} %select_n.11, s32[]{:T(128)S(6)} %select_n.10, s32[]{:T(128)S(6)} %select_n.9, s32[]{:T(128)S(6)} %select_n.8), kind=kLoop, calls=%fused_computation.16 | loop fusion | bytes 4194320 | tf_op jit(solution)/shard_map/dynamic_slice | solution.py:455
  21.9 0.1 collective-permute-start.13
  22.0 0.4 collective-permute-start.12
  22.4 0.0 collective-permute-done.2.rest_2_
  22.4 0.1 collective-permute-start.11
  22.5 0.0 collective-permute-done.1.rest_1_
  22.5 0.4 collective-permute-start.10
  22.9 0.1 fusion.1
  23.1 0.1 concatenate.33
  23.1 0.1 concatenate.34
  23.3 1.4 %all-to-all-done = bf16[8,8,4224]{2,1,0:T(8,128)(2,1)S(1)} async-done(((bf16[8,8,4224]{2,1,0:T(8,128)(2,1)}), bf16[8,8,4224]{2,1,0:T(8,128)(2,1)S(1)}, u32[]{:S(2)}, u32[]{:S(2)}) %all-to-all-start) | async-done | bytes 540704 | tf_op jit(solution)/shard_map/all_to_all | solution.py:419
  24.7 0.0 copy-start.13
  24.7 4.3 %shard_map.155 = (f32[16,1024]{1,0:T(8,128)S(1)}, f32[16,1024]{1,0:T(8,128)S(1)}) custom-call(bf16[64,4224]{1,0:T(8,128)(2,1)S(1)} %bitcast.38, bf16[8192,256]{1,0:T(8,128)(2,1)} %wq_hbm, bf16[64,8192]{1,0:T(8,128)(2,1)} %bitcast.46, bf16[64,8192]{1,0:T(8,128)(2,1)} %bitcast.47, bf16[192,4096]{1,0:T(8,128)(2,1)} %bitcast.48, ...), custom_call_target="tpu_custom_call" | custom-call | tf_op jit(solution)/shard_map/pallas_call | solution.py:327
  29.1 0.1 collective-permute-start.8
  29.2 0.0 copy-start
  29.2 1.7 %shard_map.156 = (bf16[512,128]{1,0:T(8,128)(2,1)S(1)}, bf16[512,128]{1,0:T(8,128)(2,1)S(1)}, f32[16,128]{1,0:T(8,128)S(1)}, f32[16,128]{1,0:T(8,128)S(1)}, f32[...) custom-call(bf16[64,4224]{1,0:T(8,128)(2,1)S(1)} %bitcast.39, bf16[256,8192]{1,0:T(8,128)(2,1)} %wo_hbm), custom_call_target="tpu_custom_call" | custom-call | tf_op jit(solution)/shard_map/pallas_call | solution.py:327
  31.0 0.0 collective-permute-done.11.rest_1_
  31.0 0.0 collective-permute-done.10.rest_0_
  31.0 0.7 %copy-done.7 = bf16[256,1024]{1,0:T(8,128)(2,1)} copy-done((bf16[256,1024]{1,0:T(8,128)(2,1)}, bf16[256,1024]{1,0:T(8,128)(2,1)S(1)}, u32[]{:S(2)}) %copy-start.7) | copy-done | bytes 524312
  31.8 0.2 copy-done.8
  32.0 2.0 %shard_map.157 = (bf16[16,512]{1,0:T(8,128)(2,1)S(1)}, bf16[256,4096]{1,0:T(8,128)(2,1)S(1)}, bf16[64,4096]{1,0:T(8,128)(2,1)S(1)}) custom-call(f32[16,1024]{1,0:T(8,128)S(1)} %get-tuple-element.28.mine_ref, f32[16,1024]{1,0:T(8,128)S(1)} %collective-permute-done.8.theirs_ref, bf16[192,768]{1,0:T(8,128)(2,1)S(1)} %pad_maximum_fusion.up_ref, ...), custom_call_target="tpu_custom_call" | custom-call | tf_op jit(solution)/shard_map/pallas_call | solution.py:327
  34.0 0.5 %collective-permute-start.14 = (bf16[16,512]{1,0:T(8,128)(2,1)S(1)}, bf16[16,512]{1,0:T(8,128)(2,1)S(1)}, u32[]{:S(2)}, u32[]{:S(2)}) collective-permute-start(bf16[16,512]{1,0:T(8,128)(2,1)S(1)} %get-tuple-element.39.mine_ref), channel_id=1, source_target_pairs={{0,1},{1,0},{2,3},{3,2},{4,5},{5,4},{6,7},{7,6},{8,9},{9,8},{10,11... | collective-permute-start | bytes 49160 | tf_op jit(solution)/shard_map/ppermute | solution.py:528
  34.5 0.8 %collective-permute-done.14.theirs_ref = bf16[16,512]{1,0:T(8,128)(2,1)S(1)} collective-permute-done((bf16[16,512]{1,0:T(8,128)(2,1)S(1)}, bf16[16,512]{1,0:T(8,128)(2,1)S(1)}, u32[]{:S(2)}, u32[]{:S(2)}) %collective-permute-start.14) | collective-permute-done | bytes 16416 | tf_op jit(solution)/shard_map/ppermute | solution.py:528
  35.4 1.0 %shard_map.158 = bf16[32,4096]{1,0:T(8,128)(2,1)S(1)} custom-call(bf16[16,512]{1,0:T(8,128)(2,1)S(1)} %get-tuple-element.39.mine_ref, bf16[16,512]{1,0:T(8,128)(2,1)S(1)} %collective-permute-done.14.theirs_ref, bf16[256,4096]{1,0:T(8,128)(2,1)S(1)} %get-tuple-element.40.wo_ref, bf16[256,4096]{1,0:T(8,128)(2,1)S(1)} %get-tuple-element.41.wo_other_ref, ...), custom_call_target="tpu_custom_call" | custom-call | tf_op jit(solution)/shard_map/pallas_call | solution.py:327
  36.4 0.1 reshape.42
  36.5 13.9 %all_to_all.10 = bf16[8,4,4096]{2,1,0:T(4,128)(2,1)S(1)} all-to-all(bf16[8,4,4096]{2,1,0:T(4,128)(2,1)S(1)} %reshape.42), channel_id=1, replica_groups=mesh['groups'=2,'adapter'=8,'tensor'=2] {'adapter'}, dimensions={0} | all-to-all | bytes 524288 | tf_op jit(solution)/shard_map/all_to_all | solution.py:542
  50.4 0.1 reshape.43.back_ref
  50.5 1.1 %shard_map.159 = bf16[16,4096]{1,0:T(8,128)(2,1)} custom-call(bf16[32,4096]{1,0:T(8,128)(2,1)S(1)} %reshape.43.back_ref, s32[1,16]{1,0:T(1,128)S(1)} %bitcast.43, s32[1,8]{1,0:T(1,128)S(1)} %bitcast.45), custom_call_target="tpu_custom_call" | custom-call | tf_op jit(solution)/shard_map/pallas_call | solution.py:327
  (38 shorter events, 0.2 us)
Async XLA Ops:
  2.6 22.1 %all-to-all-start = ((bf16[8,8,4224]{2,1,0:T(8,128)(2,1)}), bf16[8,8,4224]{2,1,0:T(8,128)(2,1)S(1)}, u32[]{:S(2)}, u32[]{:S(2)}) async-start(bf16[8,8,4224]{2,1,0:T(8,128)(2,1)} %bitcast.6), calls=%async_computation | async-start | bytes 1081344 | tf_op jit(solution)/shard_map/all_to_all | solution.py:419
  11.5 5.3 %collective-permute-start.9 = (bf16[64,640]{1,0:T(8,128)(2,1)S(1)}, bf16[64,640]{1,0:T(8,128)(2,1)S(1)}, u32[]{:S(2)}, u32[]{:S(2)}) collective-permute-start(bf16[64,640]{1,0:T(8,128)(2,1)S(1)} %pad_maximum_fusion.5), channel_id=1, source_target_pairs={{0,1},{1,0},{2,3},{3,2},{4,5},{5,4},{6,7},{7,6},{8,9},{9,8},{10,11... | collective-permute-start | bytes 245768 | tf_op jit(solution)/shard_map/ppermute | solution.py:467
  11.5 8.9 %copy-start.3 = (bf16[256,8192]{1,0:T(8,128)(2,1)S(1)}, bf16[256,8192]{1,0:T(8,128)(2,1)}, u32[]{:S(2)}) copy-start(bf16[256,8192]{1,0:T(8,128)(2,1)} %wo_hbm) | copy-start | bytes 12582916
  13.1 4.1 %collective-permute-start.4 = (bf16[128,1024]{1,0:T(8,128)(2,1)S(1)}, bf16[128,1024]{1,0:T(8,128)(2,1)S(1)}, u32[]{:S(2)}, u32[]{:S(2)}) collective-permute-start(bf16[128,1024]{1,0:T(8,128)(2,1)S(1)} %pad_maximum_fusion.1), channel_id=1, source_target_pairs={{0,1},{1,0},{2,3},{3,2},{4,5},{5,4},{6,7},{7,6},{8,9},{9,8},{10,11... | collective-permute-start | bytes 786440 | tf_op jit(solution)/shard_map/ppermute | solution.py:440
  13.7 3.7 %collective-permute-start.5 = (bf16[128,1024]{1,0:T(8,128)(2,1)S(1)}, bf16[128,1024]{1,0:T(8,128)(2,1)S(1)}, u32[]{:S(2)}, u32[]{:S(2)}) collective-permute-start(bf16[128,1024]{1,0:T(8,128)(2,1)S(1)} %pad_maximum_fusion.2), channel_id=1, source_target_pairs={{0,1},{1,0},{2,3},{3,2},{4,5},{5,4},{6,7},{7,6},{8,9},{9,8},{10,11... | collective-permute-start | bytes 786440 | tf_op jit(solution)/shard_map/ppermute | solution.py:440
  16.2 5.8 %collective-permute-start.3 = (bf16[1024,256]{1,0:T(8,128)(2,1)S(1)}, bf16[1024,256]{1,0:T(8,128)(2,1)S(1)}, u32[]{:S(2)}, u32[]{:S(2)}) collective-permute-start(bf16[1024,256]{1,0:T(8,128)(2,1)S(1)} %get-tuple-element.47), channel_id=1, source_target_pairs={{0,1},{1,0},{2,3},{3,2},{4,5},{5,4},{6,7},{7,6},{8,9},{9,8},{10,11... | collective-permute-start | bytes 1572872 | tf_op jit(solution)/shard_map/ppermute | solution.py:434
  16.7 5.7 %collective-permute-start.2 = (bf16[1024,256]{1,0:T(8,128)(2,1)S(1)}, bf16[1024,256]{1,0:T(8,128)(2,1)S(1)}, u32[]{:S(2)}, u32[]{:S(2)}) collective-permute-start(bf16[1024,256]{1,0:T(8,128)(2,1)S(1)} %get-tuple-element.48), channel_id=1, source_target_pairs={{0,1},{1,0},{2,3},{3,2},{4,5},{5,4},{6,7},{7,6},{8,9},{9,8},{10,11... | collective-permute-start | bytes 1572872 | tf_op jit(solution)/shard_map/ppermute | solution.py:434
  16.7 5.8 %collective-permute-start.1 = (bf16[1024,256]{1,0:T(8,128)(2,1)S(1)}, bf16[1024,256]{1,0:T(8,128)(2,1)S(1)}, u32[]{:S(2)}, u32[]{:S(2)}) collective-permute-start(bf16[1024,256]{1,0:T(8,128)(2,1)S(1)} %get-tuple-element.49), channel_id=1, source_target_pairs={{0,1},{1,0},{2,3},{3,2},{4,5},{5,4},{6,7},{7,6},{8,9},{9,8},{10,11... | collective-permute-start | bytes 1572872 | tf_op jit(solution)/shard_map/ppermute | solution.py:434
  17.2 5.8 %copy-start.9 = (bf16[128,1024]{1,0:T(8,128)(2,1)}, bf16[128,1024]{1,0:T(8,128)(2,1)S(1)}, u32[]{:S(2)}) copy-start(bf16[128,1024]{1,0:T(8,128)(2,1)S(1)} %collective-permute-done.4.rest_4_) | copy-start | bytes 786436
  17.2 2.9 %collective-permute-start.6 = (bf16[128,1024]{1,0:T(8,128)(2,1)S(1)}, bf16[128,1024]{1,0:T(8,128)(2,1)S(1)}, u32[]{:S(2)}, u32[]{:S(2)}) collective-permute-start(bf16[128,1024]{1,0:T(8,128)(2,1)S(1)} %pad_maximum_fusion.3), channel_id=1, source_target_pairs={{0,1},{1,0},{2,3},{3,2},{4,5},{5,4},{6,7},{7,6},{8,9},{9,8},{10,11... | collective-permute-start | bytes 786440 | tf_op jit(solution)/shard_map/ppermute | solution.py:440
  17.4 5.6 %copy-start.10 = (bf16[128,1024]{1,0:T(8,128)(2,1)}, bf16[128,1024]{1,0:T(8,128)(2,1)S(1)}, u32[]{:S(2)}) copy-start(bf16[128,1024]{1,0:T(8,128)(2,1)S(1)} %collective-permute-done.5.rest_5_) | copy-start | bytes 786436
  17.4 4.5 %collective-permute-start.7 = (bf16[128,1024]{1,0:T(8,128)(2,1)S(1)}, bf16[128,1024]{1,0:T(8,128)(2,1)S(1)}, u32[]{:S(2)}, u32[]{:S(2)}) collective-permute-start(bf16[128,1024]{1,0:T(8,128)(2,1)S(1)} %pad_maximum_fusion.4), channel_id=1, source_target_pairs={{0,1},{1,0},{2,3},{3,2},{4,5},{5,4},{6,7},{7,6},{8,9},{9,8},{10,11... | collective-permute-start | bytes 786440 | tf_op jit(solution)/shard_map/ppermute | solution.py:440
  20.1 2.9 %copy-start.11 = (bf16[128,1024]{1,0:T(8,128)(2,1)}, bf16[128,1024]{1,0:T(8,128)(2,1)S(1)}, u32[]{:S(2)}) copy-start(bf16[128,1024]{1,0:T(8,128)(2,1)S(1)} %collective-permute-done.6.rest_6_) | copy-start | bytes 786436
  20.1 3.2 %collective-permute-start = (bf16[1024,256]{1,0:T(8,128)(2,1)}, bf16[1024,256]{1,0:T(8,128)(2,1)}, u32[]{:S(2)}, u32[]{:S(2)}) collective-permute-start(bf16[1024,256]{1,0:T(8,128)(2,1)} %get-tuple-element.50), channel_id=1, source_target_pairs={{0,1},{1,0},{2,3},{3,2},{4,5},{5,4},{6,7},{7,6},{8,9},{9,8},{10,11... | collective-permute-start | bytes 1572872 | tf_op jit(solution)/shard_map/ppermute | solution.py:434
  21.9 1.2 %copy-start.12 = (bf16[128,1024]{1,0:T(8,128)(2,1)}, bf16[128,1024]{1,0:T(8,128)(2,1)S(1)}, u32[]{:S(2)}) copy-start(bf16[128,1024]{1,0:T(8,128)(2,1)S(1)} %collective-permute-done.7.rest_7_) | copy-start | bytes 786436
  21.9 9.1 %collective-permute-start.13 = (bf16[256,1024]{1,0:T(8,128)(2,1)}, bf16[256,1024]{1,0:T(8,128)(2,1)S(1)}, u32[]{:S(2)}, u32[]{:S(2)}) collective-permute-start(bf16[256,1024]{1,0:T(8,128)(2,1)} %get-tuple-element.43), channel_id=1, source_target_pairs={{0,1},{1,0},{2,3},{3,2},{4,5},{5,4},{6,7},{7,6},{8,9},{9,8},{10,11... | collective-permute-start | bytes 1572872 | tf_op jit(solution)/shard_map/ppermute | solution.py:454
  22.0 2.7 %copy-start.4 = (bf16[1024,256]{1,0:T(8,128)(2,1)}, bf16[1024,256]{1,0:T(8,128)(2,1)S(1)}, u32[]{:S(2)}) copy-start(bf16[1024,256]{1,0:T(8,128)(2,1)S(1)} %collective-permute-done.3.rest_3_) | copy-start | bytes 1572868
  22.0 8.9 %collective-permute-start.12 = (bf16[256,1024]{1,0:T(8,128)(2,1)}, bf16[256,1024]{1,0:T(8,128)(2,1)S(1)}, u32[]{:S(2)}, u32[]{:S(2)}) collective-permute-start(bf16[256,1024]{1,0:T(8,128)(2,1)} %get-tuple-element.44), channel_id=1, source_target_pairs={{0,1},{1,0},{2,3},{3,2},{4,5},{5,4},{6,7},{7,6},{8,9},{9,8},{10,11... | collective-permute-start | bytes 1572872 | tf_op jit(solution)/shard_map/ppermute | solution.py:454
  22.4 2.3 %copy-start.5 = (bf16[1024,256]{1,0:T(8,128)(2,1)}, bf16[1024,256]{1,0:T(8,128)(2,1)S(1)}, u32[]{:S(2)}) copy-start(bf16[1024,256]{1,0:T(8,128)(2,1)S(1)} %collective-permute-done.2.rest_2_) | copy-start | bytes 1572868
  22.4 8.6 %collective-permute-start.11 = (bf16[256,1024]{1,0:T(8,128)(2,1)}, bf16[256,1024]{1,0:T(8,128)(2,1)}, u32[]{:S(2)}, u32[]{:S(2)}) collective-permute-start(bf16[256,1024]{1,0:T(8,128)(2,1)} %get-tuple-element.45), channel_id=1, source_target_pairs={{0,1},{1,0},{2,3},{3,2},{4,5},{5,4},{6,7},{7,6},{8,9},{9,8},{10,11... | collective-permute-start | bytes 1572872 | tf_op jit(solution)/shard_map/ppermute | solution.py:454
  22.5 2.2 %copy-start.6 = (bf16[1024,256]{1,0:T(8,128)(2,1)}, bf16[1024,256]{1,0:T(8,128)(2,1)S(1)}, u32[]{:S(2)}) copy-start(bf16[1024,256]{1,0:T(8,128)(2,1)S(1)} %collective-permute-done.1.rest_1_) | copy-start | bytes 1572868
  22.5 8.5 %collective-permute-start.10 = (bf16[256,1024]{1,0:T(8,128)(2,1)}, bf16[256,1024]{1,0:T(8,128)(2,1)}, u32[]{:S(2)}, u32[]{:S(2)}) collective-permute-start(bf16[256,1024]{1,0:T(8,128)(2,1)} %get-tuple-element.46), channel_id=1, source_target_pairs={{0,1},{1,0},{2,3},{3,2},{4,5},{5,4},{6,7},{7,6},{8,9},{9,8},{10,11... | collective-permute-start | bytes 1572872 | tf_op jit(solution)/shard_map/ppermute | solution.py:454
  24.7 4.5 %copy-start.13 = (bf16[1,64,256]{2,1,0:T(8,128)(2,1)S(1)}, bf16[1,64,256]{2,1,0:T(8,128)(2,1)}, u32[]{:S(2)}) copy-start(bf16[1,64,256]{2,1,0:T(8,128)(2,1)} %param.28) | copy-start | bytes 98308
  29.1 1.9 %collective-permute-start.8 = (f32[16,1024]{1,0:T(8,128)S(1)}, f32[16,1024]{1,0:T(8,128)S(1)}, u32[]{:S(2)}, u32[]{:S(2)}) collective-permute-start(f32[16,1024]{1,0:T(8,128)S(1)} %get-tuple-element.29), channel_id=1, source_target_pairs={{0,1},{1,0},{2,3},{3,2},{4,5},{5,4},{6,7},{7,6},{8,9},{9,8},{10,11... | collective-permute-start | bytes 196616 | tf_op jit(solution)/shard_map/ppermute | solution.py:508
  29.2 6.2 %copy-start = (bf16[1,256,64]{1,2,0:T(8,128)(2,1)S(1)}, bf16[1,256,64]{1,2,0:T(8,128)(2,1)}, u32[]{:S(2)}) copy-start(bf16[1,256,64]{1,2,0:T(8,128)(2,1)} %param.30) | copy-start | bytes 98308
  31.0 0.8 %copy-start.7 = (bf16[256,1024]{1,0:T(8,128)(2,1)}, bf16[256,1024]{1,0:T(8,128)(2,1)S(1)}, u32[]{:S(2)}) copy-start(bf16[256,1024]{1,0:T(8,128)(2,1)S(1)} %collective-permute-done.13.rest_3_) | copy-start | bytes 1572868
  31.0 1.0 %copy-start.8 = (bf16[256,1024]{1,0:T(8,128)(2,1)}, bf16[256,1024]{1,0:T(8,128)(2,1)S(1)}, u32[]{:S(2)}) copy-start(bf16[256,1024]{1,0:T(8,128)(2,1)S(1)} %collective-permute-done.12.rest_2_) | copy-start | bytes 1572868
  32.0 18.5 %copy-start.1 = (s32[16,1]{0,1:T(1,128)S(1)}, s32[16,1]{0,1:T(1,128)}, u32[]{:S(2)}) copy-start(s32[16,1]{0,1:T(1,128)} %param.24) | copy-start | bytes 196
  32.0 18.5 %copy-start.2 = (s32[8]{0:T(128)S(1)}, s32[8]{0:T(128)}, u32[]{:S(2)}) copy-start(s32[8]{0:T(128)} %param.25) | copy-start | bytes 100
  34.0 1.4 %collective-permute-start.14 = (bf16[16,512]{1,0:T(8,128)(2,1)S(1)}, bf16[16,512]{1,0:T(8,128)(2,1)S(1)}, u32[]{:S(2)}, u32[]{:S(2)}) collective-permute-start(bf16[16,512]{1,0:T(8,128)(2,1)S(1)} %get-tuple-element.39.mine_ref), channel_id=1, source_target_pairs={{0,1},{1,0},{2,3},{3,2},{4,5},{5,4},{6,7},{7,6},{8,9},{9,8},{10,11... | collective-permute-start | bytes 49160 | tf_op jit(solution)/shard_map/ppermute | solution.py:528

commit v3 on v1

v3 whole, which is shorter than its diff:
```python
import functools
import math

import jax
import jax.numpy as jnp
from jax import lax
from jax.experimental import pallas as pl
from jax.experimental.pallas import tpu as pltpu
from jax.sharding import PartitionSpec as P

HEAD_SIZE = 128
LANES = 128
EPSILON = 1e-05
THETA = 500000.0
BF16 = jnp.bfloat16
F32 = jnp.float32
SWAP = [(0, 1), (1, 0)]
GROUP = 16
MIB = 1024 * 1024


def nn(a, b):
    return lax.dot_general(a, b, (((1,), (0,)), ((), ())), preferred_element_type=F32)


def nt(a, b):
    return lax.dot_general(a, b, (((1,), (1,)), ((), ())), preferred_element_type=F32)


def iota(shape, dim):
    return lax.broadcasted_iota(jnp.int32, shape, dim)


def ones_where(condition):
    return jnp.where(condition, 1.0, 0.0).astype(BF16)


def owner_and_standing(named, table):
    requests, adapters = named.shape[1], table.shape[1]
    table_column = jnp.sum(
        jnp.where(iota((adapters, adapters), 0) == iota((adapters, adapters), 1), table, 0),
        axis=1,
        keepdims=True,
    )
    owner = jnp.sum(
        jnp.where(iota((adapters, requests), 0) == named, table_column, 0), axis=0, keepdims=True
    )
    square = (requests, requests)
    owner_column = jnp.sum(
        jnp.where(iota(square, 0) == iota(square, 1), owner, 0), axis=1, keepdims=True
    )
    earlier = (owner_column == owner) & (iota(square, 0) < iota(square, 1))
    standing = jnp.sum(jnp.where(earlier, 1, 0), axis=0, keepdims=True)
    return owner, standing


def copy_all(pairs, sems):
    copies = [pltpu.make_async_copy(a, b, sems.at[i]) for i, (a, b) in enumerate(pairs)]
    for copy in copies:
        copy.start()
    return copies


def pack_kernel(capacity, x_hbm, gain_hbm, k_hbm, v_hbm, named_hbm, table_hbm, length_hbm, up_hbm, kv_up_hbm, out_down_hbm, *rest):
    up_ref, kv_up_ref, out_down_ref = rest[-4:-1]
    rest = rest[:-4] + rest[-1:]
    small_ref, x_ref, gain_ref, k_ref, v_ref, named_ref, table_ref, length_ref, flat_ref, spread_ref, sems = rest[-11:]
    blocks = rest[:-11]
    count = len(blocks)
    owners = 2 * count
    named_copy, table_copy, length_copy, x_copy, gain_copy, k_copy, v_copy, *up_copies = copy_all(
        [
            (named_hbm, named_ref),
            (table_hbm, table_ref),
            (length_hbm, length_ref),
            (x_hbm, x_ref),
            (gain_hbm, gain_ref),
            (k_hbm, k_ref),
            (v_hbm, v_ref),
            (up_hbm, up_ref),
            (kv_up_hbm, kv_up_ref),
            (out_down_hbm, out_down_ref),
        ],
        sems,
    )
    requests, width = x_ref.shape
    positions = k_ref.shape[0] // requests
    per_block = blocks[0].shape[0]
    rows = per_block * count
    first = lax.axis_index("adapter") + lax.axis_index("tensor") * count
    named_copy.wait()
    table_copy.wait()
    length_copy.wait()
    owner, standing = owner_and_standing(named_ref[...], table_ref[...])
    ahead = owner - first
    ahead = jnp.where(ahead < -owners, ahead + 2 * owners, jnp.where(ahead < 0, ahead + owners, ahead))
    row = jnp.where(ahead < count, ahead * per_block + 2 * standing, -2)
    order = iota((rows, requests), 0)
    put_x = ones_where(order == row)
    put_kv = ones_where(order == row + 1)
    put = jnp.concatenate([put_x, put_kv], axis=1)

    x_copy.wait()
    gain_copy.wait()
    floats = x_ref[...].astype(F32)
    scale = lax.rsqrt(jnp.mean(floats * floats, axis=1, keepdims=True) + EPSILON)
    flat_ref[0:requests, :] = (floats * scale * gain_ref[...]).astype(BF16)
    for n, (source, copy) in enumerate(((k_ref, k_copy), (v_ref, v_copy))):
        copy.wait()
        spread_ref[...] = source[...].astype(F32)
        for p in range(positions):
            to = slice((n * positions + p) * LANES, (n * positions + p + 1) * LANES)
            flat_ref[requests : 2 * requests, to] = spread_ref[
                pl.ds(p, requests, stride=positions), :
            ].astype(BF16)
    step = 512
    for c in range(0, width, step):
        placed = nn(put, flat_ref[:, c : c + step]).astype(BF16)
        for j, block in enumerate(blocks):
            block[:, c : c + step] = placed[j * per_block : (j + 1) * per_block]
    square = (requests, requests)
    length_column = jnp.sum(
        jnp.where(iota(square, 0) == iota(square, 1), length_ref[...], 0), axis=1, keepdims=True
    )
    lengths = jnp.broadcast_to(length_column.astype(F32), (requests, LANES)).astype(BF16)
    placed = nn(put_x, lengths).astype(BF16)
    for j, block in enumerate(blocks):
        block[:, width:] = placed[j * per_block : (j + 1) * per_block]
    for copy in up_copies:
        copy.wait()
    small_ref[...] = jnp.concatenate(
        [up_ref[...], kv_up_ref[0], kv_up_ref[1], out_down_ref[...]], axis=1
    )


def stacked(blocks, columns):
    return jnp.concatenate([block[:, columns] for block in blocks], axis=0)


def stage_kernel(wq_hbm, wk_hbm, wv_hbm, down_hbm, wq_ref, kv_ref, down_ref, sems):
    width = wq_hbm.shape[0]
    hcols = wk_hbm.shape[0]
    ranks = down_hbm.shape[0]
    pieces = 4
    pairs = [(wk_hbm, kv_ref.at[0:hcols, :]), (wv_hbm, kv_ref.at[hcols:, :])]
    for n in range(pieces):
        rows = pl.ds(n * (width // pieces), width // pieces)
        pairs.append((wq_hbm.at[rows, :], wq_ref.at[rows, :]))
    for n in range(2):
        rows = pl.ds(n * (ranks // 2), ranks // 2)
        pairs.append((down_hbm.at[rows, :], down_ref.at[rows, :]))
    for copy in copy_all(pairs, sems):
        copy.wait()


def project_kernel(count, *refs):
    blocks = refs[: 2 * count]
    wq_ref, kv_ref, down_ref, mine_ref, theirs_ref, sums_ref = refs[2 * count :]
    width = wq_ref.shape[0]
    half = down_ref.shape[1]
    slots = mine_ref.shape[0]
    rows = sums_ref.shape[1]
    x_all = stacked(blocks, slice(0, width))
    halves = [x_all[:, :half], x_all[:, half:]]
    x_half = jnp.where(lax.axis_index("tensor") == 0, halves[0], halves[1])
    ranks = nt(x_half, down_ref[...])
    spare = jnp.zeros((rows, -ranks.shape[1] % LANES), F32)
    sums = [nn(x_all, wq_ref[...]), nt(x_all, kv_ref[...]), jnp.concatenate([ranks, spare], axis=1)]
    tile = 0
    for part in sums:
        for c in range(0, part.shape[1], LANES):
            sums_ref[tile] = part[:, c : c + LANES]
            columns = slice(tile * LANES, (tile + 1) * LANES)
            mine_ref[:, columns] = sums_ref[tile, pl.ds(0, slots, stride=2), :]
            theirs_ref[:, columns] = sums_ref[tile, pl.ds(rows // 2, slots, stride=2), :]
            tile += 1


def unpack_kernel(count, *refs):
    blocks = refs[:count]
    k_ref, v_ref, length_ref, cosine_ref, sine_ref = refs[count:]
    slots = length_ref.shape[0]
    per_block = blocks[0].shape[0]
    positions = k_ref.shape[0] // slots
    width = 2 * positions * LANES
    together = GROUP // (per_block // 2)
    pick = iota((GROUP, 2 * GROUP), 1) - 2 * iota((GROUP, 2 * GROUP), 0)
    pick_x, pick_kv = ones_where(pick == 0), ones_where(pick == 1)
    step = 512
    for g in range(slots // GROUP):
        members = blocks[g * together : (g + 1) * together]
        for c in range(0, width, step):
            picked = nn(pick_kv, stacked(members, slice(c, c + step))).astype(BF16)
            for j in range(step // LANES):
                p = c // LANES + j
                target, p = (k_ref, p) if p < positions else (v_ref, p - positions)
                first = (g * positions + p) * GROUP
                target[first : first + GROUP, :] = picked[:, j * LANES : (j + 1) * LANES]
        length_ref[g * GROUP : (g + 1) * GROUP, :] = nn(
            pick_x, stacked(members, slice(width, width + LANES))
        )
    halfway = HEAD_SIZE // 2
    lane = iota((slots, LANES), 1)
    exponent = (lane % halfway).astype(F32) * (-math.log(THETA) / halfway)
    angle = length_ref[...] * jnp.exp(exponent)
    cosine_ref[...] = jnp.cos(angle)
    sine = jnp.sin(angle)
    sine_ref[...] = jnp.where(lane < halfway, -sine, sine)


def attend_kernel(mine_ref, theirs_ref, small_ref, small_other_ref, k_ref, v_ref, length_ref, cosine_ref, sine_ref, out_ref):
    core = lax.axis_index("tensor")
    slots = mine_ref.shape[0]
    rank = small_ref.shape[0]
    kvcols = LANES
    qcols = out_ref.shape[1] // 2
    heads = 2 * qcols // HEAD_SIZE
    halfway = HEAD_SIZE // 2
    both = qcols + kvcols
    mine = mine_ref[...]
    theirs = theirs_ref[...]
    ranks = (mine + theirs)[:, both : both + 3 * rank].astype(BF16)
    ranks = [ranks[:, n * rank : (n + 1) * rank] for n in range(3)]

    def added(projected, up_ref):
        change = jnp.concatenate(
            [
                nn(ranks[0], up_ref[:, :qcols]),
                nn(ranks[1], up_ref[:, qcols : qcols + halfway]),
                nn(ranks[2], up_ref[:, qcols + halfway : both]),
            ],
            axis=1,
        )
        return projected[:, :both] + change.astype(BF16).astype(F32)

    mine = added(mine, small_ref)
    theirs = added(theirs, small_other_ref)
    combined = jnp.concatenate([mine[:, :qcols], theirs[:, :qcols]], axis=1)
    cosine, sine = cosine_ref[...], sine_ref[...]

    def rotate(part):
        return part * cosine + pltpu.roll(part, halfway, 1) * sine

    queries = [
        rotate(combined[:, h * HEAD_SIZE : (h + 1) * HEAD_SIZE]).astype(BF16) for h in range(heads)
    ]
    kv_mine = mine[:, qcols:]
    kv_theirs = theirs[:, qcols:]
    leading = jnp.where(core == 0, kv_mine, kv_theirs)
    trailing = jnp.where(core == 0, kv_theirs, kv_mine)
    first = iota((slots, LANES), 1) < halfway
    own_keys = rotate(jnp.where(first, leading, pltpu.roll(trailing, halfway, 1))).astype(BF16)
    own_values = jnp.where(first, pltpu.roll(leading, halfway, 1), trailing).astype(BF16)

    cached = k_ref.shape[0] * GROUP // slots
    rows = heads * GROUP
    shrink = math.sqrt(HEAD_SIZE)
    column = iota((rows, cached), 1)
    same = column % GROUP == iota((rows, cached), 0) % GROUP
    position = column // GROUP
    own = iota((rows, GROUP), 1) == iota((rows, GROUP), 0) % GROUP
    for g in range(slots // GROUP):
        members = slice(g * GROUP, (g + 1) * GROUP)
        held = slice(g * cached, (g + 1) * cached)
        query = jnp.concatenate([part[members] for part in queries], axis=0)
        length = jnp.concatenate([length_ref[members, 0:1]] * heads, axis=0).astype(jnp.int32)
        scores = jnp.where(
            same & (position < length), nt(query, k_ref[held, :]) / shrink, -jnp.inf
        )
        own_scores = jnp.where(own, nt(query, own_keys[members]) / shrink, -jnp.inf)
        highest = jnp.maximum(
            jnp.max(scores, axis=1, keepdims=True), jnp.max(own_scores, axis=1, keepdims=True)
        )
        raised = jnp.exp(scores - highest)
        own_raised = jnp.exp(own_scores - highest)
        total = jnp.sum(raised, axis=1, keepdims=True) + jnp.sum(own_raised, axis=1, keepdims=True)
        weights = (raised / total).astype(BF16)
        own_weights = (own_raised / total).astype(BF16)
        attended = (nn(weights, v_ref[held, :]) + nn(own_weights, own_values[members])).astype(BF16)
        for h in range(heads):
            out_ref[members, h * HEAD_SIZE : (h + 1) * HEAD_SIZE] = attended[
                h * GROUP : (h + 1) * GROUP
            ]


def output_kernel(capacity, owners, mine_ref, theirs_ref, wo_ref, wo_other_ref, small_ref, small_other_ref, up_ref, out_ref):
    core = lax.axis_index("tensor")
    slots, cols = mine_ref.shape
    hcols = cols // 2
    half = out_ref.shape[1]
    rows = owners * capacity
    theirs = theirs_ref[...]
    rows_in = jnp.concatenate(
        [mine_ref[...], jnp.concatenate([theirs[:, hcols:], theirs[:, :hcols]], axis=1)], axis=0
    )
    count = owners // 2
    per_owner = slots // count
    out_row = iota((rows, 2 * slots), 0)
    ahead = lax.axis_index("adapter") - core * count - out_row // capacity
    ahead = jnp.where(ahead < -owners, ahead + 2 * owners, jnp.where(ahead < 0, ahead + owners, ahead))
    source = jnp.where(ahead < count, ahead * per_owner, slots + (ahead - count) * per_owner)
    source = source + out_row % capacity
    arrange = ones_where(iota((rows, 2 * slots), 1) == source)
    attended = nn(arrange, rows_in).astype(BF16)
    left, right = attended[:, :hcols], attended[:, hcols:]
    down = slice(small_ref.shape[1] - hcols, small_ref.shape[1])
    ranks = (nt(left, small_ref[:, down]) + nt(right, small_other_ref[:, down])).astype(BF16)
    step = 512
    for c in range(0, half, step):
        delta = nn(ranks, up_ref[:, c : c + step]).astype(BF16).astype(F32)
        columns = pl.ds(pl.multiple_of(core * half + c, step), step)
        terms = nn(left, wo_ref[:, columns]) + nn(right, wo_other_ref[:, columns])
        out_ref[:, c : c + step] = (terms + delta).astype(BF16)


def pick_kernel(capacity, back_ref, named_ref, table_ref, out_ref):
    rows, half = back_ref.shape
    requests = out_ref.shape[0]
    owner, standing = owner_and_standing(named_ref[...], table_ref[...])
    place = ones_where(iota((rows, requests), 0) == owner * capacity + standing)
    step = 512
    for c in range(0, half, step):
        out_ref[:, c : c + step] = lax.dot_general(
            place,
            back_ref[:, c : c + step],
            (((0,), (0,)), ((), ())),
            preferred_element_type=F32,
        ).astype(BF16)


OUTSIDE = pl.BlockSpec(memory_space=pltpu.HBM)
INSIDE = pl.BlockSpec(memory_space=pltpu.VMEM)


def call(kernel, outs, scratch=(), vmem=8, outside=(), out_spec=INSIDE, moved=0):
    many = isinstance(outs, (list, tuple))
    return lambda *args: pl.pallas_call(
        kernel,
        out_shape=outs,
        in_specs=[OUTSIDE if i in outside else INSIDE for i in range(len(args))],
        out_specs=[out_spec] * len(outs) if many else out_spec,
        scratch_shapes=list(scratch),
        compiler_params=pltpu.CompilerParams(vmem_limit_bytes=vmem * MIB),
        cost_estimate=pl.CostEstimate(flops=0, bytes_accessed=moved, transcendentals=0),
    )(
        *[
            pltpu.with_memory_space_constraint(arg, pltpu.HBM) if i in outside else arg
            for i, arg in enumerate(args)
        ]
    )


def body(
    layer_input,
    input_norm_gain,
    query_projection,
    key_projection,
    value_projection,
    output_projection,
    cached_key_rows,
    cached_value_rows,
    request_adapter,
    adapter_row_table,
    cached_length,
    projection_adapter_down,
    query_adapter_up,
    key_value_adapter_up,
    output_adapter_down,
    output_adapter_up,
):
    shape = jax.ShapeDtypeStruct
    requests, width = layer_input.shape
    owners = lax.axis_size("adapter")
    adapters = adapter_row_table.shape[0]
    positions = cached_key_rows.shape[1]
    half = width // 2
    capacity = max(2, 2 * ((requests + adapters - 1) // adapters))
    count = owners // 2
    kept = (capacity + 3) // 4 * 4
    slots = count * kept
    block = shape((2 * kept, width + LANES), BF16)
    named = request_adapter.reshape(1, requests)
    table = adapter_row_table.reshape(1, adapters)

    rank, qcols = query_adapter_up.shape[1:]
    hcols = key_value_adapter_up.shape[3]
    hrows = output_projection.shape[0]
    *packed, small = call(
        functools.partial(pack_kernel, capacity),
        [block] * count + [shape((rank, qcols + 2 * hcols + hrows), BF16)],
        [
            pltpu.VMEM((requests, width), BF16),
            pltpu.VMEM((1, width), F32),
            pltpu.VMEM((positions * requests, LANES), BF16),
            pltpu.VMEM((positions * requests, LANES), BF16),
            pltpu.VMEM((1, requests), jnp.int32),
            pltpu.VMEM((1, adapters), jnp.int32),
            pltpu.VMEM((1, requests), jnp.int32),
            pltpu.VMEM((2 * requests, width), BF16),
            pltpu.VMEM((positions * requests, LANES), F32),
            pltpu.VMEM((rank, qcols), BF16),
            pltpu.VMEM((2, rank, hcols), BF16),
            pltpu.VMEM((rank, hrows), BF16),
            pltpu.SemaphoreType.DMA((10,)),
        ],
        outside=range(10),
    )(
        layer_input,
        input_norm_gain.reshape(1, width),
        cached_key_rows.reshape(requests * positions, HEAD_SIZE),
        cached_value_rows.reshape(requests * positions, HEAD_SIZE),
        named,
        table,
        cached_length.reshape(1, requests),
        query_adapter_up[0],
        key_value_adapter_up[0],
        output_adapter_down[0].T,
    )
    down = projection_adapter_down[0].T
    wk, wv = key_projection.T, value_projection.T
    kvcols = 2 * wk.shape[0]
    *packed, query_projection, wk, wv, down, output_projection, output_adapter_up = (
        lax.optimization_barrier(
            (*packed, query_projection, wk, wv, down, output_projection, output_adapter_up)
        )
    )
    weights = call(
        stage_kernel,
        [
            shape(query_projection.shape, BF16),
            shape((kvcols, width), BF16),
            shape(down.shape, BF16),
        ],
        [pltpu.SemaphoreType.DMA((8,))],
        outside=range(4),
        moved=2 * (query_projection.size + kvcols * width + down.size),
    )(query_projection, wk, wv, down)

    def onward(n):
        return [
            (a * 2 + t, (a + t * count + n) % owners * 2 + t) for a in range(owners) for t in range(2)
        ]

    arrived = [
        lax.ppermute(one, ("adapter", "tensor"), onward(n)) for n, one in enumerate(packed)
    ]
    arrived[0], *weights = lax.optimization_barrier((arrived[0], *weights))
    passed = [lax.ppermute(one, "tensor", SWAP) for one in arrived]
    wo_other = lax.ppermute(output_projection, "tensor", SWAP)
    small_other = lax.ppermute(small, "tensor", SWAP)
    pcols = qcols + kvcols + (down.shape[0] + LANES - 1) // LANES * LANES
    mine, theirs = call(
        functools.partial(project_kernel, count),
        [shape((slots, pcols), F32), shape((slots, pcols), F32)],
        [pltpu.VMEM((pcols // LANES, 4 * slots, LANES), F32)],
        vmem=24,
    )(*arrived, *passed, *weights)
    theirs = lax.ppermute(theirs, "tensor", SWAP)
    keys, values, lengths, cosine, sine = call(
        functools.partial(unpack_kernel, count),
        [shape((slots * positions, HEAD_SIZE), BF16)] * 2 + [shape((slots, LANES), F32)] * 3,
    )(*arrived)
    attended = call(attend_kernel, shape((slots, 2 * qcols), BF16), vmem=16)(
        mine, theirs, small, small_other, keys, values, lengths, cosine, sine
    )
    attended_other = lax.ppermute(attended, "tensor", SWAP)
    finished = call(
        functools.partial(output_kernel, capacity, owners),
        shape((owners * capacity, half), BF16),
        vmem=16,
    )(
        attended,
        attended_other,
        output_projection,
        wo_other,
        small,
        small_other,
        output_adapter_up[0],
    )
    back = lax.all_to_all(
        finished.reshape(owners, capacity, half), "adapter", split_axis=0, concat_axis=0, tiled=True
    ).reshape(owners * capacity, half)
    return call(functools.partial(pick_kernel, capacity), shape((requests, half), BF16))(
        back, named, table
    )


def solution(mesh):
    placed = (
        P(("groups", "adapter"), None),
        P(),
        P(None, "tensor"),
        P(None, "tensor"),
        P(None, "tensor"),
        P("tensor", None),
        P(("groups", "adapter"), None, None),
        P(("groups", "adapter"), None, None),
        P(("groups", "adapter"), None),
        P(),
        P(("groups", "adapter")),
        P("adapter", "tensor", None),
        P("adapter", None, "tensor"),
        P("adapter", None, None, "tensor"),
        P("adapter", "tensor", None),
        P("adapter", None, "tensor"),
    )
    return jax.shard_map(
        body,
        mesh=mesh,
        in_specs=placed,
        out_specs=P(("groups", "adapter"), "tensor"),
        check_vma=False,
    )
```

time: 59 us -> 44.9 us (0.76)
  waiting for transfers between devices: 15 us -> 4.9 us
  local copies, waits for them, and re-layouts: 8.85 us -> 0.2 us
  blocking collectives: 12.7 us -> 16.6 us
  starting transfers between devices: 8.76 us -> 12.4 us
  other arithmetic: 2.86 us -> 0 us
    all_to_all x1 -> x0, waiting for transfers between devices: 13 us -> none  [body(): lax.all_to_all(packed.reshape(owners, 2 * capacity, half + LANES), 'adapt...]
    ppermute x3 -> x9, starting transfers between devices: 0.7 us -> 11.4 us  [the longest x4 7.36 us: body(): lax.ppermute(one, ('adapter', 'tensor'), onward(n))]
    all_to_all x1 -> x0, starting transfers between devices: 7.25 us -> none  [body(): lax.all_to_all(packed.reshape(owners, 2 * capacity, half + LANES), 'adapt...]
    dynamic_slice x2 -> x0, local copies, waits for them, and re-layouts: 4.71 us -> none  [the longest x1 3.24 us: body(): lax.dynamic_slice(query_projection, (other, 0), (half, qcols))]
    all_to_all x1, blocking collectives: 12.7 us -> 16.6 us  [body(): lax.all_to_all(finished.reshape(owners, capacity, half), 'adapter', split...]
    unnamed x34 -> x8, local copies, waits for them, and re-layouts: 3.66 us -> 0.02 us
    ppermute x3 -> x9, waiting for transfers between devices: 0.01 us -> 3.07 us  [the longest x4 2.24 us: body(): lax.ppermute(one, ('adapter', 'tensor'), onward(n))]
    concatenate x4 -> x0, other arithmetic: 2.86 us -> none  [the longest x2 2.75 us: body(): kv = jnp.concatenate([key_projection.T, value_projection.T], axis=0)]
  transfers between devices with their start and end apart: 7 -> 12, of which waited for: 3 -> 4; matrix products, arithmetic and copies ran while one was open for 8% -> 0% of each run, Pallas kernels for 11% -> 15%
where the time goes in v3:
time: 44.9 us; the launch traced here: 44.7 us
  blocking collectives  16.6 us (37%)
  starting transfers between devices  12.4 us (28%)
  Pallas kernels  10.5 us (23%)
  waiting for transfers between devices  4.9 us (11%)
    all_to_all x1, blocking collectives, body(): lax.all_to_all(finished.reshape(owners, capacity, half), 'adapter', split...  16.6 us
    pallas_call x7, Pallas kernels, call(): pl.pallas_call(kernel, out_shape=outs, in_specs=[OUTSIDE if i in outside...  10.5 us
    ppermute x4, starting transfers between devices, body(): lax.ppermute(one, ('adapter', 'tensor'), onward(n))  7.36 us
    ppermute x4, starting transfers between devices, body(): passed = [lax.ppermute(one, 'tensor', SWAP) for one in arrived]  3.54 us
    ppermute x4, waiting for transfers between devices, body(): lax.ppermute(one, ('adapter', 'tensor'), onward(n))  2.24 us
    ppermute x1, waiting for transfers between devices, body(): attended_other = lax.ppermute(attended, 'tensor', SWAP)  1.02 us
  transfers between devices with their start and end apart: 12, of which 4 were waited for; matrix products, arithmetic and copies ran while one was open for 0% of the time, Pallas kernels for 15%

profile of v3, /device:TPU:0, one launch (start us, length us, event | category | flops | bytes accessed | tf_op | source)
XLA Modules:
  0.0 44.7 jit_solution(16746052514762342055)
XLA Ops:
  0.0 1.9 %shard_map.154 = (bf16[8,8320]{1,0:T(8,128)(2,1)S(1)}, bf16[8,8320]{1,0:T(8,128)(2,1)S(1)}, bf16[8,8320]{1,0:T(8,128)(2,1)S(1)}, bf16[8,8320]{1,0:T(8,128)(2,1)S(1)}, bf16[64,640]{1,0:T(8,128)(2,1)S(1)}) custom-call(bf16[16,8192]{1,0:T(8,128)(2,1)} %x_hbm.1, f32[1,8192]{1,0:T(1,128)} %bitcast.27, bf16[512,128]{1,0:T(8,128)(2,1)} %bitcast.25, ...), custom_call_target="tpu_custom_call" | custom-call | tf_op jit(solution)/shard_map/pallas_call | solution.py:337
  1.9 0.5 %collective-permute-start.11 = (bf16[256,8192]{1,0:T(8,128)(2,1)}, bf16[256,8192]{1,0:T(8,128)(2,1)S(1)}, u32[]{:S(2)}, u32[]{:S(2)}) collective-permute-start(bf16[256,8192]{1,0:T(8,128)(2,1)} %wo_ref), channel_id=1, source_target_pairs={{0,1},{1,0},{2,3},{3,2},{4,5},{5,4},{6,7},{7,6},{8,9},{9,8},{10,11... | collective-permute-start | bytes 12582920 | tf_op jit(solution)/shard_map/ppermute | solution.py:449
  2.5 0.7 %collective-permute-start = (bf16[8,8320]{1,0:T(8,128)(2,1)S(1)}, bf16[8,8320]{1,0:T(8,128)(2,1)S(1)}, u32[]{:S(2)}, u32[]{:S(2)}) collective-permute-start(bf16[8,8320]{1,0:T(8,128)(2,1)S(1)} %get-tuple-element.38), channel_id=1, source_target_pairs={{0,0},{1,9},{2,2},{3,11},{4,4},{5,13},{6,6},{7,15},{8,8},{9,1},{10... | collective-permute-start | bytes 399368 | tf_op jit(solution)/shard_map/ppermute | solution.py:445
  3.1 2.6 %collective-permute-start.1 = (bf16[8,8320]{1,0:T(8,128)(2,1)S(1)}, bf16[8,8320]{1,0:T(8,128)(2,1)S(1)}, u32[]{:S(2)}, u32[]{:S(2)}) collective-permute-start(bf16[8,8320]{1,0:T(8,128)(2,1)S(1)} %get-tuple-element.47), channel_id=1, source_target_pairs={{0,2},{1,11},{2,4},{3,13},{4,6},{5,15},{6,8},{7,1},{8,10},{9,3},{1... | collective-permute-start | bytes 399368 | tf_op jit(solution)/shard_map/ppermute | solution.py:445
  5.7 1.6 %collective-permute-start.2 = (bf16[8,8320]{1,0:T(8,128)(2,1)S(1)}, bf16[8,8320]{1,0:T(8,128)(2,1)S(1)}, u32[]{:S(2)}, u32[]{:S(2)}) collective-permute-start(bf16[8,8320]{1,0:T(8,128)(2,1)S(1)} %get-tuple-element.48), channel_id=1, source_target_pairs={{0,4},{1,13},{2,6},{3,15},{4,8},{5,1},{6,10},{7,3},{8,12},{9,5},{1... | collective-permute-start | bytes 399368 | tf_op jit(solution)/shard_map/ppermute | solution.py:445
  7.3 2.6 %collective-permute-start.3 = (bf16[8,8320]{1,0:T(8,128)(2,1)S(1)}, bf16[8,8320]{1,0:T(8,128)(2,1)S(1)}, u32[]{:S(2)}, u32[]{:S(2)}) collective-permute-start(bf16[8,8320]{1,0:T(8,128)(2,1)S(1)} %get-tuple-element.49), channel_id=1, source_target_pairs={{0,6},{1,15},{2,8},{3,1},{4,10},{5,3},{6,12},{7,5},{8,14},{9,7},{1... | collective-permute-start | bytes 399368 | tf_op jit(solution)/shard_map/ppermute | solution.py:445
  9.8 3.3 %shard_map.155 = (bf16[8192,256]{1,0:T(8,128)(2,1)S(1)}, bf16[128,8192]{1,0:T(8,128)(2,1)S(1)}, bf16[192,4096]{1,0:T(8,128)(2,1)S(1)}) custom-call(bf16[8192,256]{1,0:T(8,128)(2,1)} %wq_hbm, bf16[64,8192]{1,0:T(8,128)(2,1)} %bitcast.23, bf16[64,8192]{1,0:T(8,128)(2,1)} %bitcast.24, bf16[192,4096]{1,0:T(8,128)(2,1)} %bitcast.22), custom_call_target="tpu_custom_call" | custom-call | bytes 7864320 | tf_op jit(solution)/shard_map/pallas_call | solution.py:337
  13.1 0.0 collective-permute-done.refs_0_
  13.2 3.0 %collective-permute-start.4 = (bf16[8,8320]{1,0:T(8,128)(2,1)S(1)}, bf16[8,8320]{1,0:T(8,128)(2,1)S(1)}, u32[]{:S(2)}, u32[]{:S(2)}) collective-permute-start(bf16[8,8320]{1,0:T(8,128)(2,1)S(1)} %collective-permute-done.refs_0_), channel_id=1, source_target_pairs={{0,1},{1,0},{2,3},{3,2},{4,5},{5,4},{6,7},{7,6},{8,9},{9,8},{10,11... | collective-permute-start | bytes 399368 | tf_op jit(solution)/shard_map/ppermute | solution.py:448
  16.2 0.0 collective-permute-done.1.refs_1_
  16.2 0.1 collective-permute-start.5
  16.3 0.0 collective-permute-done.2.refs_2_
  16.3 0.4 collective-permute-start.6
  16.7 2.2 %collective-permute-done.3.refs_3_ = bf16[8,8320]{1,0:T(8,128)(2,1)S(1)} collective-permute-done((bf16[8,8320]{1,0:T(8,128)(2,1)S(1)}, bf16[8,8320]{1,0:T(8,128)(2,1)S(1)}, u32[]{:S(2)}, u32[]{:S(2)}) %collective-permute-start.3) | collective-permute-done | bytes 133152 | tf_op jit(solution)/shard_map/ppermute | solution.py:445
  18.9 0.0 collective-permute-start.7
  18.9 0.0 collective-permute-done.4.refs_4_
  18.9 0.0 copy-start
  18.9 0.0 copy-start.1
  19.0 0.5 %collective-permute-start.9 = (bf16[64,640]{1,0:T(8,128)(2,1)S(1)}, bf16[64,640]{1,0:T(8,128)(2,1)S(1)}, u32[]{:S(2)}, u32[]{:S(2)}) collective-permute-start(bf16[64,640]{1,0:T(8,128)(2,1)S(1)} %get-tuple-element.55.small_ref), channel_id=1, source_target_pairs={{0,1},{1,0},{2,3},{3,2},{4,5},{5,4},{6,7},{7,6},{8,9},{9,8},{10,11... | collective-permute-start | bytes 245768 | tf_op jit(solution)/shard_map/ppermute | solution.py:450
  19.5 0.0 collective-permute-done.5.refs_5_
  19.5 0.0 collective-permute-done.6.refs_6_
  19.5 0.8 %collective-permute-done.7.refs_7_ = bf16[8,8320]{1,0:T(8,128)(2,1)S(1)} collective-permute-done((bf16[8,8320]{1,0:T(8,128)(2,1)S(1)}, bf16[8,8320]{1,0:T(8,128)(2,1)S(1)}, u32[]{:S(2)}, u32[]{:S(2)}) %collective-permute-start.7) | collective-permute-done | bytes 133152 | tf_op jit(solution)/shard_map/ppermute | solution.py:448
  20.3 2.1 %shard_map.156 = (f32[16,640]{1,0:T(8,128)S(1)}, f32[16,640]{1,0:T(8,128)S(1)}) custom-call(bf16[8,8320]{1,0:T(8,128)(2,1)S(1)} %collective-permute-done.refs_0_, bf16[8,8320]{1,0:T(8,128)(2,1)S(1)} %collective-permute-done.1.refs_1_, bf16[8,8320]{1,0:T(8,128)(2,1)S(1)} %collective-permute-done.2.refs_2_, ...), custom_call_target="tpu_custom_call" | custom-call | tf_op jit(solution)/shard_map/pallas_call | solution.py:337
  22.4 0.2 collective-permute-start.8
  22.6 0.2 shard_map.157
  22.8 0.0 collective-permute-done.9.small_other_ref
  22.8 0.8 %collective-permute-done.8.theirs_ref = f32[16,640]{1,0:T(8,128)S(1)} collective-permute-done((f32[16,640]{1,0:T(8,128)S(1)}, f32[16,640]{1,0:T(8,128)S(1)}, u32[]{:S(2)}, u32[]{:S(2)}) %collective-permute-start.8) | collective-permute-done | bytes 40992 | tf_op jit(solution)/shard_map/ppermute | solution.py:458
  23.6 0.9 %shard_map.158.mine_ref = bf16[16,512]{1,0:T(8,128)(2,1)S(1)} custom-call(f32[16,640]{1,0:T(8,128)S(1)} %get-tuple-element.53.mine_ref, f32[16,640]{1,0:T(8,128)S(1)} %collective-permute-done.8.theirs_ref, bf16[64,640]{1,0:T(8,128)(2,1)S(1)} %get-tuple-element.55.small_ref, bf16[64,640]{1,0:T(8,128)(2,1)S(1)} %collective-permute-done.9.small_other_ref, ...), custom_call_target="tpu_custom_call" | custom-call | tf_op jit(solution)/shard_map/pallas_call | solution.py:337
  24.5 0.2 collective-permute-start.10
  24.8 1.0 %collective-permute-done.10.theirs_ref = bf16[16,512]{1,0:T(8,128)(2,1)S(1)} collective-permute-done((bf16[16,512]{1,0:T(8,128)(2,1)S(1)}, bf16[16,512]{1,0:T(8,128)(2,1)S(1)}, u32[]{:S(2)}, u32[]{:S(2)}) %collective-permute-start.10) | collective-permute-done | bytes 16416 | tf_op jit(solution)/shard_map/ppermute | solution.py:466
  25.8 0.0 collective-permute-done.11.wo_other_ref
  25.8 0.0 copy-done
  25.8 0.0 copy-done.1
  25.8 0.0 copy-start.2
  25.8 0.0 copy-start.3
  25.8 1.0 %shard_map.159 = bf16[32,4096]{1,0:T(8,128)(2,1)S(1)} custom-call(bf16[16,512]{1,0:T(8,128)(2,1)S(1)} %shard_map.158.mine_ref, bf16[16,512]{1,0:T(8,128)(2,1)S(1)} %collective-permute-done.10.theirs_ref, bf16[256,8192]{1,0:T(8,128)(2,1)S(1)} %copy-done, bf16[256,8192]{1,0:T(8,128)(2,1)S(1)} %collective-permute-done.11.wo_other_ref, ...), custom_call_target="tpu_custom_call" | custom-call | tf_op jit(solution)/shard_map/pallas_call | solution.py:337
  26.9 0.1 reshape.30
  27.0 16.6 %all_to_all.5 = bf16[8,4,4096]{2,1,0:T(4,128)(2,1)S(1)} all-to-all(bf16[8,4,4096]{2,1,0:T(4,128)(2,1)S(1)} %reshape.30), channel_id=1, replica_groups=mesh['groups'=2,'adapter'=8,'tensor'=2] {'adapter'}, dimensions={0} | all-to-all | bytes 524288 | tf_op jit(solution)/shard_map/all_to_all | solution.py:480
  43.6 0.1 reshape.31.back_ref
  43.7 0.0 copy-done.2
  43.7 0.0 copy-done.3
  43.7 1.1 %shard_map.160 = bf16[16,4096]{1,0:T(8,128)(2,1)} custom-call(bf16[32,4096]{1,0:T(8,128)(2,1)S(1)} %reshape.31.back_ref, s32[1,16]{1,0:T(1,128)S(1)} %bitcast.19, s32[1,8]{1,0:T(1,128)S(1)} %bitcast.21), custom_call_target="tpu_custom_call" | custom-call | tf_op jit(solution)/shard_map/pallas_call | solution.py:337
Async XLA Ops:
  1.9 23.8 %collective-permute-start.11 = (bf16[256,8192]{1,0:T(8,128)(2,1)}, bf16[256,8192]{1,0:T(8,128)(2,1)S(1)}, u32[]{:S(2)}, u32[]{:S(2)}) collective-permute-start(bf16[256,8192]{1,0:T(8,128)(2,1)} %wo_ref), channel_id=1, source_target_pairs={{0,1},{1,0},{2,3},{3,2},{4,5},{5,4},{6,7},{7,6},{8,9},{9,8},{10,11... | collective-permute-start | bytes 12582920 | tf_op jit(solution)/shard_map/ppermute | solution.py:449
  2.5 10.7 %collective-permute-start = (bf16[8,8320]{1,0:T(8,128)(2,1)S(1)}, bf16[8,8320]{1,0:T(8,128)(2,1)S(1)}, u32[]{:S(2)}, u32[]{:S(2)}) collective-permute-start(bf16[8,8320]{1,0:T(8,128)(2,1)S(1)} %get-tuple-element.38), channel_id=1, source_target_pairs={{0,0},{1,9},{2,2},{3,11},{4,4},{5,13},{6,6},{7,15},{8,8},{9,1},{10... | collective-permute-start | bytes 399368 | tf_op jit(solution)/shard_map/ppermute | solution.py:445
  3.1 13.1 %collective-permute-start.1 = (bf16[8,8320]{1,0:T(8,128)(2,1)S(1)}, bf16[8,8320]{1,0:T(8,128)(2,1)S(1)}, u32[]{:S(2)}, u32[]{:S(2)}) collective-permute-start(bf16[8,8320]{1,0:T(8,128)(2,1)S(1)} %get-tuple-element.47), channel_id=1, source_target_pairs={{0,2},{1,11},{2,4},{3,13},{4,6},{5,15},{6,8},{7,1},{8,10},{9,3},{1... | collective-permute-start | bytes 399368 | tf_op jit(solution)/shard_map/ppermute | solution.py:445
  5.7 10.6 %collective-permute-start.2 = (bf16[8,8320]{1,0:T(8,128)(2,1)S(1)}, bf16[8,8320]{1,0:T(8,128)(2,1)S(1)}, u32[]{:S(2)}, u32[]{:S(2)}) collective-permute-start(bf16[8,8320]{1,0:T(8,128)(2,1)S(1)} %get-tuple-element.48), channel_id=1, source_target_pairs={{0,4},{1,13},{2,6},{3,15},{4,8},{5,1},{6,10},{7,3},{8,12},{9,5},{1... | collective-permute-start | bytes 399368 | tf_op jit(solution)/shard_map/ppermute | solution.py:445
  7.3 11.7 %collective-permute-start.3 = (bf16[8,8320]{1,0:T(8,128)(2,1)S(1)}, bf16[8,8320]{1,0:T(8,128)(2,1)S(1)}, u32[]{:S(2)}, u32[]{:S(2)}) collective-permute-start(bf16[8,8320]{1,0:T(8,128)(2,1)S(1)} %get-tuple-element.49), channel_id=1, source_target_pairs={{0,6},{1,15},{2,8},{3,1},{4,10},{5,3},{6,12},{7,5},{8,14},{9,7},{1... | collective-permute-start | bytes 399368 | tf_op jit(solution)/shard_map/ppermute | solution.py:445
  13.2 5.8 %collective-permute-start.4 = (bf16[8,8320]{1,0:T(8,128)(2,1)S(1)}, bf16[8,8320]{1,0:T(8,128)(2,1)S(1)}, u32[]{:S(2)}, u32[]{:S(2)}) collective-permute-start(bf16[8,8320]{1,0:T(8,128)(2,1)S(1)} %collective-permute-done.refs_0_), channel_id=1, source_target_pairs={{0,1},{1,0},{2,3},{3,2},{4,5},{5,4},{6,7},{7,6},{8,9},{9,8},{10,11... | collective-permute-start | bytes 399368 | tf_op jit(solution)/shard_map/ppermute | solution.py:448
  16.2 3.3 %collective-permute-start.5 = (bf16[8,8320]{1,0:T(8,128)(2,1)S(1)}, bf16[8,8320]{1,0:T(8,128)(2,1)S(1)}, u32[]{:S(2)}, u32[]{:S(2)}) collective-permute-start(bf16[8,8320]{1,0:T(8,128)(2,1)S(1)} %collective-permute-done.1.refs_1_), channel_id=1, source_target_pairs={{0,1},{1,0},{2,3},{3,2},{4,5},{5,4},{6,7},{7,6},{8,9},{9,8},{10,11... | collective-permute-start | bytes 399368 | tf_op jit(solution)/shard_map/ppermute | solution.py:448
  16.3 3.2 %collective-permute-start.6 = (bf16[8,8320]{1,0:T(8,128)(2,1)S(1)}, bf16[8,8320]{1,0:T(8,128)(2,1)S(1)}, u32[]{:S(2)}, u32[]{:S(2)}) collective-permute-start(bf16[8,8320]{1,0:T(8,128)(2,1)S(1)} %collective-permute-done.2.refs_2_), channel_id=1, source_target_pairs={{0,1},{1,0},{2,3},{3,2},{4,5},{5,4},{6,7},{7,6},{8,9},{9,8},{10,11... | collective-permute-start | bytes 399368 | tf_op jit(solution)/shard_map/ppermute | solution.py:448
  18.9 1.4 %collective-permute-start.7 = (bf16[8,8320]{1,0:T(8,128)(2,1)S(1)}, bf16[8,8320]{1,0:T(8,128)(2,1)S(1)}, u32[]{:S(2)}, u32[]{:S(2)}) collective-permute-start(bf16[8,8320]{1,0:T(8,128)(2,1)S(1)} %collective-permute-done.3.refs_3_), channel_id=1, source_target_pairs={{0,1},{1,0},{2,3},{3,2},{4,5},{5,4},{6,7},{7,6},{8,9},{9,8},{10,11... | collective-permute-start | bytes 399368 | tf_op jit(solution)/shard_map/ppermute | solution.py:448
  18.9 6.8 %copy-start = (bf16[256,8192]{1,0:T(8,128)(2,1)S(1)}, bf16[256,8192]{1,0:T(8,128)(2,1)}, u32[]{:S(2)}) copy-start(bf16[256,8192]{1,0:T(8,128)(2,1)} %wo_ref) | copy-start | bytes 12582916
  18.9 6.8 %copy-start.1 = (bf16[1,64,4096]{2,1,0:T(8,128)(2,1)S(1)}, bf16[1,64,4096]{2,1,0:T(8,128)(2,1)}, u32[]{:S(2)}) copy-start(bf16[1,64,4096]{2,1,0:T(8,128)(2,1)} %param.31) | copy-start | bytes 1572868
  19.0 3.9 %collective-permute-start.9 = (bf16[64,640]{1,0:T(8,128)(2,1)S(1)}, bf16[64,640]{1,0:T(8,128)(2,1)S(1)}, u32[]{:S(2)}, u32[]{:S(2)}) collective-permute-start(bf16[64,640]{1,0:T(8,128)(2,1)S(1)} %get-tuple-element.55.small_ref), channel_id=1, source_target_pairs={{0,1},{1,0},{2,3},{3,2},{4,5},{5,4},{6,7},{7,6},{8,9},{9,8},{10,11... | collective-permute-start | bytes 245768 | tf_op jit(solution)/shard_map/ppermute | solution.py:450
  22.4 1.3 %collective-permute-start.8 = (f32[16,640]{1,0:T(8,128)S(1)}, f32[16,640]{1,0:T(8,128)S(1)}, u32[]{:S(2)}, u32[]{:S(2)}) collective-permute-start(f32[16,640]{1,0:T(8,128)S(1)} %get-tuple-element.54), channel_id=1, source_target_pairs={{0,1},{1,0},{2,3},{3,2},{4,5},{5,4},{6,7},{7,6},{8,9},{9,8},{10,11... | collective-permute-start | bytes 122888 | tf_op jit(solution)/shard_map/ppermute | solution.py:458
  24.5 1.2 %collective-permute-start.10 = (bf16[16,512]{1,0:T(8,128)(2,1)S(1)}, bf16[16,512]{1,0:T(8,128)(2,1)S(1)}, u32[]{:S(2)}, u32[]{:S(2)}) collective-permute-start(bf16[16,512]{1,0:T(8,128)(2,1)S(1)} %shard_map.158.mine_ref), channel_id=1, source_target_pairs={{0,1},{1,0},{2,3},{3,2},{4,5},{5,4},{6,7},{7,6},{8,9},{9,8},{10,11... | collective-permute-start | bytes 49160 | tf_op jit(solution)/shard_map/ppermute | solution.py:466
  25.8 17.9 %copy-start.2 = (s32[16,1]{0,1:T(1,128)S(1)}, s32[16,1]{0,1:T(1,128)}, u32[]{:S(2)}) copy-start(s32[16,1]{0,1:T(1,128)} %param.24) | copy-start | bytes 196
  25.8 17.9 %copy-start.3 = (s32[8]{0:T(128)S(1)}, s32[8]{0:T(128)}, u32[]{:S(2)}) copy-start(s32[8]{0:T(128)} %param.25) | copy-start | bytes 100

commit v4 on v3

--- a/solution.py
+++ b/solution.py
@@ -283,46 +283,52 @@
             ]
 
 
-def output_kernel(capacity, owners, mine_ref, theirs_ref, wo_ref, wo_other_ref, small_ref, small_other_ref, up_ref, out_ref):
+def output_kernel(count, attended_ref, wo_ref, wo_other_ref, small_ref, small_other_ref, up_ref, up_other_ref, *blocks):
     core = lax.axis_index("tensor")
-    slots, cols = mine_ref.shape
+    slots, cols = attended_ref.shape
     hcols = cols // 2
-    half = out_ref.shape[1]
-    rows = owners * capacity
-    theirs = theirs_ref[...]
-    rows_in = jnp.concatenate(
-        [mine_ref[...], jnp.concatenate([theirs[:, hcols:], theirs[:, :hcols]], axis=1)], axis=0
-    )
-    count = owners // 2
-    per_owner = slots // count
-    out_row = iota((rows, 2 * slots), 0)
-    ahead = lax.axis_index("adapter") - core * count - out_row // capacity
-    ahead = jnp.where(ahead < -owners, ahead + 2 * owners, jnp.where(ahead < 0, ahead + owners, ahead))
-    source = jnp.where(ahead < count, ahead * per_owner, slots + (ahead - count) * per_owner)
-    source = source + out_row % capacity
-    arrange = ones_where(iota((rows, 2 * slots), 1) == source)
-    attended = nn(arrange, rows_in).astype(BF16)
+    per_block, half = blocks[0].shape
+    kept = per_block // 2
+    rows = count * per_block
+    slot = iota((rows, slots), 0)
+    slot = slot // per_block * kept + slot % kept
+    attended = nn(ones_where(iota((rows, slots), 1) == slot), attended_ref[...]).astype(BF16)
     left, right = attended[:, :hcols], attended[:, hcols:]
     down = slice(small_ref.shape[1] - hcols, small_ref.shape[1])
     ranks = (nt(left, small_ref[:, down]) + nt(right, small_other_ref[:, down])).astype(BF16)
     step = 512
+    side = iota((rows, step), 0) % per_block // kept
     for c in range(0, half, step):
-        delta = nn(ranks, up_ref[:, c : c + step]).astype(BF16).astype(F32)
-        columns = pl.ds(pl.multiple_of(core * half + c, step), step)
-        terms = nn(left, wo_ref[:, columns]) + nn(right, wo_other_ref[:, columns])
-        out_ref[:, c : c + step] = (terms + delta).astype(BF16)
-
-
-def pick_kernel(capacity, back_ref, named_ref, table_ref, out_ref):
-    rows, half = back_ref.shape
+        near, far = slice(c, c + step), slice(half + c, half + c + step)
+        terms = jnp.where(
+            side == 0,
+            nn(left, wo_ref[:, near]) + nn(right, wo_other_ref[:, near]),
+            nn(left, wo_ref[:, far]) + nn(right, wo_other_ref[:, far]),
+        )
+        delta = jnp.where(side == core, nn(ranks, up_ref[:, near]), nn(ranks, up_other_ref[:, near]))
+        done = (terms + delta.astype(BF16).astype(F32)).astype(BF16)
+        for j, block in enumerate(blocks):
+            block[:, near] = done[j * per_block : (j + 1) * per_block]
+
+
+def pick_kernel(count, *refs):
+    blocks = refs[: 2 * count]
+    named_ref, table_ref, out_ref = refs[2 * count :]
+    core = lax.axis_index("tensor")
+    owners = 2 * count
+    per_block, half = blocks[0].shape
+    rows = owners * per_block
     requests = out_ref.shape[0]
     owner, standing = owner_and_standing(named_ref[...], table_ref[...])
-    place = ones_where(iota((rows, requests), 0) == owner * capacity + standing)
+    ahead = owner - lax.axis_index("adapter") - core * count
+    ahead = jnp.where(ahead < -owners, ahead + 2 * owners, jnp.where(ahead < 0, ahead + owners, ahead))
+    source = ahead * per_block + core * (per_block // 2) + standing
+    place = ones_where(iota((rows, requests), 0) == source)
     step = 512
     for c in range(0, half, step):
         out_ref[:, c : c + step] = lax.dot_general(
             place,
-            back_ref[:, c : c + step],
+            stacked(blocks, slice(c, c + step)),
             (((0,), (0,)), ((), ())),
             preferred_element_type=F32,
         ).astype(BF16)
@@ -419,10 +425,8 @@
     down = projection_adapter_down[0].T
     wk, wv = key_projection.T, value_projection.T
     kvcols = 2 * wk.shape[0]
-    *packed, query_projection, wk, wv, down, output_projection, output_adapter_up = (
-        lax.optimization_barrier(
-            (*packed, query_projection, wk, wv, down, output_projection, output_adapter_up)
-        )
+    *packed, query_projection, wk, wv, down, output_projection = lax.optimization_barrier(
+        (*packed, query_projection, wk, wv, down, output_projection)
     )
     weights = call(
         stage_kernel,
@@ -447,7 +451,6 @@
     arrived[0], *weights = lax.optimization_barrier((arrived[0], *weights))
     passed = [lax.ppermute(one, "tensor", SWAP) for one in arrived]
     wo_other = lax.ppermute(output_projection, "tensor", SWAP)
-    small_other = lax.ppermute(small, "tensor", SWAP)
     pcols = qcols + kvcols + (down.shape[0] + LANES - 1) // LANES * LANES
     mine, theirs = call(
         functools.partial(project_kernel, count),
@@ -455,7 +458,12 @@
         [pltpu.VMEM((pcols // LANES, 4 * slots, LANES), F32)],
         vmem=24,
     )(*arrived, *passed, *weights)
+    theirs, mine, small, out_up = lax.optimization_barrier(
+        (theirs, mine, small, output_adapter_up[0])
+    )
     theirs = lax.ppermute(theirs, "tensor", SWAP)
+    small_other = lax.ppermute(small, "tensor", SWAP)
+    out_up_other = lax.ppermute(out_up, "tensor", SWAP)
     keys, values, lengths, cosine, sine = call(
         functools.partial(unpack_kernel, count),
         [shape((slots * positions, HEAD_SIZE), BF16)] * 2 + [shape((slots, LANES), F32)] * 3,
@@ -463,25 +471,18 @@
     attended = call(attend_kernel, shape((slots, 2 * qcols), BF16), vmem=16)(
         mine, theirs, small, small_other, keys, values, lengths, cosine, sine
     )
-    attended_other = lax.ppermute(attended, "tensor", SWAP)
     finished = call(
-        functools.partial(output_kernel, capacity, owners),
-        shape((owners * capacity, half), BF16),
+        functools.partial(output_kernel, count),
+        [shape((2 * kept, half), BF16)] * count,
         vmem=16,
-    )(
-        attended,
-        attended_other,
-        output_projection,
-        wo_other,
-        small,
-        small_other,
-        output_adapter_up[0],
-    )
-    back = lax.all_to_all(
-        finished.reshape(owners, capacity, half), "adapter", split_axis=0, concat_axis=0, tiled=True
-    ).reshape(owners * capacity, half)
-    return call(functools.partial(pick_kernel, capacity), shape((requests, half), BF16))(
-        back, named, table
+    )(attended, output_projection, wo_other, small, small_other, out_up, out_up_other)
+    returned = [
+        lax.ppermute(one, ("adapter", "tensor"), [(b, a) for a, b in onward(n)])
+        for n, one in enumerate(finished)
+    ]
+    returned += [lax.ppermute(one, "tensor", SWAP) for one in returned]
+    return call(functools.partial(pick_kernel, count), shape((requests, half), BF16))(
+        *returned, named, table
     )
 
 

time: 44.9 us -> 43.6 us (0.971)
  blocking collectives: 16.6 us -> 0 us
  starting transfers between devices: 12.4 us -> 25.8 us
  waiting for transfers between devices: 4.9 us -> 6.2 us
  Pallas kernels: 10.5 us -> 11.3 us
    all_to_all x1 -> x0, blocking collectives: 16.6 us -> none  [body(): lax.all_to_all(finished.reshape(owners, capacity, half), 'adapter', split...]
    ppermute x1 -> x9, starting transfers between devices: 0.23 us -> 13.9 us  [the longest x4 7.27 us: body(): lax.ppermute(one, ('adapter', 'tensor'), [(b, a) for a, b in onward(n)])]
    pallas_call x7, Pallas kernels: 10.5 us -> 11.3 us  [call(): pl.pallas_call(kernel, out_shape=outs, in_specs=[OUTSIDE if i in outside...]
    ppermute x4, waiting for transfers between devices: 0.83 us -> 1.34 us  [body(): passed = [lax.ppermute(one, 'tensor', SWAP) for one in arrived]]
    ppermute x1 -> x9, waiting for transfers between devices: 1.02 us -> 1.47 us  [the longest x4 0.9 us: body(): returned += [lax.ppermute(one, 'tensor', SWAP) for one in returned]]
  transfers between devices with their start and end apart: 12 -> 20, of which waited for: 4 -> 5; matrix products, arithmetic and copies ran while one was open for 0% -> 0% of each run, Pallas kernels for 15% -> 15%
where the time goes in v4:
time: 43.6 us; the launch traced here: 43.5 us
  starting transfers between devices  25.8 us (59%)
  Pallas kernels  11.3 us (26%)
  waiting for transfers between devices  6.2 us (14%)
    pallas_call x7, Pallas kernels, call(): pl.pallas_call(kernel, out_shape=outs, in_specs=[OUTSIDE if i in outside...  11.3 us
    ppermute x4, starting transfers between devices, body(): lax.ppermute(one, ('adapter', 'tensor'), onward(n))  7.36 us
    ppermute x4, starting transfers between devices, body(): lax.ppermute(one, ('adapter', 'tensor'), [(b, a) for a, b in onward(n)])  7.27 us
    ppermute x4, starting transfers between devices, body(): returned += [lax.ppermute(one, 'tensor', SWAP) for one in returned]  6.41 us
    ppermute x4, starting transfers between devices, body(): passed = [lax.ppermute(one, 'tensor', SWAP) for one in arrived]  3.54 us
    ppermute x4, waiting for transfers between devices, body(): lax.ppermute(one, ('adapter', 'tensor'), onward(n))  2.21 us
    ppermute x4, waiting for transfers between devices, body(): passed = [lax.ppermute(one, 'tensor', SWAP) for one in arrived]  1.34 us
    ppermute x1, waiting for transfers between devices, body(): theirs = lax.ppermute(theirs, 'tensor', SWAP)  1.17 us
  transfers between devices with their start and end apart: 20, of which 5 were waited for; matrix products, arithmetic and copies ran while one was open for 0% of the time, Pallas kernels for 15%

profile of v4, /device:TPU:0, one launch (start us, length us, event | category | flops | bytes accessed | tf_op | source)
XLA Modules:
  0.0 43.5 jit_solution(5748906157194749618)
XLA Ops:
  0.0 1.9 %shard_map.154 = (bf16[8,8320]{1,0:T(8,128)(2,1)S(1)}, bf16[8,8320]{1,0:T(8,128)(2,1)S(1)}, bf16[8,8320]{1,0:T(8,128)(2,1)S(1)}, bf16[8,8320]{1,0:T(8,128)(2,1)S(1)}, bf16[64,640]{1,0:T(8,128)(2,1)S(1)}) custom-call(bf16[16,8192]{1,0:T(8,128)(2,1)} %x_hbm.1, f32[1,8192]{1,0:T(1,128)} %bitcast.28, bf16[512,128]{1,0:T(8,128)(2,1)} %bitcast.26, ...), custom_call_target="tpu_custom_call" | custom-call | tf_op jit(solution)/shard_map/pallas_call | solution.py:343
  1.9 0.5 %collective-permute-start.10 = (bf16[256,8192]{1,0:T(8,128)(2,1)}, bf16[256,8192]{1,0:T(8,128)(2,1)S(1)}, u32[]{:S(2)}, u32[]{:S(2)}) collective-permute-start(bf16[256,8192]{1,0:T(8,128)(2,1)} %wo_ref), channel_id=1, source_target_pairs={{0,1},{1,0},{2,3},{3,2},{4,5},{5,4},{6,7},{7,6},{8,9},{9,8},{10,11... | collective-permute-start | bytes 12582920 | tf_op jit(solution)/shard_map/ppermute | solution.py:453
  2.5 0.7 %collective-permute-start = (bf16[8,8320]{1,0:T(8,128)(2,1)S(1)}, bf16[8,8320]{1,0:T(8,128)(2,1)S(1)}, u32[]{:S(2)}, u32[]{:S(2)}) collective-permute-start(bf16[8,8320]{1,0:T(8,128)(2,1)S(1)} %get-tuple-element.45), channel_id=1, source_target_pairs={{0,0},{1,9},{2,2},{3,11},{4,4},{5,13},{6,6},{7,15},{8,8},{9,1},{10... | collective-permute-start | bytes 399368 | tf_op jit(solution)/shard_map/ppermute | solution.py:449
  3.1 2.6 %collective-permute-start.1 = (bf16[8,8320]{1,0:T(8,128)(2,1)S(1)}, bf16[8,8320]{1,0:T(8,128)(2,1)S(1)}, u32[]{:S(2)}, u32[]{:S(2)}) collective-permute-start(bf16[8,8320]{1,0:T(8,128)(2,1)S(1)} %get-tuple-element.54), channel_id=1, source_target_pairs={{0,2},{1,11},{2,4},{3,13},{4,6},{5,15},{6,8},{7,1},{8,10},{9,3},{1... | collective-permute-start | bytes 399368 | tf_op jit(solution)/shard_map/ppermute | solution.py:449
  5.7 1.6 %collective-permute-start.2 = (bf16[8,8320]{1,0:T(8,128)(2,1)S(1)}, bf16[8,8320]{1,0:T(8,128)(2,1)S(1)}, u32[]{:S(2)}, u32[]{:S(2)}) collective-permute-start(bf16[8,8320]{1,0:T(8,128)(2,1)S(1)} %get-tuple-element.55), channel_id=1, source_target_pairs={{0,4},{1,13},{2,6},{3,15},{4,8},{5,1},{6,10},{7,3},{8,12},{9,5},{1... | collective-permute-start | bytes 399368 | tf_op jit(solution)/shard_map/ppermute | solution.py:449
  7.3 2.6 %collective-permute-start.3 = (bf16[8,8320]{1,0:T(8,128)(2,1)S(1)}, bf16[8,8320]{1,0:T(8,128)(2,1)S(1)}, u32[]{:S(2)}, u32[]{:S(2)}) collective-permute-start(bf16[8,8320]{1,0:T(8,128)(2,1)S(1)} %get-tuple-element.56), channel_id=1, source_target_pairs={{0,6},{1,15},{2,8},{3,1},{4,10},{5,3},{6,12},{7,5},{8,14},{9,7},{1... | collective-permute-start | bytes 399368 | tf_op jit(solution)/shard_map/ppermute | solution.py:449
  9.8 3.3 %shard_map.155 = (bf16[8192,256]{1,0:T(8,128)(2,1)S(1)}, bf16[128,8192]{1,0:T(8,128)(2,1)S(1)}, bf16[192,4096]{1,0:T(8,128)(2,1)S(1)}) custom-call(bf16[8192,256]{1,0:T(8,128)(2,1)} %wq_hbm, bf16[64,8192]{1,0:T(8,128)(2,1)} %bitcast.24, bf16[64,8192]{1,0:T(8,128)(2,1)} %bitcast.25, bf16[192,4096]{1,0:T(8,128)(2,1)} %bitcast.23), custom_call_target="tpu_custom_call" | custom-call | bytes 7864320 | tf_op jit(solution)/shard_map/pallas_call | solution.py:343
  13.1 0.0 collective-permute-done.refs_0_
  13.2 0.0 copy-start.1
  13.2 0.0 copy-start
  13.2 3.0 %collective-permute-start.4 = (bf16[8,8320]{1,0:T(8,128)(2,1)S(1)}, bf16[8,8320]{1,0:T(8,128)(2,1)S(1)}, u32[]{:S(2)}, u32[]{:S(2)}) collective-permute-start(bf16[8,8320]{1,0:T(8,128)(2,1)S(1)} %collective-permute-done.refs_0_), channel_id=1, source_target_pairs={{0,1},{1,0},{2,3},{3,2},{4,5},{5,4},{6,7},{7,6},{8,9},{9,8},{10,11... | collective-permute-start | bytes 399368 | tf_op jit(solution)/shard_map/ppermute | solution.py:452
  16.2 0.0 collective-permute-done.1.refs_1_
  16.2 0.1 collective-permute-start.5
  16.3 0.0 collective-permute-done.2.refs_2_
  16.3 0.4 collective-permute-start.6
  16.7 2.2 %collective-permute-done.3.refs_3_ = bf16[8,8320]{1,0:T(8,128)(2,1)S(1)} collective-permute-done((bf16[8,8320]{1,0:T(8,128)(2,1)S(1)}, bf16[8,8320]{1,0:T(8,128)(2,1)S(1)}, u32[]{:S(2)}, u32[]{:S(2)}) %collective-permute-start.3) | collective-permute-done | bytes 133152 | tf_op jit(solution)/shard_map/ppermute | solution.py:449
  18.9 0.0 collective-permute-start.7
  18.9 0.0 collective-permute-done.4.refs_4_
  18.9 0.0 collective-permute-done.5.refs_5_
  18.9 0.0 collective-permute-done.6.refs_6_
  19.0 1.3 %collective-permute-done.7.refs_7_ = bf16[8,8320]{1,0:T(8,128)(2,1)S(1)} collective-permute-done((bf16[8,8320]{1,0:T(8,128)(2,1)S(1)}, bf16[8,8320]{1,0:T(8,128)(2,1)S(1)}, u32[]{:S(2)}, u32[]{:S(2)}) %collective-permute-start.7) | collective-permute-done | bytes 133152 | tf_op jit(solution)/shard_map/ppermute | solution.py:452
  20.3 2.1 %shard_map.156 = (f32[16,640]{1,0:T(8,128)S(1)}, f32[16,640]{1,0:T(8,128)S(1)}) custom-call(bf16[8,8320]{1,0:T(8,128)(2,1)S(1)} %collective-permute-done.refs_0_, bf16[8,8320]{1,0:T(8,128)(2,1)S(1)} %collective-permute-done.1.refs_1_, bf16[8,8320]{1,0:T(8,128)(2,1)S(1)} %collective-permute-done.2.refs_2_, ...), custom_call_target="tpu_custom_call" | custom-call | tf_op jit(solution)/shard_map/pallas_call | solution.py:343
  22.4 0.2 collective-permute-start.11
  22.6 0.4 collective-permute-start.9
  22.9 0.1 collective-permute-start.8
  23.1 0.2 shard_map.157
  23.3 1.2 %collective-permute-done.8.theirs_ref = f32[16,640]{1,0:T(8,128)S(1)} collective-permute-done((f32[16,640]{1,0:T(8,128)S(1)}, f32[16,640]{1,0:T(8,128)S(1)}, u32[]{:S(2)}, u32[]{:S(2)}) %collective-permute-start.8) | collective-permute-done | bytes 40992 | tf_op jit(solution)/shard_map/ppermute | solution.py:464
  24.5 0.0 collective-permute-done.9.small_other_ref
  24.5 0.9 %shard_map.158.attended_ref = bf16[16,512]{1,0:T(8,128)(2,1)S(1)} custom-call(f32[16,640]{1,0:T(8,128)S(1)} %get-tuple-element.63.mine_ref, f32[16,640]{1,0:T(8,128)S(1)} %collective-permute-done.8.theirs_ref, bf16[64,640]{1,0:T(8,128)(2,1)S(1)} %get-tuple-element.65.small_ref, bf16[64,640]{1,0:T(8,128)(2,1)S(1)} %collective-permute-done.9.small_other_ref, ...), custom_call_target="tpu_custom_call" | custom-call | tf_op jit(solution)/shard_map/pallas_call | solution.py:343
  25.4 0.0 copy-start.2
  25.4 0.0 copy-start.3
  25.4 0.0 collective-permute-done.11.up_other_ref
  25.4 0.0 collective-permute-done.10.wo_other_ref
  25.5 1.8 %shard_map.159 = (bf16[8,4096]{1,0:T(8,128)(2,1)S(1)}, bf16[8,4096]{1,0:T(8,128)(2,1)S(1)}, bf16[8,4096]{1,0:T(8,128)(2,1)S(1)}, bf16[8,4096]{1,0:T(8,128)(2,1)S(1)}) custom-call(bf16[16,512]{1,0:T(8,128)(2,1)S(1)} %shard_map.158.attended_ref, bf16[256,8192]{1,0:T(8,128)(2,1)S(1)} %copy-done, bf16[256,8192]{1,0:T(8,128)(2,1)S(1)} %collective-permute-done.10.wo_other_ref, ...), custom_call_target="tpu_custom_call" | custom-call | tf_op jit(solution)/shard_map/pallas_call | solution.py:343
  27.2 0.7 %collective-permute-start.12 = (bf16[8,4096]{1,0:T(8,128)(2,1)S(1)}, bf16[8,4096]{1,0:T(8,128)(2,1)S(1)}, u32[]{:S(2)}, u32[]{:S(2)}) collective-permute-start(bf16[8,4096]{1,0:T(8,128)(2,1)S(1)} %get-tuple-element.73), channel_id=1, source_target_pairs={{0,0},{9,1},{2,2},{11,3},{4,4},{13,5},{6,6},{15,7},{8,8},{1,9},{10... | collective-permute-start | bytes 196616 | tf_op jit(solution)/shard_map/ppermute | solution.py:480
  27.9 6.2 %collective-permute-start.13 = (bf16[8,4096]{1,0:T(8,128)(2,1)S(1)}, bf16[8,4096]{1,0:T(8,128)(2,1)S(1)}, u32[]{:S(2)}, u32[]{:S(2)}) collective-permute-start(bf16[8,4096]{1,0:T(8,128)(2,1)S(1)} %get-tuple-element.74), channel_id=1, source_target_pairs={{2,0},{11,1},{4,2},{13,3},{6,4},{15,5},{8,6},{1,7},{10,8},{3,9},{1... | collective-permute-start | bytes 196616 | tf_op jit(solution)/shard_map/ppermute | solution.py:480
  34.1 0.4 collective-permute-start.14
  34.5 0.0 collective-permute-start.15
  34.5 0.0 collective-permute-done.12.refs_0_
  34.5 1.5 %collective-permute-start.16 = (bf16[8,4096]{1,0:T(8,128)(2,1)S(1)}, bf16[8,4096]{1,0:T(8,128)(2,1)S(1)}, u32[]{:S(2)}, u32[]{:S(2)}) collective-permute-start(bf16[8,4096]{1,0:T(8,128)(2,1)S(1)} %collective-permute-done.12.refs_0_), channel_id=1, source_target_pairs={{0,1},{1,0},{2,3},{3,2},{4,5},{5,4},{6,7},{7,6},{8,9},{9,8},{10,11... | collective-permute-start | bytes 196616 | tf_op jit(solution)/shard_map/ppermute | solution.py:483
  36.0 0.0 collective-permute-done.13.refs_1_
  36.0 1.8 %collective-permute-start.17 = (bf16[8,4096]{1,0:T(8,128)(2,1)S(1)}, bf16[8,4096]{1,0:T(8,128)(2,1)S(1)}, u32[]{:S(2)}, u32[]{:S(2)}) collective-permute-start(bf16[8,4096]{1,0:T(8,128)(2,1)S(1)} %collective-permute-done.13.refs_1_), channel_id=1, source_target_pairs={{0,1},{1,0},{2,3},{3,2},{4,5},{5,4},{6,7},{7,6},{8,9},{9,8},{10,11... | collective-permute-start | bytes 196616 | tf_op jit(solution)/shard_map/ppermute | solution.py:483
  37.8 0.6 %collective-permute-done.14.refs_2_ = bf16[8,4096]{1,0:T(8,128)(2,1)S(1)} collective-permute-done((bf16[8,4096]{1,0:T(8,128)(2,1)S(1)}, bf16[8,4096]{1,0:T(8,128)(2,1)S(1)}, u32[]{:S(2)}, u32[]{:S(2)}) %collective-permute-start.14) | collective-permute-done | bytes 65568 | tf_op jit(solution)/shard_map/ppermute | solution.py:480
  38.4 2.2 %collective-permute-start.18 = (bf16[8,4096]{1,0:T(8,128)(2,1)S(1)}, bf16[8,4096]{1,0:T(8,128)(2,1)S(1)}, u32[]{:S(2)}, u32[]{:S(2)}) collective-permute-start(bf16[8,4096]{1,0:T(8,128)(2,1)S(1)} %collective-permute-done.14.refs_2_), channel_id=1, source_target_pairs={{0,1},{1,0},{2,3},{3,2},{4,5},{5,4},{6,7},{7,6},{8,9},{9,8},{10,11... | collective-permute-start | bytes 196616 | tf_op jit(solution)/shard_map/ppermute | solution.py:483
  40.6 0.0 collective-permute-done.15.refs_3_
  40.6 0.9 %collective-permute-start.19 = (bf16[8,4096]{1,0:T(8,128)(2,1)S(1)}, bf16[8,4096]{1,0:T(8,128)(2,1)S(1)}, u32[]{:S(2)}, u32[]{:S(2)}) collective-permute-start(bf16[8,4096]{1,0:T(8,128)(2,1)S(1)} %collective-permute-done.15.refs_3_), channel_id=1, source_target_pairs={{0,1},{1,0},{2,3},{3,2},{4,5},{5,4},{6,7},{7,6},{8,9},{9,8},{10,11... | collective-permute-start | bytes 196616 | tf_op jit(solution)/shard_map/ppermute | solution.py:483
  41.5 0.9 %collective-permute-done.19.refs_7_ = bf16[8,4096]{1,0:T(8,128)(2,1)S(1)} collective-permute-done((bf16[8,4096]{1,0:T(8,128)(2,1)S(1)}, bf16[8,4096]{1,0:T(8,128)(2,1)S(1)}, u32[]{:S(2)}, u32[]{:S(2)}) %collective-permute-start.19) | collective-permute-done | bytes 65568 | tf_op jit(solution)/shard_map/ppermute | solution.py:483
  42.4 1.1 %shard_map.160 = bf16[16,4096]{1,0:T(8,128)(2,1)} custom-call(bf16[8,4096]{1,0:T(8,128)(2,1)S(1)} %collective-permute-done.12.refs_0_, bf16[8,4096]{1,0:T(8,128)(2,1)S(1)} %collective-permute-done.13.refs_1_, bf16[8,4096]{1,0:T(8,128)(2,1)S(1)} %collective-permute-done.14.refs_2_, bf16[8,4096]{1,0:T(8,128)(2,1)S(1)} %collective-permute-done.15.refs_3_, ...), custom_call_target="tpu_custom_call" | custom-call | tf_op jit(solution)/shard_map/pallas_call | solution.py:343
  (7 shorter events, 0.0 us)
Async XLA Ops:
  1.9 23.5 %collective-permute-start.10 = (bf16[256,8192]{1,0:T(8,128)(2,1)}, bf16[256,8192]{1,0:T(8,128)(2,1)S(1)}, u32[]{:S(2)}, u32[]{:S(2)}) collective-permute-start(bf16[256,8192]{1,0:T(8,128)(2,1)} %wo_ref), channel_id=1, source_target_pairs={{0,1},{1,0},{2,3},{3,2},{4,5},{5,4},{6,7},{7,6},{8,9},{9,8},{10,11... | collective-permute-start | bytes 12582920 | tf_op jit(solution)/shard_map/ppermute | solution.py:453
  2.5 10.7 %collective-permute-start = (bf16[8,8320]{1,0:T(8,128)(2,1)S(1)}, bf16[8,8320]{1,0:T(8,128)(2,1)S(1)}, u32[]{:S(2)}, u32[]{:S(2)}) collective-permute-start(bf16[8,8320]{1,0:T(8,128)(2,1)S(1)} %get-tuple-element.45), channel_id=1, source_target_pairs={{0,0},{1,9},{2,2},{3,11},{4,4},{5,13},{6,6},{7,15},{8,8},{9,1},{10... | collective-permute-start | bytes 399368 | tf_op jit(solution)/shard_map/ppermute | solution.py:449
  3.1 13.1 %collective-permute-start.1 = (bf16[8,8320]{1,0:T(8,128)(2,1)S(1)}, bf16[8,8320]{1,0:T(8,128)(2,1)S(1)}, u32[]{:S(2)}, u32[]{:S(2)}) collective-permute-start(bf16[8,8320]{1,0:T(8,128)(2,1)S(1)} %get-tuple-element.54), channel_id=1, source_target_pairs={{0,2},{1,11},{2,4},{3,13},{4,6},{5,15},{6,8},{7,1},{8,10},{9,3},{1... | collective-permute-start | bytes 399368 | tf_op jit(solution)/shard_map/ppermute | solution.py:449
  5.7 10.6 %collective-permute-start.2 = (bf16[8,8320]{1,0:T(8,128)(2,1)S(1)}, bf16[8,8320]{1,0:T(8,128)(2,1)S(1)}, u32[]{:S(2)}, u32[]{:S(2)}) collective-permute-start(bf16[8,8320]{1,0:T(8,128)(2,1)S(1)} %get-tuple-element.55), channel_id=1, source_target_pairs={{0,4},{1,13},{2,6},{3,15},{4,8},{5,1},{6,10},{7,3},{8,12},{9,5},{1... | collective-permute-start | bytes 399368 | tf_op jit(solution)/shard_map/ppermute | solution.py:449
  7.3 11.7 %collective-permute-start.3 = (bf16[8,8320]{1,0:T(8,128)(2,1)S(1)}, bf16[8,8320]{1,0:T(8,128)(2,1)S(1)}, u32[]{:S(2)}, u32[]{:S(2)}) collective-permute-start(bf16[8,8320]{1,0:T(8,128)(2,1)S(1)} %get-tuple-element.56), channel_id=1, source_target_pairs={{0,6},{1,15},{2,8},{3,1},{4,10},{5,3},{6,12},{7,5},{8,14},{9,7},{1... | collective-permute-start | bytes 399368 | tf_op jit(solution)/shard_map/ppermute | solution.py:449
  13.2 9.2 %copy-start.1 = (bf16[1,64,4096]{2,1,0:T(8,128)(2,1)S(1)}, bf16[1,64,4096]{2,1,0:T(8,128)(2,1)}, u32[]{:S(2)}) copy-start(bf16[1,64,4096]{2,1,0:T(8,128)(2,1)} %param.31) | copy-start | bytes 1572868
  13.2 12.3 %copy-start = (bf16[256,8192]{1,0:T(8,128)(2,1)S(1)}, bf16[256,8192]{1,0:T(8,128)(2,1)}, u32[]{:S(2)}) copy-start(bf16[256,8192]{1,0:T(8,128)(2,1)} %wo_ref) | copy-start | bytes 12582916
  13.2 5.8 %collective-permute-start.4 = (bf16[8,8320]{1,0:T(8,128)(2,1)S(1)}, bf16[8,8320]{1,0:T(8,128)(2,1)S(1)}, u32[]{:S(2)}, u32[]{:S(2)}) collective-permute-start(bf16[8,8320]{1,0:T(8,128)(2,1)S(1)} %collective-permute-done.refs_0_), channel_id=1, source_target_pairs={{0,1},{1,0},{2,3},{3,2},{4,5},{5,4},{6,7},{7,6},{8,9},{9,8},{10,11... | collective-permute-start | bytes 399368 | tf_op jit(solution)/shard_map/ppermute | solution.py:452
  16.2 2.7 %collective-permute-start.5 = (bf16[8,8320]{1,0:T(8,128)(2,1)S(1)}, bf16[8,8320]{1,0:T(8,128)(2,1)S(1)}, u32[]{:S(2)}, u32[]{:S(2)}) collective-permute-start(bf16[8,8320]{1,0:T(8,128)(2,1)S(1)} %collective-permute-done.1.refs_1_), channel_id=1, source_target_pairs={{0,1},{1,0},{2,3},{3,2},{4,5},{5,4},{6,7},{7,6},{8,9},{9,8},{10,11... | collective-permute-start | bytes 399368 | tf_op jit(solution)/shard_map/ppermute | solution.py:452
  16.3 2.6 %collective-permute-start.6 = (bf16[8,8320]{1,0:T(8,128)(2,1)S(1)}, bf16[8,8320]{1,0:T(8,128)(2,1)S(1)}, u32[]{:S(2)}, u32[]{:S(2)}) collective-permute-start(bf16[8,8320]{1,0:T(8,128)(2,1)S(1)} %collective-permute-done.2.refs_2_), channel_id=1, source_target_pairs={{0,1},{1,0},{2,3},{3,2},{4,5},{5,4},{6,7},{7,6},{8,9},{9,8},{10,11... | collective-permute-start | bytes 399368 | tf_op jit(solution)/shard_map/ppermute | solution.py:452
  18.9 1.4 %collective-permute-start.7 = (bf16[8,8320]{1,0:T(8,128)(2,1)S(1)}, bf16[8,8320]{1,0:T(8,128)(2,1)S(1)}, u32[]{:S(2)}, u32[]{:S(2)}) collective-permute-start(bf16[8,8320]{1,0:T(8,128)(2,1)S(1)} %collective-permute-done.3.refs_3_), channel_id=1, source_target_pairs={{0,1},{1,0},{2,3},{3,2},{4,5},{5,4},{6,7},{7,6},{8,9},{9,8},{10,11... | collective-permute-start | bytes 399368 | tf_op jit(solution)/shard_map/ppermute | solution.py:452
  22.4 3.1 %collective-permute-start.11 = (bf16[64,4096]{1,0:T(8,128)(2,1)S(1)}, bf16[64,4096]{1,0:T(8,128)(2,1)S(1)}, u32[]{:S(2)}, u32[]{:S(2)}) collective-permute-start(bf16[64,4096]{1,0:T(8,128)(2,1)S(1)} %bitcast.17), channel_id=1, source_target_pairs={{0,1},{1,0},{2,3},{3,2},{4,5},{5,4},{6,7},{7,6},{8,9},{9,8},{10,11... | collective-permute-start | bytes 1572872 | tf_op jit(solution)/shard_map/ppermute | solution.py:466
  22.6 1.9 %collective-permute-start.9 = (bf16[64,640]{1,0:T(8,128)(2,1)S(1)}, bf16[64,640]{1,0:T(8,128)(2,1)S(1)}, u32[]{:S(2)}, u32[]{:S(2)}) collective-permute-start(bf16[64,640]{1,0:T(8,128)(2,1)S(1)} %get-tuple-element.65.small_ref), channel_id=1, source_target_pairs={{0,1},{1,0},{2,3},{3,2},{4,5},{5,4},{6,7},{7,6},{8,9},{9,8},{10,11... | collective-permute-start | bytes 245768 | tf_op jit(solution)/shard_map/ppermute | solution.py:465
  22.9 1.6 %collective-permute-start.8 = (f32[16,640]{1,0:T(8,128)S(1)}, f32[16,640]{1,0:T(8,128)S(1)}, u32[]{:S(2)}, u32[]{:S(2)}) collective-permute-start(f32[16,640]{1,0:T(8,128)S(1)} %get-tuple-element.64), channel_id=1, source_target_pairs={{0,1},{1,0},{2,3},{3,2},{4,5},{5,4},{6,7},{7,6},{8,9},{9,8},{10,11... | collective-permute-start | bytes 122888 | tf_op jit(solution)/shard_map/ppermute | solution.py:464
  25.4 17.0 %copy-start.2 = (s32[16,1]{0,1:T(1,128)S(1)}, s32[16,1]{0,1:T(1,128)}, u32[]{:S(2)}) copy-start(s32[16,1]{0,1:T(1,128)} %param.24) | copy-start | bytes 196
  25.4 17.0 %copy-start.3 = (s32[8]{0:T(128)S(1)}, s32[8]{0:T(128)}, u32[]{:S(2)}) copy-start(s32[8]{0:T(128)} %param.25) | copy-start | bytes 100
  27.2 7.3 %collective-permute-start.12 = (bf16[8,4096]{1,0:T(8,128)(2,1)S(1)}, bf16[8,4096]{1,0:T(8,128)(2,1)S(1)}, u32[]{:S(2)}, u32[]{:S(2)}) collective-permute-start(bf16[8,4096]{1,0:T(8,128)(2,1)S(1)} %get-tuple-element.73), channel_id=1, source_target_pairs={{0,0},{9,1},{2,2},{11,3},{4,4},{13,5},{6,6},{15,7},{8,8},{1,9},{10... | collective-permute-start | bytes 196616 | tf_op jit(solution)/shard_map/ppermute | solution.py:480
  27.9 8.1 %collective-permute-start.13 = (bf16[8,4096]{1,0:T(8,128)(2,1)S(1)}, bf16[8,4096]{1,0:T(8,128)(2,1)S(1)}, u32[]{:S(2)}, u32[]{:S(2)}) collective-permute-start(bf16[8,4096]{1,0:T(8,128)(2,1)S(1)} %get-tuple-element.74), channel_id=1, source_target_pairs={{2,0},{11,1},{4,2},{13,3},{6,4},{15,5},{8,6},{1,7},{10,8},{3,9},{1... | collective-permute-start | bytes 196616 | tf_op jit(solution)/shard_map/ppermute | solution.py:480
  34.1 4.3 %collective-permute-start.14 = (bf16[8,4096]{1,0:T(8,128)(2,1)S(1)}, bf16[8,4096]{1,0:T(8,128)(2,1)S(1)}, u32[]{:S(2)}, u32[]{:S(2)}) collective-permute-start(bf16[8,4096]{1,0:T(8,128)(2,1)S(1)} %get-tuple-element.75), channel_id=1, source_target_pairs={{4,0},{13,1},{6,2},{15,3},{8,4},{1,5},{10,6},{3,7},{12,8},{5,9},{1... | collective-permute-start | bytes 196616 | tf_op jit(solution)/shard_map/ppermute | solution.py:480
  34.5 6.1 %collective-permute-start.15 = (bf16[8,4096]{1,0:T(8,128)(2,1)S(1)}, bf16[8,4096]{1,0:T(8,128)(2,1)S(1)}, u32[]{:S(2)}, u32[]{:S(2)}) collective-permute-start(bf16[8,4096]{1,0:T(8,128)(2,1)S(1)} %get-tuple-element.76), channel_id=1, source_target_pairs={{6,0},{15,1},{8,2},{1,3},{10,4},{3,5},{12,6},{5,7},{14,8},{7,9},{0... | collective-permute-start | bytes 196616 | tf_op jit(solution)/shard_map/ppermute | solution.py:480
  34.5 7.0 %collective-permute-start.16 = (bf16[8,4096]{1,0:T(8,128)(2,1)S(1)}, bf16[8,4096]{1,0:T(8,128)(2,1)S(1)}, u32[]{:S(2)}, u32[]{:S(2)}) collective-permute-start(bf16[8,4096]{1,0:T(8,128)(2,1)S(1)} %collective-permute-done.12.refs_0_), channel_id=1, source_target_pairs={{0,1},{1,0},{2,3},{3,2},{4,5},{5,4},{6,7},{7,6},{8,9},{9,8},{10,11... | collective-permute-start | bytes 196616 | tf_op jit(solution)/shard_map/ppermute | solution.py:483
  36.0 5.5 %collective-permute-start.17 = (bf16[8,4096]{1,0:T(8,128)(2,1)S(1)}, bf16[8,4096]{1,0:T(8,128)(2,1)S(1)}, u32[]{:S(2)}, u32[]{:S(2)}) collective-permute-start(bf16[8,4096]{1,0:T(8,128)(2,1)S(1)} %collective-permute-done.13.refs_1_), channel_id=1, source_target_pairs={{0,1},{1,0},{2,3},{3,2},{4,5},{5,4},{6,7},{7,6},{8,9},{9,8},{10,11... | collective-permute-start | bytes 196616 | tf_op jit(solution)/shard_map/ppermute | solution.py:483
  38.4 3.1 %collective-permute-start.18 = (bf16[8,4096]{1,0:T(8,128)(2,1)S(1)}, bf16[8,4096]{1,0:T(8,128)(2,1)S(1)}, u32[]{:S(2)}, u32[]{:S(2)}) collective-permute-start(bf16[8,4096]{1,0:T(8,128)(2,1)S(1)} %collective-permute-done.14.refs_2_), channel_id=1, source_target_pairs={{0,1},{1,0},{2,3},{3,2},{4,5},{5,4},{6,7},{7,6},{8,9},{9,8},{10,11... | collective-permute-start | bytes 196616 | tf_op jit(solution)/shard_map/ppermute | solution.py:483
  40.6 1.8 %collective-permute-start.19 = (bf16[8,4096]{1,0:T(8,128)(2,1)S(1)}, bf16[8,4096]{1,0:T(8,128)(2,1)S(1)}, u32[]{:S(2)}, u32[]{:S(2)}) collective-permute-start(bf16[8,4096]{1,0:T(8,128)(2,1)S(1)} %collective-permute-done.15.refs_3_), channel_id=1, source_target_pairs={{0,1},{1,0},{2,3},{3,2},{4,5},{5,4},{6,7},{7,6},{8,9},{9,8},{10,11... | collective-permute-start | bytes 196616 | tf_op jit(solution)/shard_map/ppermute | solution.py:483

commit v5 on v4

--- a/solution.py
+++ b/solution.py
@@ -59,6 +59,11 @@
     for copy in copies:
         copy.start()
     return copies
+
+
+def block_of(ahead, core, count):
+    ahead = jnp.where(ahead < 0, ahead + 2 * count, ahead)
+    return jnp.where(ahead // count == core, jnp.where(core == 0, count - 1 - ahead, ahead - count), -1)
 
 
 def pack_kernel(capacity, x_hbm, gain_hbm, k_hbm, v_hbm, named_hbm, table_hbm, length_hbm, up_hbm, kv_up_hbm, out_down_hbm, *rest):
@@ -87,14 +92,12 @@
     positions = k_ref.shape[0] // requests
     per_block = blocks[0].shape[0]
     rows = per_block * count
-    first = lax.axis_index("adapter") + lax.axis_index("tensor") * count
     named_copy.wait()
     table_copy.wait()
     length_copy.wait()
     owner, standing = owner_and_standing(named_ref[...], table_ref[...])
-    ahead = owner - first
-    ahead = jnp.where(ahead < -owners, ahead + 2 * owners, jnp.where(ahead < 0, ahead + owners, ahead))
-    row = jnp.where(ahead < count, ahead * per_block + 2 * standing, -2)
+    block = block_of(owner - lax.axis_index("adapter"), lax.axis_index("tensor"), count)
+    row = jnp.where(block < 0, -2, block * per_block + 2 * standing)
     order = iota((rows, requests), 0)
     put_x = ones_where(order == row)
     put_kv = ones_where(order == row + 1)
@@ -320,9 +323,10 @@
     rows = owners * per_block
     requests = out_ref.shape[0]
     owner, standing = owner_and_standing(named_ref[...], table_ref[...])
-    ahead = owner - lax.axis_index("adapter") - core * count
-    ahead = jnp.where(ahead < -owners, ahead + 2 * owners, jnp.where(ahead < 0, ahead + owners, ahead))
-    source = ahead * per_block + core * (per_block // 2) + standing
+    ahead = owner - lax.axis_index("adapter")
+    mine, theirs = block_of(ahead, core, count), block_of(ahead, 1 - core, count)
+    source = jnp.where(mine < 0, count + theirs, mine) * per_block
+    source = source + core * (per_block // 2) + standing
     place = ones_where(iota((rows, requests), 0) == source)
     step = 512
     for c in range(0, half, step):
@@ -441,8 +445,9 @@
     )(query_projection, wk, wv, down)
 
     def onward(n):
+        shifts = (count - 1 - n, count + n)
         return [
-            (a * 2 + t, (a + t * count + n) % owners * 2 + t) for a in range(owners) for t in range(2)
+            (a * 2 + t, (a + shifts[t]) % owners * 2 + t) for a in range(owners) for t in range(2)
         ]
 
     arrived = [

time: 43.6 us -> 41.7 us (0.956)
  starting transfers between devices: 25.8 us -> 20.6 us
  waiting for transfers between devices: 6.2 us -> 9.5 us
    ppermute x4, starting transfers between devices: 6.41 us -> 3.38 us  [body(): returned += [lax.ppermute(one, 'tensor', SWAP) for one in returned]]
    ppermute x4, starting transfers between devices: 3.54 us -> 1.02 us  [body(): passed = [lax.ppermute(one, 'tensor', SWAP) for one in arrived]]
    ppermute x4, waiting for transfers between devices: 2.21 us -> 4.41 us  [body(): lax.ppermute(one, ('adapter', 'tensor'), onward(n))]
    ppermute x4, waiting for transfers between devices: 0.57 us -> 2.17 us  [body(): lax.ppermute(one, ('adapter', 'tensor'), [(b, a) for a, b in onward(n)])]
  transfers between devices with their start and end apart: 20 -> 20, of which waited for: 5 -> 8; matrix products, arithmetic and copies ran while one was open for 0% -> 0% of each run, Pallas kernels for 15% -> 16%
where the time goes in v5:
time: 41.7 us; the launch traced here: 41.5 us
  starting transfers between devices  20.6 us (49%)
  Pallas kernels  11.3 us (27%)
  waiting for transfers between devices  9.5 us (23%)
    pallas_call x7, Pallas kernels, call(): pl.pallas_call(kernel, out_shape=outs, in_specs=[OUTSIDE if i in outside...  11.3 us
    ppermute x4, starting transfers between devices, body(): lax.ppermute(one, ('adapter', 'tensor'), [(b, a) for a, b in onward(n)])  7.44 us
    ppermute x4, starting transfers between devices, body(): lax.ppermute(one, ('adapter', 'tensor'), onward(n))  7.35 us
    ppermute x4, waiting for transfers between devices, body(): lax.ppermute(one, ('adapter', 'tensor'), onward(n))  4.41 us
    ppermute x4, starting transfers between devices, body(): returned += [lax.ppermute(one, 'tensor', SWAP) for one in returned]  3.38 us
    ppermute x4, waiting for transfers between devices, body(): lax.ppermute(one, ('adapter', 'tensor'), [(b, a) for a, b in onward(n)])  2.17 us
    ppermute x4, waiting for transfers between devices, body(): passed = [lax.ppermute(one, 'tensor', SWAP) for one in arrived]  1.03 us
    ppermute x4, starting transfers between devices, body(): passed = [lax.ppermute(one, 'tensor', SWAP) for one in arrived]  1.02 us
  transfers between devices with their start and end apart: 20, of which 8 were waited for; matrix products, arithmetic and copies ran while one was open for 0% of the time, Pallas kernels for 16%

profile of v5, /device:TPU:0, one launch (start us, length us, event | category | flops | bytes accessed | tf_op | source)
XLA Modules:
  0.0 41.5 jit_solution(12529339481951723608)
XLA Ops:
  0.0 1.9 %shard_map.154 = (bf16[8,8320]{1,0:T(8,128)(2,1)S(1)}, bf16[8,8320]{1,0:T(8,128)(2,1)S(1)}, bf16[8,8320]{1,0:T(8,128)(2,1)S(1)}, bf16[8,8320]{1,0:T(8,128)(2,1)S(1)}, bf16[64,640]{1,0:T(8,128)(2,1)S(1)}) custom-call(bf16[16,8192]{1,0:T(8,128)(2,1)} %x_hbm.1, f32[1,8192]{1,0:T(1,128)} %bitcast.28, bf16[512,128]{1,0:T(8,128)(2,1)} %bitcast.26, ...), custom_call_target="tpu_custom_call" | custom-call | tf_op jit(solution)/shard_map/pallas_call | solution.py:347
  1.9 0.5 %collective-permute-start.10 = (bf16[256,8192]{1,0:T(8,128)(2,1)}, bf16[256,8192]{1,0:T(8,128)(2,1)S(1)}, u32[]{:S(2)}, u32[]{:S(2)}) collective-permute-start(bf16[256,8192]{1,0:T(8,128)(2,1)} %wo_ref), channel_id=1, source_target_pairs={{0,1},{1,0},{2,3},{3,2},{4,5},{5,4},{6,7},{7,6},{8,9},{9,8},{10,11... | collective-permute-start | bytes 12582920 | tf_op jit(solution)/shard_map/ppermute | solution.py:458
  2.5 3.6 %collective-permute-start = (bf16[8,8320]{1,0:T(8,128)(2,1)S(1)}, bf16[8,8320]{1,0:T(8,128)(2,1)S(1)}, u32[]{:S(2)}, u32[]{:S(2)}) collective-permute-start(bf16[8,8320]{1,0:T(8,128)(2,1)S(1)} %get-tuple-element.45), channel_id=1, source_target_pairs={{0,6},{1,9},{2,8},{3,11},{4,10},{5,13},{6,12},{7,15},{8,14},{9,1},... | collective-permute-start | bytes 399368 | tf_op jit(solution)/shard_map/ppermute | solution.py:454
  6.0 1.6 %collective-permute-start.1 = (bf16[8,8320]{1,0:T(8,128)(2,1)S(1)}, bf16[8,8320]{1,0:T(8,128)(2,1)S(1)}, u32[]{:S(2)}, u32[]{:S(2)}) collective-permute-start(bf16[8,8320]{1,0:T(8,128)(2,1)S(1)} %get-tuple-element.54), channel_id=1, source_target_pairs={{0,4},{1,11},{2,6},{3,13},{4,8},{5,15},{6,10},{7,1},{8,12},{9,3},{... | collective-permute-start | bytes 399368 | tf_op jit(solution)/shard_map/ppermute | solution.py:454
  7.6 1.5 %collective-permute-start.2 = (bf16[8,8320]{1,0:T(8,128)(2,1)S(1)}, bf16[8,8320]{1,0:T(8,128)(2,1)S(1)}, u32[]{:S(2)}, u32[]{:S(2)}) collective-permute-start(bf16[8,8320]{1,0:T(8,128)(2,1)S(1)} %get-tuple-element.55), channel_id=1, source_target_pairs={{0,2},{1,13},{2,4},{3,15},{4,6},{5,1},{6,8},{7,3},{8,10},{9,5},{10... | collective-permute-start | bytes 399368 | tf_op jit(solution)/shard_map/ppermute | solution.py:454
  9.2 0.7 %collective-permute-start.3 = (bf16[8,8320]{1,0:T(8,128)(2,1)S(1)}, bf16[8,8320]{1,0:T(8,128)(2,1)S(1)}, u32[]{:S(2)}, u32[]{:S(2)}) collective-permute-start(bf16[8,8320]{1,0:T(8,128)(2,1)S(1)} %get-tuple-element.56), channel_id=1, source_target_pairs={{0,0},{1,15},{2,2},{3,1},{4,4},{5,3},{6,6},{7,5},{8,8},{9,7},{10,1... | collective-permute-start | bytes 399368 | tf_op jit(solution)/shard_map/ppermute | solution.py:454
  9.8 3.3 %shard_map.155 = (bf16[8192,256]{1,0:T(8,128)(2,1)S(1)}, bf16[128,8192]{1,0:T(8,128)(2,1)S(1)}, bf16[192,4096]{1,0:T(8,128)(2,1)S(1)}) custom-call(bf16[8192,256]{1,0:T(8,128)(2,1)} %wq_hbm, bf16[64,8192]{1,0:T(8,128)(2,1)} %bitcast.24, bf16[64,8192]{1,0:T(8,128)(2,1)} %bitcast.25, bf16[192,4096]{1,0:T(8,128)(2,1)} %bitcast.23), custom_call_target="tpu_custom_call" | custom-call | bytes 7864320 | tf_op jit(solution)/shard_map/pallas_call | solution.py:347
  13.1 2.8 %collective-permute-done.refs_0_ = bf16[8,8320]{1,0:T(8,128)(2,1)S(1)} collective-permute-done((bf16[8,8320]{1,0:T(8,128)(2,1)S(1)}, bf16[8,8320]{1,0:T(8,128)(2,1)S(1)}, u32[]{:S(2)}, u32[]{:S(2)}) %collective-permute-start) | collective-permute-done | bytes 133152 | tf_op jit(solution)/shard_map/ppermute | solution.py:454
  16.0 0.2 collective-permute-start.4
  16.2 0.0 collective-permute-done.1.refs_1_
  16.2 0.3 collective-permute-start.5
  16.5 1.6 %collective-permute-done.2.refs_2_ = bf16[8,8320]{1,0:T(8,128)(2,1)S(1)} collective-permute-done((bf16[8,8320]{1,0:T(8,128)(2,1)S(1)}, bf16[8,8320]{1,0:T(8,128)(2,1)S(1)}, u32[]{:S(2)}, u32[]{:S(2)}) %collective-permute-start.2) | collective-permute-done | bytes 133152 | tf_op jit(solution)/shard_map/ppermute | solution.py:454
  18.1 0.0 collective-permute-start.6
  18.1 0.0 collective-permute-done.3.refs_3_
  18.1 0.5 %collective-permute-start.7 = (bf16[8,8320]{1,0:T(8,128)(2,1)S(1)}, bf16[8,8320]{1,0:T(8,128)(2,1)S(1)}, u32[]{:S(2)}, u32[]{:S(2)}) collective-permute-start(bf16[8,8320]{1,0:T(8,128)(2,1)S(1)} %collective-permute-done.3.refs_3_), channel_id=1, source_target_pairs={{0,1},{1,0},{2,3},{3,2},{4,5},{5,4},{6,7},{7,6},{8,9},{9,8},{10,11... | collective-permute-start | bytes 399368 | tf_op jit(solution)/shard_map/ppermute | solution.py:457
  18.6 0.0 collective-permute-done.4.refs_4_
  18.6 0.0 collective-permute-done.5.refs_5_
  18.6 0.8 %collective-permute-done.6.refs_6_ = bf16[8,8320]{1,0:T(8,128)(2,1)S(1)} collective-permute-done((bf16[8,8320]{1,0:T(8,128)(2,1)S(1)}, bf16[8,8320]{1,0:T(8,128)(2,1)S(1)}, u32[]{:S(2)}, u32[]{:S(2)}) %collective-permute-start.6) | collective-permute-done | bytes 133152 | tf_op jit(solution)/shard_map/ppermute | solution.py:457
  19.4 0.2 collective-permute-done.7.refs_7_
  19.6 2.1 %shard_map.156 = (f32[16,640]{1,0:T(8,128)S(1)}, f32[16,640]{1,0:T(8,128)S(1)}) custom-call(bf16[8,8320]{1,0:T(8,128)(2,1)S(1)} %collective-permute-done.refs_0_, bf16[8,8320]{1,0:T(8,128)(2,1)S(1)} %collective-permute-done.1.refs_1_, bf16[8,8320]{1,0:T(8,128)(2,1)S(1)} %collective-permute-done.2.refs_2_, ...), custom_call_target="tpu_custom_call" | custom-call | tf_op jit(solution)/shard_map/pallas_call | solution.py:347
  21.7 0.4 collective-permute-start.11
  22.1 0.2 collective-permute-start.9
  22.3 0.3 collective-permute-start.8
  22.6 0.2 shard_map.157
  22.8 1.0 %collective-permute-done.8.theirs_ref = f32[16,640]{1,0:T(8,128)S(1)} collective-permute-done((f32[16,640]{1,0:T(8,128)S(1)}, f32[16,640]{1,0:T(8,128)S(1)}, u32[]{:S(2)}, u32[]{:S(2)}) %collective-permute-start.8) | collective-permute-done | bytes 40992 | tf_op jit(solution)/shard_map/ppermute | solution.py:469
  23.8 0.0 collective-permute-done.9.small_other_ref
  23.8 0.9 %shard_map.158.attended_ref = bf16[16,512]{1,0:T(8,128)(2,1)S(1)} custom-call(f32[16,640]{1,0:T(8,128)S(1)} %get-tuple-element.63.mine_ref, f32[16,640]{1,0:T(8,128)S(1)} %collective-permute-done.8.theirs_ref, bf16[64,640]{1,0:T(8,128)(2,1)S(1)} %get-tuple-element.65.small_ref, bf16[64,640]{1,0:T(8,128)(2,1)S(1)} %collective-permute-done.9.small_other_ref, ...), custom_call_target="tpu_custom_call" | custom-call | tf_op jit(solution)/shard_map/pallas_call | solution.py:347
  24.7 0.0 copy-start.2
  24.7 0.0 copy-start.3
  24.7 0.0 collective-permute-done.11.up_other_ref
  24.8 0.0 collective-permute-done.10.wo_other_ref
  24.8 1.8 %shard_map.159 = (bf16[8,4096]{1,0:T(8,128)(2,1)S(1)}, bf16[8,4096]{1,0:T(8,128)(2,1)S(1)}, bf16[8,4096]{1,0:T(8,128)(2,1)S(1)}, bf16[8,4096]{1,0:T(8,128)(2,1)S(1)}) custom-call(bf16[16,512]{1,0:T(8,128)(2,1)S(1)} %shard_map.158.attended_ref, bf16[256,8192]{1,0:T(8,128)(2,1)S(1)} %copy-done, bf16[256,8192]{1,0:T(8,128)(2,1)S(1)} %collective-permute-done.10.wo_other_ref, ...), custom_call_target="tpu_custom_call" | custom-call | tf_op jit(solution)/shard_map/pallas_call | solution.py:347
  26.6 3.3 %collective-permute-start.12 = (bf16[8,4096]{1,0:T(8,128)(2,1)S(1)}, bf16[8,4096]{1,0:T(8,128)(2,1)S(1)}, u32[]{:S(2)}, u32[]{:S(2)}) collective-permute-start(bf16[8,4096]{1,0:T(8,128)(2,1)S(1)} %get-tuple-element.73), channel_id=1, source_target_pairs={{6,0},{9,1},{8,2},{11,3},{10,4},{13,5},{12,6},{15,7},{14,8},{1,9},... | collective-permute-start | bytes 196616 | tf_op jit(solution)/shard_map/ppermute | solution.py:485
  29.9 1.5 %collective-permute-start.13 = (bf16[8,4096]{1,0:T(8,128)(2,1)S(1)}, bf16[8,4096]{1,0:T(8,128)(2,1)S(1)}, u32[]{:S(2)}, u32[]{:S(2)}) collective-permute-start(bf16[8,4096]{1,0:T(8,128)(2,1)S(1)} %get-tuple-element.74), channel_id=1, source_target_pairs={{4,0},{11,1},{6,2},{13,3},{8,4},{15,5},{10,6},{1,7},{12,8},{3,9},{... | collective-permute-start | bytes 196616 | tf_op jit(solution)/shard_map/ppermute | solution.py:485
  31.4 1.9 %collective-permute-start.14 = (bf16[8,4096]{1,0:T(8,128)(2,1)S(1)}, bf16[8,4096]{1,0:T(8,128)(2,1)S(1)}, u32[]{:S(2)}, u32[]{:S(2)}) collective-permute-start(bf16[8,4096]{1,0:T(8,128)(2,1)S(1)} %get-tuple-element.75), channel_id=1, source_target_pairs={{2,0},{13,1},{4,2},{15,3},{6,4},{1,5},{8,6},{3,7},{10,8},{5,9},{12... | collective-permute-start | bytes 196616 | tf_op jit(solution)/shard_map/ppermute | solution.py:485
  33.3 0.7 %collective-permute-start.15 = (bf16[8,4096]{1,0:T(8,128)(2,1)S(1)}, bf16[8,4096]{1,0:T(8,128)(2,1)S(1)}, u32[]{:S(2)}, u32[]{:S(2)}) collective-permute-start(bf16[8,4096]{1,0:T(8,128)(2,1)S(1)} %get-tuple-element.76), channel_id=1, source_target_pairs={{0,0},{15,1},{2,2},{1,3},{4,4},{3,5},{6,6},{5,7},{8,8},{7,9},{10,1... | collective-permute-start | bytes 196616 | tf_op jit(solution)/shard_map/ppermute | solution.py:485
  34.0 0.0 collective-permute-done.12.refs_0_
  34.0 0.2 collective-permute-start.16
  34.3 1.4 %collective-permute-done.13.refs_1_ = bf16[8,4096]{1,0:T(8,128)(2,1)S(1)} collective-permute-done((bf16[8,4096]{1,0:T(8,128)(2,1)S(1)}, bf16[8,4096]{1,0:T(8,128)(2,1)S(1)}, u32[]{:S(2)}, u32[]{:S(2)}) %collective-permute-start.13) | collective-permute-done | bytes 65568 | tf_op jit(solution)/shard_map/ppermute | solution.py:485
  35.6 0.4 collective-permute-start.17
  36.0 0.8 %collective-permute-done.14.refs_2_ = bf16[8,4096]{1,0:T(8,128)(2,1)S(1)} collective-permute-done((bf16[8,4096]{1,0:T(8,128)(2,1)S(1)}, bf16[8,4096]{1,0:T(8,128)(2,1)S(1)}, u32[]{:S(2)}, u32[]{:S(2)}) %collective-permute-start.14) | collective-permute-done | bytes 65568 | tf_op jit(solution)/shard_map/ppermute | solution.py:485
  36.8 0.1 collective-permute-start.18
  36.9 0.0 collective-permute-done.15.refs_3_
  36.9 2.7 %collective-permute-start.19 = (bf16[8,4096]{1,0:T(8,128)(2,1)S(1)}, bf16[8,4096]{1,0:T(8,128)(2,1)S(1)}, u32[]{:S(2)}, u32[]{:S(2)}) collective-permute-start(bf16[8,4096]{1,0:T(8,128)(2,1)S(1)} %collective-permute-done.15.refs_3_), channel_id=1, source_target_pairs={{0,1},{1,0},{2,3},{3,2},{4,5},{5,4},{6,7},{7,6},{8,9},{9,8},{10,11... | collective-permute-start | bytes 196616 | tf_op jit(solution)/shard_map/ppermute | solution.py:488
  39.6 0.0 collective-permute-done.16.refs_4_
  39.6 0.0 collective-permute-done.17.refs_5_
  39.6 0.9 %collective-permute-done.19.refs_7_ = bf16[8,4096]{1,0:T(8,128)(2,1)S(1)} collective-permute-done((bf16[8,4096]{1,0:T(8,128)(2,1)S(1)}, bf16[8,4096]{1,0:T(8,128)(2,1)S(1)}, u32[]{:S(2)}, u32[]{:S(2)}) %collective-permute-start.19) | collective-permute-done | bytes 65568 | tf_op jit(solution)/shard_map/ppermute | solution.py:488
  40.5 1.1 %shard_map.160 = bf16[16,4096]{1,0:T(8,128)(2,1)} custom-call(bf16[8,4096]{1,0:T(8,128)(2,1)S(1)} %collective-permute-done.12.refs_0_, bf16[8,4096]{1,0:T(8,128)(2,1)S(1)} %collective-permute-done.13.refs_1_, bf16[8,4096]{1,0:T(8,128)(2,1)S(1)} %collective-permute-done.14.refs_2_, bf16[8,4096]{1,0:T(8,128)(2,1)S(1)} %collective-permute-done.15.refs_3_, ...), custom_call_target="tpu_custom_call" | custom-call | tf_op jit(solution)/shard_map/pallas_call | solution.py:347
  (7 shorter events, 0.0 us)
Async XLA Ops:
  1.9 22.8 %collective-permute-start.10 = (bf16[256,8192]{1,0:T(8,128)(2,1)}, bf16[256,8192]{1,0:T(8,128)(2,1)S(1)}, u32[]{:S(2)}, u32[]{:S(2)}) collective-permute-start(bf16[256,8192]{1,0:T(8,128)(2,1)} %wo_ref), channel_id=1, source_target_pairs={{0,1},{1,0},{2,3},{3,2},{4,5},{5,4},{6,7},{7,6},{8,9},{9,8},{10,11... | collective-permute-start | bytes 12582920 | tf_op jit(solution)/shard_map/ppermute | solution.py:458
  2.5 13.5 %collective-permute-start = (bf16[8,8320]{1,0:T(8,128)(2,1)S(1)}, bf16[8,8320]{1,0:T(8,128)(2,1)S(1)}, u32[]{:S(2)}, u32[]{:S(2)}) collective-permute-start(bf16[8,8320]{1,0:T(8,128)(2,1)S(1)} %get-tuple-element.45), channel_id=1, source_target_pairs={{0,6},{1,9},{2,8},{3,11},{4,10},{5,13},{6,12},{7,15},{8,14},{9,1},... | collective-permute-start | bytes 399368 | tf_op jit(solution)/shard_map/ppermute | solution.py:454
  6.0 10.1 %collective-permute-start.1 = (bf16[8,8320]{1,0:T(8,128)(2,1)S(1)}, bf16[8,8320]{1,0:T(8,128)(2,1)S(1)}, u32[]{:S(2)}, u32[]{:S(2)}) collective-permute-start(bf16[8,8320]{1,0:T(8,128)(2,1)S(1)} %get-tuple-element.54), channel_id=1, source_target_pairs={{0,4},{1,11},{2,6},{3,13},{4,8},{5,15},{6,10},{7,1},{8,12},{9,3},{... | collective-permute-start | bytes 399368 | tf_op jit(solution)/shard_map/ppermute | solution.py:454
  7.6 10.5 %collective-permute-start.2 = (bf16[8,8320]{1,0:T(8,128)(2,1)S(1)}, bf16[8,8320]{1,0:T(8,128)(2,1)S(1)}, u32[]{:S(2)}, u32[]{:S(2)}) collective-permute-start(bf16[8,8320]{1,0:T(8,128)(2,1)S(1)} %get-tuple-element.55), channel_id=1, source_target_pairs={{0,2},{1,13},{2,4},{3,15},{4,6},{5,1},{6,8},{7,3},{8,10},{9,5},{10... | collective-permute-start | bytes 399368 | tf_op jit(solution)/shard_map/ppermute | solution.py:454
  9.2 8.9 %collective-permute-start.3 = (bf16[8,8320]{1,0:T(8,128)(2,1)S(1)}, bf16[8,8320]{1,0:T(8,128)(2,1)S(1)}, u32[]{:S(2)}, u32[]{:S(2)}) collective-permute-start(bf16[8,8320]{1,0:T(8,128)(2,1)S(1)} %get-tuple-element.56), channel_id=1, source_target_pairs={{0,0},{1,15},{2,2},{3,1},{4,4},{5,3},{6,6},{7,5},{8,8},{9,7},{10,1... | collective-permute-start | bytes 399368 | tf_op jit(solution)/shard_map/ppermute | solution.py:454
  16.0 5.7 %copy-start.1 = (bf16[1,64,4096]{2,1,0:T(8,128)(2,1)S(1)}, bf16[1,64,4096]{2,1,0:T(8,128)(2,1)}, u32[]{:S(2)}) copy-start(bf16[1,64,4096]{2,1,0:T(8,128)(2,1)} %param.31) | copy-start | bytes 1572868
  16.0 8.8 %copy-start = (bf16[256,8192]{1,0:T(8,128)(2,1)S(1)}, bf16[256,8192]{1,0:T(8,128)(2,1)}, u32[]{:S(2)}) copy-start(bf16[256,8192]{1,0:T(8,128)(2,1)} %wo_ref) | copy-start | bytes 12582916
  16.0 2.6 %collective-permute-start.4 = (bf16[8,8320]{1,0:T(8,128)(2,1)S(1)}, bf16[8,8320]{1,0:T(8,128)(2,1)S(1)}, u32[]{:S(2)}, u32[]{:S(2)}) collective-permute-start(bf16[8,8320]{1,0:T(8,128)(2,1)S(1)} %collective-permute-done.refs_0_), channel_id=1, source_target_pairs={{0,1},{1,0},{2,3},{3,2},{4,5},{5,4},{6,7},{7,6},{8,9},{9,8},{10,11... | collective-permute-start | bytes 399368 | tf_op jit(solution)/shard_map/ppermute | solution.py:457
  16.2 2.4 %collective-permute-start.5 = (bf16[8,8320]{1,0:T(8,128)(2,1)S(1)}, bf16[8,8320]{1,0:T(8,128)(2,1)S(1)}, u32[]{:S(2)}, u32[]{:S(2)}) collective-permute-start(bf16[8,8320]{1,0:T(8,128)(2,1)S(1)} %collective-permute-done.1.refs_1_), channel_id=1, source_target_pairs={{0,1},{1,0},{2,3},{3,2},{4,5},{5,4},{6,7},{7,6},{8,9},{9,8},{10,11... | collective-permute-start | bytes 399368 | tf_op jit(solution)/shard_map/ppermute | solution.py:457
  18.1 1.4 %collective-permute-start.6 = (bf16[8,8320]{1,0:T(8,128)(2,1)S(1)}, bf16[8,8320]{1,0:T(8,128)(2,1)S(1)}, u32[]{:S(2)}, u32[]{:S(2)}) collective-permute-start(bf16[8,8320]{1,0:T(8,128)(2,1)S(1)} %collective-permute-done.2.refs_2_), channel_id=1, source_target_pairs={{0,1},{1,0},{2,3},{3,2},{4,5},{5,4},{6,7},{7,6},{8,9},{9,8},{10,11... | collective-permute-start | bytes 399368 | tf_op jit(solution)/shard_map/ppermute | solution.py:457
  18.1 1.5 %collective-permute-start.7 = (bf16[8,8320]{1,0:T(8,128)(2,1)S(1)}, bf16[8,8320]{1,0:T(8,128)(2,1)S(1)}, u32[]{:S(2)}, u32[]{:S(2)}) collective-permute-start(bf16[8,8320]{1,0:T(8,128)(2,1)S(1)} %collective-permute-done.3.refs_3_), channel_id=1, source_target_pairs={{0,1},{1,0},{2,3},{3,2},{4,5},{5,4},{6,7},{7,6},{8,9},{9,8},{10,11... | collective-permute-start | bytes 399368 | tf_op jit(solution)/shard_map/ppermute | solution.py:457
  21.7 3.1 %collective-permute-start.11 = (bf16[64,4096]{1,0:T(8,128)(2,1)S(1)}, bf16[64,4096]{1,0:T(8,128)(2,1)S(1)}, u32[]{:S(2)}, u32[]{:S(2)}) collective-permute-start(bf16[64,4096]{1,0:T(8,128)(2,1)S(1)} %bitcast.17), channel_id=1, source_target_pairs={{0,1},{1,0},{2,3},{3,2},{4,5},{5,4},{6,7},{7,6},{8,9},{9,8},{10,11... | collective-permute-start | bytes 1572872 | tf_op jit(solution)/shard_map/ppermute | solution.py:471
  22.1 1.8 %collective-permute-start.9 = (bf16[64,640]{1,0:T(8,128)(2,1)S(1)}, bf16[64,640]{1,0:T(8,128)(2,1)S(1)}, u32[]{:S(2)}, u32[]{:S(2)}) collective-permute-start(bf16[64,640]{1,0:T(8,128)(2,1)S(1)} %get-tuple-element.65.small_ref), channel_id=1, source_target_pairs={{0,1},{1,0},{2,3},{3,2},{4,5},{5,4},{6,7},{7,6},{8,9},{9,8},{10,11... | collective-permute-start | bytes 245768 | tf_op jit(solution)/shard_map/ppermute | solution.py:470
  22.3 1.6 %collective-permute-start.8 = (f32[16,640]{1,0:T(8,128)S(1)}, f32[16,640]{1,0:T(8,128)S(1)}, u32[]{:S(2)}, u32[]{:S(2)}) collective-permute-start(f32[16,640]{1,0:T(8,128)S(1)} %get-tuple-element.64), channel_id=1, source_target_pairs={{0,1},{1,0},{2,3},{3,2},{4,5},{5,4},{6,7},{7,6},{8,9},{9,8},{10,11... | collective-permute-start | bytes 122888 | tf_op jit(solution)/shard_map/ppermute | solution.py:469
  24.7 15.7 %copy-start.2 = (s32[16,1]{0,1:T(1,128)S(1)}, s32[16,1]{0,1:T(1,128)}, u32[]{:S(2)}) copy-start(s32[16,1]{0,1:T(1,128)} %param.24) | copy-start | bytes 196
  24.7 15.7 %copy-start.3 = (s32[8]{0:T(128)S(1)}, s32[8]{0:T(128)}, u32[]{:S(2)}) copy-start(s32[8]{0:T(128)} %param.25) | copy-start | bytes 100
  26.6 7.5 %collective-permute-start.12 = (bf16[8,4096]{1,0:T(8,128)(2,1)S(1)}, bf16[8,4096]{1,0:T(8,128)(2,1)S(1)}, u32[]{:S(2)}, u32[]{:S(2)}) collective-permute-start(bf16[8,4096]{1,0:T(8,128)(2,1)S(1)} %get-tuple-element.73), channel_id=1, source_target_pairs={{6,0},{9,1},{8,2},{11,3},{10,4},{13,5},{12,6},{15,7},{14,8},{1,9},... | collective-permute-start | bytes 196616 | tf_op jit(solution)/shard_map/ppermute | solution.py:485
  29.9 5.7 %collective-permute-start.13 = (bf16[8,4096]{1,0:T(8,128)(2,1)S(1)}, bf16[8,4096]{1,0:T(8,128)(2,1)S(1)}, u32[]{:S(2)}, u32[]{:S(2)}) collective-permute-start(bf16[8,4096]{1,0:T(8,128)(2,1)S(1)} %get-tuple-element.74), channel_id=1, source_target_pairs={{4,0},{11,1},{6,2},{13,3},{8,4},{15,5},{10,6},{1,7},{12,8},{3,9},{... | collective-permute-start | bytes 196616 | tf_op jit(solution)/shard_map/ppermute | solution.py:485
  31.4 5.4 %collective-permute-start.14 = (bf16[8,4096]{1,0:T(8,128)(2,1)S(1)}, bf16[8,4096]{1,0:T(8,128)(2,1)S(1)}, u32[]{:S(2)}, u32[]{:S(2)}) collective-permute-start(bf16[8,4096]{1,0:T(8,128)(2,1)S(1)} %get-tuple-element.75), channel_id=1, source_target_pairs={{2,0},{13,1},{4,2},{15,3},{6,4},{1,5},{8,6},{3,7},{10,8},{5,9},{12... | collective-permute-start | bytes 196616 | tf_op jit(solution)/shard_map/ppermute | solution.py:485
  33.3 3.5 %collective-permute-start.15 = (bf16[8,4096]{1,0:T(8,128)(2,1)S(1)}, bf16[8,4096]{1,0:T(8,128)(2,1)S(1)}, u32[]{:S(2)}, u32[]{:S(2)}) collective-permute-start(bf16[8,4096]{1,0:T(8,128)(2,1)S(1)} %get-tuple-element.76), channel_id=1, source_target_pairs={{0,0},{15,1},{2,2},{1,3},{4,4},{3,5},{6,6},{5,7},{8,8},{7,9},{10,1... | collective-permute-start | bytes 196616 | tf_op jit(solution)/shard_map/ppermute | solution.py:485
  34.0 5.5 %collective-permute-start.16 = (bf16[8,4096]{1,0:T(8,128)(2,1)S(1)}, bf16[8,4096]{1,0:T(8,128)(2,1)S(1)}, u32[]{:S(2)}, u32[]{:S(2)}) collective-permute-start(bf16[8,4096]{1,0:T(8,128)(2,1)S(1)} %collective-permute-done.12.refs_0_), channel_id=1, source_target_pairs={{0,1},{1,0},{2,3},{3,2},{4,5},{5,4},{6,7},{7,6},{8,9},{9,8},{10,11... | collective-permute-start | bytes 196616 | tf_op jit(solution)/shard_map/ppermute | solution.py:488
  35.6 4.0 %collective-permute-start.17 = (bf16[8,4096]{1,0:T(8,128)(2,1)S(1)}, bf16[8,4096]{1,0:T(8,128)(2,1)S(1)}, u32[]{:S(2)}, u32[]{:S(2)}) collective-permute-start(bf16[8,4096]{1,0:T(8,128)(2,1)S(1)} %collective-permute-done.13.refs_1_), channel_id=1, source_target_pairs={{0,1},{1,0},{2,3},{3,2},{4,5},{5,4},{6,7},{7,6},{8,9},{9,8},{10,11... | collective-permute-start | bytes 196616 | tf_op jit(solution)/shard_map/ppermute | solution.py:488
  36.8 2.7 %collective-permute-start.18 = (bf16[8,4096]{1,0:T(8,128)(2,1)S(1)}, bf16[8,4096]{1,0:T(8,128)(2,1)S(1)}, u32[]{:S(2)}, u32[]{:S(2)}) collective-permute-start(bf16[8,4096]{1,0:T(8,128)(2,1)S(1)} %collective-permute-done.14.refs_2_), channel_id=1, source_target_pairs={{0,1},{1,0},{2,3},{3,2},{4,5},{5,4},{6,7},{7,6},{8,9},{9,8},{10,11... | collective-permute-start | bytes 196616 | tf_op jit(solution)/shard_map/ppermute | solution.py:488
  36.9 3.6 %collective-permute-start.19 = (bf16[8,4096]{1,0:T(8,128)(2,1)S(1)}, bf16[8,4096]{1,0:T(8,128)(2,1)S(1)}, u32[]{:S(2)}, u32[]{:S(2)}) collective-permute-start(bf16[8,4096]{1,0:T(8,128)(2,1)S(1)} %collective-permute-done.15.refs_3_), channel_id=1, source_target_pairs={{0,1},{1,0},{2,3},{3,2},{4,5},{5,4},{6,7},{7,6},{8,9},{9,8},{10,11... | collective-permute-start | bytes 196616 | tf_op jit(solution)/shard_map/ppermute | solution.py:488

commit v6 on v5

--- a/solution.py
+++ b/solution.py
@@ -66,14 +66,12 @@
     return jnp.where(ahead // count == core, jnp.where(core == 0, count - 1 - ahead, ahead - count), -1)
 
 
-def pack_kernel(capacity, x_hbm, gain_hbm, k_hbm, v_hbm, named_hbm, table_hbm, length_hbm, up_hbm, kv_up_hbm, out_down_hbm, *rest):
-    up_ref, kv_up_ref, out_down_ref = rest[-4:-1]
-    rest = rest[:-4] + rest[-1:]
-    small_ref, x_ref, gain_ref, k_ref, v_ref, named_ref, table_ref, length_ref, flat_ref, spread_ref, sems = rest[-11:]
-    blocks = rest[:-11]
+def pack_kernel(capacity, x_hbm, gain_hbm, k_hbm, v_hbm, named_hbm, table_hbm, length_hbm, *rest):
+    x_ref, gain_ref, k_ref, v_ref, named_ref, table_ref, length_ref, flat_ref, spread_ref, sems = rest[-10:]
+    blocks = rest[:-10]
     count = len(blocks)
     owners = 2 * count
-    named_copy, table_copy, length_copy, x_copy, gain_copy, k_copy, v_copy, *up_copies = copy_all(
+    named_copy, table_copy, length_copy, x_copy, gain_copy, k_copy, v_copy = copy_all(
         [
             (named_hbm, named_ref),
             (table_hbm, table_ref),
@@ -82,9 +80,6 @@
             (gain_hbm, gain_ref),
             (k_hbm, k_ref),
             (v_hbm, v_ref),
-            (up_hbm, up_ref),
-            (kv_up_hbm, kv_up_ref),
-            (out_down_hbm, out_down_ref),
         ],
         sems,
     )
@@ -129,30 +124,38 @@
     placed = nn(put_x, lengths).astype(BF16)
     for j, block in enumerate(blocks):
         block[:, width:] = placed[j * per_block : (j + 1) * per_block]
-    for copy in up_copies:
-        copy.wait()
-    small_ref[...] = jnp.concatenate(
-        [up_ref[...], kv_up_ref[0], kv_up_ref[1], out_down_ref[...]], axis=1
-    )
 
 
 def stacked(blocks, columns):
     return jnp.concatenate([block[:, columns] for block in blocks], axis=0)
 
 
-def stage_kernel(wq_hbm, wk_hbm, wv_hbm, down_hbm, wq_ref, kv_ref, down_ref, sems):
+def stage_kernel(wq_hbm, wk_hbm, wv_hbm, down_hbm, up_hbm, kv_up_hbm, out_down_hbm, out_up_hbm, wq_ref, kv_ref, down_ref, small_ref, up_ref, kv_up_ref, out_down_ref, sems):
     width = wq_hbm.shape[0]
     hcols = wk_hbm.shape[0]
     ranks = down_hbm.shape[0]
     pieces = 4
-    pairs = [(wk_hbm, kv_ref.at[0:hcols, :]), (wv_hbm, kv_ref.at[hcols:, :])]
+    pairs = [
+        (up_hbm, up_ref),
+        (kv_up_hbm, kv_up_ref),
+        (out_down_hbm, out_down_ref),
+        (wk_hbm, kv_ref.at[0:hcols, :]),
+        (wv_hbm, kv_ref.at[hcols:, :]),
+        (out_up_hbm, small_ref.at[:, 0 : out_up_hbm.shape[1]]),
+    ]
     for n in range(pieces):
         rows = pl.ds(n * (width // pieces), width // pieces)
         pairs.append((wq_hbm.at[rows, :], wq_ref.at[rows, :]))
     for n in range(2):
         rows = pl.ds(n * (ranks // 2), ranks // 2)
         pairs.append((down_hbm.at[rows, :], down_ref.at[rows, :]))
-    for copy in copy_all(pairs, sems):
+    copies = copy_all(pairs, sems)
+    for copy in copies[:3]:
+        copy.wait()
+    small_ref[:, out_up_hbm.shape[1] :] = jnp.concatenate(
+        [up_ref[...], kv_up_ref[0], kv_up_ref[1], out_down_ref[...]], axis=1
+    )
+    for copy in copies[3:]:
         copy.wait()
 
 
@@ -181,7 +184,19 @@
 
 def unpack_kernel(count, *refs):
     blocks = refs[:count]
-    k_ref, v_ref, length_ref, cosine_ref, sine_ref = refs[count:]
+    named_ref, table_ref, k_ref, v_ref, length_ref, cosine_ref, sine_ref, place_ref = refs[count:]
+    requests, rows = place_ref.shape
+    core = lax.axis_index("tensor")
+    owner, standing = owner_and_standing(named_ref[...], table_ref[...])
+    ahead = owner - lax.axis_index("adapter")
+    near, far = block_of(ahead, core, count), block_of(ahead, 1 - core, count)
+    back = rows // (2 * count)
+    source = jnp.where(near < 0, count + far, near) * back + core * (back // 2) + standing
+    square = (requests, requests)
+    source = jnp.sum(
+        jnp.where(iota(square, 0) == iota(square, 1), source, 0), axis=1, keepdims=True
+    )
+    place_ref[...] = ones_where(iota((requests, rows), 1) == source)
     slots = length_ref.shape[0]
     per_block = blocks[0].shape[0]
     positions = k_ref.shape[0] // slots
@@ -220,6 +235,7 @@
     heads = 2 * qcols // HEAD_SIZE
     halfway = HEAD_SIZE // 2
     both = qcols + kvcols
+    base = small_ref.shape[1] - both - qcols
     mine = mine_ref[...]
     theirs = theirs_ref[...]
     ranks = (mine + theirs)[:, both : both + 3 * rank].astype(BF16)
@@ -228,9 +244,9 @@
     def added(projected, up_ref):
         change = jnp.concatenate(
             [
-                nn(ranks[0], up_ref[:, :qcols]),
-                nn(ranks[1], up_ref[:, qcols : qcols + halfway]),
-                nn(ranks[2], up_ref[:, qcols + halfway : both]),
+                nn(ranks[0], up_ref[:, base : base + qcols]),
+                nn(ranks[1], up_ref[:, base + qcols : base + qcols + halfway]),
+                nn(ranks[2], up_ref[:, base + qcols + halfway : base + both]),
             ],
             axis=1,
         )
@@ -286,7 +302,7 @@
             ]
 
 
-def output_kernel(count, attended_ref, wo_ref, wo_other_ref, small_ref, small_other_ref, up_ref, up_other_ref, *blocks):
+def output_kernel(count, attended_ref, wo_ref, wo_other_ref, small_ref, small_other_ref, *blocks):
     core = lax.axis_index("tensor")
     slots, cols = attended_ref.shape
     hcols = cols // 2
@@ -308,34 +324,17 @@
             nn(left, wo_ref[:, near]) + nn(right, wo_other_ref[:, near]),
             nn(left, wo_ref[:, far]) + nn(right, wo_other_ref[:, far]),
         )
-        delta = jnp.where(side == core, nn(ranks, up_ref[:, near]), nn(ranks, up_other_ref[:, near]))
+        delta = jnp.where(side == core, nn(ranks, small_ref[:, near]), nn(ranks, small_other_ref[:, near]))
         done = (terms + delta.astype(BF16).astype(F32)).astype(BF16)
         for j, block in enumerate(blocks):
             block[:, near] = done[j * per_block : (j + 1) * per_block]
 
 
-def pick_kernel(count, *refs):
-    blocks = refs[: 2 * count]
-    named_ref, table_ref, out_ref = refs[2 * count :]
-    core = lax.axis_index("tensor")
-    owners = 2 * count
-    per_block, half = blocks[0].shape
-    rows = owners * per_block
-    requests = out_ref.shape[0]
-    owner, standing = owner_and_standing(named_ref[...], table_ref[...])
-    ahead = owner - lax.axis_index("adapter")
-    mine, theirs = block_of(ahead, core, count), block_of(ahead, 1 - core, count)
-    source = jnp.where(mine < 0, count + theirs, mine) * per_block
-    source = source + core * (per_block // 2) + standing
-    place = ones_where(iota((rows, requests), 0) == source)
+def pick_kernel(place_ref, *refs):
+    blocks, out_ref = refs[:-1], refs[-1]
     step = 512
-    for c in range(0, half, step):
-        out_ref[:, c : c + step] = lax.dot_general(
-            place,
-            stacked(blocks, slice(c, c + step)),
-            (((0,), (0,)), ((), ())),
-            preferred_element_type=F32,
-        ).astype(BF16)
+    for c in range(0, out_ref.shape[1], step):
+        out_ref[:, c : c + step] = nn(place_ref[...], stacked(blocks, slice(c, c + step))).astype(BF16)
 
 
 OUTSIDE = pl.BlockSpec(memory_space=pltpu.HBM)
@@ -395,9 +394,9 @@
     rank, qcols = query_adapter_up.shape[1:]
     hcols = key_value_adapter_up.shape[3]
     hrows = output_projection.shape[0]
-    *packed, small = call(
+    packed = call(
         functools.partial(pack_kernel, capacity),
-        [block] * count + [shape((rank, qcols + 2 * hcols + hrows), BF16)],
+        [block] * count,
         [
             pltpu.VMEM((requests, width), BF16),
             pltpu.VMEM((1, width), F32),
@@ -408,12 +407,9 @@
             pltpu.VMEM((1, requests), jnp.int32),
             pltpu.VMEM((2 * requests, width), BF16),
             pltpu.VMEM((positions * requests, LANES), F32),
-            pltpu.VMEM((rank, qcols), BF16),
-            pltpu.VMEM((2, rank, hcols), BF16),
-            pltpu.VMEM((rank, hrows), BF16),
-            pltpu.SemaphoreType.DMA((10,)),
+            pltpu.SemaphoreType.DMA((7,)),
         ],
-        outside=range(10),
+        outside=range(7),
     )(
         layer_input,
         input_norm_gain.reshape(1, width),
@@ -422,9 +418,6 @@
         named,
         table,
         cached_length.reshape(1, requests),
-        query_adapter_up[0],
-        key_value_adapter_up[0],
-        output_adapter_down[0].T,
     )
     down = projection_adapter_down[0].T
     wk, wv = key_projection.T, value_projection.T
@@ -432,17 +425,32 @@
     *packed, query_projection, wk, wv, down, output_projection = lax.optimization_barrier(
         (*packed, query_projection, wk, wv, down, output_projection)
     )
-    weights = call(
+    *weights, small = call(
         stage_kernel,
         [
             shape(query_projection.shape, BF16),
             shape((kvcols, width), BF16),
             shape(down.shape, BF16),
+            shape((rank, half + qcols + 2 * hcols + hrows), BF16),
         ],
-        [pltpu.SemaphoreType.DMA((8,))],
-        outside=range(4),
+        [
+            pltpu.VMEM((rank, qcols), BF16),
+            pltpu.VMEM((2, rank, hcols), BF16),
+            pltpu.VMEM((rank, hrows), BF16),
+            pltpu.SemaphoreType.DMA((12,)),
+        ],
+        outside=range(8),
         moved=2 * (query_projection.size + kvcols * width + down.size),
-    )(query_projection, wk, wv, down)
+    )(
+        query_projection,
+        wk,
+        wv,
+        down,
+        query_adapter_up[0],
+        key_value_adapter_up[0],
+        output_adapter_down[0].T,
+        output_adapter_up[0],
+    )
 
     def onward(n):
         shifts = (count - 1 - n, count + n)
@@ -463,16 +471,15 @@
         [pltpu.VMEM((pcols // LANES, 4 * slots, LANES), F32)],
         vmem=24,
     )(*arrived, *passed, *weights)
-    theirs, mine, small, out_up = lax.optimization_barrier(
-        (theirs, mine, small, output_adapter_up[0])
-    )
+    theirs, mine, small = lax.optimization_barrier((theirs, mine, small))
     theirs = lax.ppermute(theirs, "tensor", SWAP)
     small_other = lax.ppermute(small, "tensor", SWAP)
-    out_up_other = lax.ppermute(out_up, "tensor", SWAP)
-    keys, values, lengths, cosine, sine = call(
+    keys, values, lengths, cosine, sine, place = call(
         functools.partial(unpack_kernel, count),
-        [shape((slots * positions, HEAD_SIZE), BF16)] * 2 + [shape((slots, LANES), F32)] * 3,
-    )(*arrived)
+        [shape((slots * positions, HEAD_SIZE), BF16)] * 2
+        + [shape((slots, LANES), F32)] * 3
+        + [shape((requests, 4 * slots), BF16)],
+    )(*arrived, named, table)
     attended = call(attend_kernel, shape((slots, 2 * qcols), BF16), vmem=16)(
         mine, theirs, small, small_other, keys, values, lengths, cosine, sine
     )
@@ -480,15 +487,13 @@
         functools.partial(output_kernel, count),
         [shape((2 * kept, half), BF16)] * count,
         vmem=16,
-    )(attended, output_projection, wo_other, small, small_other, out_up, out_up_other)
+    )(attended, output_projection, wo_other, small, small_other)
     returned = [
         lax.ppermute(one, ("adapter", "tensor"), [(b, a) for a, b in onward(n)])
         for n, one in enumerate(finished)
     ]
     returned += [lax.ppermute(one, "tensor", SWAP) for one in returned]
-    return call(functools.partial(pick_kernel, count), shape((requests, half), BF16))(
-        *returned, named, table
-    )
+    return call(pick_kernel, shape((requests, half), BF16))(place, *returned)
 
 
 def solution(mesh):

time: 41.7 us -> 41.3 us (level)
  transfers between devices with their start and end apart: 20 -> 19, of which waited for: 8 -> 8; matrix products, arithmetic and copies ran while one was open for 0% -> 0% of each run, Pallas kernels for 16% -> 16%
where the time goes in v6:
time: 41.3 us; the launch traced here: 41.1 us
  starting transfers between devices  20.3 us (49%)
  Pallas kernels  11.2 us (27%)
  waiting for transfers between devices  9.54 us (23%)
    pallas_call x7, Pallas kernels, call(): pl.pallas_call(kernel, out_shape=outs, in_specs=[OUTSIDE if i in outside...  11.2 us
    ppermute x4, starting transfers between devices, body(): lax.ppermute(one, ('adapter', 'tensor'), [(b, a) for a, b in onward(n)])  7.45 us
    ppermute x4, starting transfers between devices, body(): lax.ppermute(one, ('adapter', 'tensor'), onward(n))  7.35 us
    ppermute x4, waiting for transfers between devices, body(): lax.ppermute(one, ('adapter', 'tensor'), onward(n))  4.15 us
    ppermute x4, starting transfers between devices, body(): returned += [lax.ppermute(one, 'tensor', SWAP) for one in returned]  3.37 us
    ppermute x4, waiting for transfers between devices, body(): lax.ppermute(one, ('adapter', 'tensor'), [(b, a) for a, b in onward(n)])  2.17 us
    ppermute x1, waiting for transfers between devices, body(): theirs = lax.ppermute(theirs, 'tensor', SWAP)  1.29 us
    ppermute x4, starting transfers between devices, body(): passed = [lax.ppermute(one, 'tensor', SWAP) for one in arrived]  1.03 us
  transfers between devices with their start and end apart: 19, of which 8 were waited for; matrix products, arithmetic and copies ran while one was open for 0% of the time, Pallas kernels for 16%

profile of v6, /device:TPU:0, one launch (start us, length us, event | category | flops | bytes accessed | tf_op | source)
XLA Modules:
  0.0 41.1 jit_solution(16475265608331683298)
XLA Ops:
  0.0 1.8 %shard_map.154 = (bf16[8,8320]{1,0:T(8,128)(2,1)S(1)}, bf16[8,8320]{1,0:T(8,128)(2,1)S(1)}, bf16[8,8320]{1,0:T(8,128)(2,1)S(1)}, bf16[8,8320]{1,0:T(8,128)(2,1)S(1)}) custom-call(bf16[16,8192]{1,0:T(8,128)(2,1)} %x_hbm.1, f32[1,8192]{1,0:T(1,128)} %bitcast.30, bf16[512,128]{1,0:T(8,128)(2,1)} %bitcast.25, bf16[512,128]{1,0:T(8,128)(2,1)} %bitcast.26, ...), custom_call_target="tpu_custom_call" | custom-call | tf_op jit(solution)/shard_map/pallas_call | solution.py:346
  1.8 0.5 %collective-permute-start.10 = (bf16[256,8192]{1,0:T(8,128)(2,1)}, bf16[256,8192]{1,0:T(8,128)(2,1)S(1)}, u32[]{:S(2)}, u32[]{:S(2)}) collective-permute-start(bf16[256,8192]{1,0:T(8,128)(2,1)} %wo_ref), channel_id=1, source_target_pairs={{0,1},{1,0},{2,3},{3,2},{4,5},{5,4},{6,7},{7,6},{8,9},{9,8},{10,11... | collective-permute-start | bytes 12582920 | tf_op jit(solution)/shard_map/ppermute | solution.py:466
  2.4 3.6 %collective-permute-start = (bf16[8,8320]{1,0:T(8,128)(2,1)S(1)}, bf16[8,8320]{1,0:T(8,128)(2,1)S(1)}, u32[]{:S(2)}, u32[]{:S(2)}) collective-permute-start(bf16[8,8320]{1,0:T(8,128)(2,1)S(1)} %get-tuple-element.45), channel_id=1, source_target_pairs={{0,6},{1,9},{2,8},{3,11},{4,10},{5,13},{6,12},{7,15},{8,14},{9,1},... | collective-permute-start | bytes 399368 | tf_op jit(solution)/shard_map/ppermute | solution.py:462
  5.9 1.6 %collective-permute-start.1 = (bf16[8,8320]{1,0:T(8,128)(2,1)S(1)}, bf16[8,8320]{1,0:T(8,128)(2,1)S(1)}, u32[]{:S(2)}, u32[]{:S(2)}) collective-permute-start(bf16[8,8320]{1,0:T(8,128)(2,1)S(1)} %get-tuple-element.54), channel_id=1, source_target_pairs={{0,4},{1,11},{2,6},{3,13},{4,8},{5,15},{6,10},{7,1},{8,12},{9,3},{... | collective-permute-start | bytes 399368 | tf_op jit(solution)/shard_map/ppermute | solution.py:462
  7.5 1.5 %collective-permute-start.2 = (bf16[8,8320]{1,0:T(8,128)(2,1)S(1)}, bf16[8,8320]{1,0:T(8,128)(2,1)S(1)}, u32[]{:S(2)}, u32[]{:S(2)}) collective-permute-start(bf16[8,8320]{1,0:T(8,128)(2,1)S(1)} %get-tuple-element.55), channel_id=1, source_target_pairs={{0,2},{1,13},{2,4},{3,15},{4,6},{5,1},{6,8},{7,3},{8,10},{9,5},{10... | collective-permute-start | bytes 399368 | tf_op jit(solution)/shard_map/ppermute | solution.py:462
  9.1 0.7 %collective-permute-start.3 = (bf16[8,8320]{1,0:T(8,128)(2,1)S(1)}, bf16[8,8320]{1,0:T(8,128)(2,1)S(1)}, u32[]{:S(2)}, u32[]{:S(2)}) collective-permute-start(bf16[8,8320]{1,0:T(8,128)(2,1)S(1)} %get-tuple-element.56), channel_id=1, source_target_pairs={{0,0},{1,15},{2,2},{3,1},{4,4},{5,3},{6,6},{7,5},{8,8},{9,7},{10,1... | collective-permute-start | bytes 399368 | tf_op jit(solution)/shard_map/ppermute | solution.py:462
  9.7 3.5 %shard_map.155 = (bf16[8192,256]{1,0:T(8,128)(2,1)S(1)}, bf16[128,8192]{1,0:T(8,128)(2,1)S(1)}, bf16[192,4096]{1,0:T(8,128)(2,1)S(1)}, bf16[64,4736]{1,0:T(8,128)(2,1)S(1)}) custom-call(bf16[8192,256]{1,0:T(8,128)(2,1)} %wq_hbm, bf16[64,8192]{1,0:T(8,128)(2,1)} %bitcast.22, bf16[64,8192]{1,0:T(8,128)(2,1)} %bitcast.23, bf16[192,4096]{1,0:T(8,128)(2,1)} %bitcast.21, ...), custom_call_target="tpu_custom_call" | custom-call | bytes 7864320 | tf_op jit(solution)/shard_map/pallas_call | solution.py:346
  13.3 2.6 %collective-permute-done.refs_0_ = bf16[8,8320]{1,0:T(8,128)(2,1)S(1)} collective-permute-done((bf16[8,8320]{1,0:T(8,128)(2,1)S(1)}, bf16[8,8320]{1,0:T(8,128)(2,1)S(1)}, u32[]{:S(2)}, u32[]{:S(2)}) %collective-permute-start) | collective-permute-done | bytes 133152 | tf_op jit(solution)/shard_map/ppermute | solution.py:462
  15.9 0.4 %collective-permute-start.4 = (bf16[8,8320]{1,0:T(8,128)(2,1)S(1)}, bf16[8,8320]{1,0:T(8,128)(2,1)S(1)}, u32[]{:S(2)}, u32[]{:S(2)}) collective-permute-start(bf16[8,8320]{1,0:T(8,128)(2,1)S(1)} %collective-permute-done.refs_0_), channel_id=1, source_target_pairs={{0,1},{1,0},{2,3},{3,2},{4,5},{5,4},{6,7},{7,6},{8,9},{9,8},{10,11... | collective-permute-start | bytes 399368 | tf_op jit(solution)/shard_map/ppermute | solution.py:465
  16.3 0.0 collective-permute-done.1.refs_1_
  16.3 0.1 collective-permute-start.5
  16.4 1.6 %collective-permute-done.2.refs_2_ = bf16[8,8320]{1,0:T(8,128)(2,1)S(1)} collective-permute-done((bf16[8,8320]{1,0:T(8,128)(2,1)S(1)}, bf16[8,8320]{1,0:T(8,128)(2,1)S(1)}, u32[]{:S(2)}, u32[]{:S(2)}) %collective-permute-start.2) | collective-permute-done | bytes 133152 | tf_op jit(solution)/shard_map/ppermute | solution.py:462
  18.0 0.0 collective-permute-start.6
  18.0 0.0 collective-permute-done.3.refs_3_
  18.0 0.5 %collective-permute-start.7 = (bf16[8,8320]{1,0:T(8,128)(2,1)S(1)}, bf16[8,8320]{1,0:T(8,128)(2,1)S(1)}, u32[]{:S(2)}, u32[]{:S(2)}) collective-permute-start(bf16[8,8320]{1,0:T(8,128)(2,1)S(1)} %collective-permute-done.3.refs_3_), channel_id=1, source_target_pairs={{0,1},{1,0},{2,3},{3,2},{4,5},{5,4},{6,7},{7,6},{8,9},{9,8},{10,11... | collective-permute-start | bytes 399368 | tf_op jit(solution)/shard_map/ppermute | solution.py:465
  18.5 0.0 collective-permute-done.4.refs_4_
  18.5 0.0 collective-permute-done.5.refs_5_
  18.5 0.8 %collective-permute-done.6.refs_6_ = bf16[8,8320]{1,0:T(8,128)(2,1)S(1)} collective-permute-done((bf16[8,8320]{1,0:T(8,128)(2,1)S(1)}, bf16[8,8320]{1,0:T(8,128)(2,1)S(1)}, u32[]{:S(2)}, u32[]{:S(2)}) %collective-permute-start.6) | collective-permute-done | bytes 133152 | tf_op jit(solution)/shard_map/ppermute | solution.py:465
  19.3 0.2 collective-permute-done.7.refs_7_
  19.5 2.1 %shard_map.157 = (f32[16,640]{1,0:T(8,128)S(1)}, f32[16,640]{1,0:T(8,128)S(1)}) custom-call(bf16[8,8320]{1,0:T(8,128)(2,1)S(1)} %collective-permute-done.refs_0_, bf16[8,8320]{1,0:T(8,128)(2,1)S(1)} %collective-permute-done.1.refs_1_, bf16[8,8320]{1,0:T(8,128)(2,1)S(1)} %collective-permute-done.2.refs_2_, ...), custom_call_target="tpu_custom_call" | custom-call | tf_op jit(solution)/shard_map/pallas_call | solution.py:346
  21.6 0.4 collective-permute-start.9
  22.0 0.2 collective-permute-start.8
  22.1 0.0 copy-done.1
  22.1 0.0 copy-done.2
  22.1 0.3 shard_map.156
  22.4 1.3 %collective-permute-done.8.theirs_ref = f32[16,640]{1,0:T(8,128)S(1)} collective-permute-done((f32[16,640]{1,0:T(8,128)S(1)}, f32[16,640]{1,0:T(8,128)S(1)}, u32[]{:S(2)}, u32[]{:S(2)}) %collective-permute-start.8) | collective-permute-done | bytes 40992 | tf_op jit(solution)/shard_map/ppermute | solution.py:475
  23.7 0.0 collective-permute-done.9.small_other_ref
  23.7 0.9 %shard_map.158.attended_ref = bf16[16,512]{1,0:T(8,128)(2,1)S(1)} custom-call(f32[16,640]{1,0:T(8,128)S(1)} %get-tuple-element.64.mine_ref, f32[16,640]{1,0:T(8,128)S(1)} %collective-permute-done.8.theirs_ref, bf16[64,4736]{1,0:T(8,128)(2,1)S(1)} %get-tuple-element.66.small_ref, bf16[64,4736]{1,0:T(8,128)(2,1)S(1)} %collective-permute-done.9.small_other_ref, ...), custom_call_target="tpu_custom_call" | custom-call | tf_op jit(solution)/shard_map/pallas_call | solution.py:346
  24.6 0.0 collective-permute-done.10.wo_other_ref
  24.6 0.0 copy-done
  24.6 1.7 %shard_map.159 = (bf16[8,4096]{1,0:T(8,128)(2,1)S(1)}, bf16[8,4096]{1,0:T(8,128)(2,1)S(1)}, bf16[8,4096]{1,0:T(8,128)(2,1)S(1)}, bf16[8,4096]{1,0:T(8,128)(2,1)S(1)}) custom-call(bf16[16,512]{1,0:T(8,128)(2,1)S(1)} %shard_map.158.attended_ref, bf16[256,8192]{1,0:T(8,128)(2,1)S(1)} %copy-done, bf16[256,8192]{1,0:T(8,128)(2,1)S(1)} %collective-permute-done.10.wo_other_ref, ...), custom_call_target="tpu_custom_call" | custom-call | tf_op jit(solution)/shard_map/pallas_call | solution.py:346
  26.4 3.3 %collective-permute-start.11 = (bf16[8,4096]{1,0:T(8,128)(2,1)S(1)}, bf16[8,4096]{1,0:T(8,128)(2,1)S(1)}, u32[]{:S(2)}, u32[]{:S(2)}) collective-permute-start(bf16[8,4096]{1,0:T(8,128)(2,1)S(1)} %get-tuple-element.73), channel_id=1, source_target_pairs={{6,0},{9,1},{8,2},{11,3},{10,4},{13,5},{12,6},{15,7},{14,8},{1,9},... | collective-permute-start | bytes 196616 | tf_op jit(solution)/shard_map/ppermute | solution.py:492
  29.7 1.5 %collective-permute-start.12 = (bf16[8,4096]{1,0:T(8,128)(2,1)S(1)}, bf16[8,4096]{1,0:T(8,128)(2,1)S(1)}, u32[]{:S(2)}, u32[]{:S(2)}) collective-permute-start(bf16[8,4096]{1,0:T(8,128)(2,1)S(1)} %get-tuple-element.74), channel_id=1, source_target_pairs={{4,0},{11,1},{6,2},{13,3},{8,4},{15,5},{10,6},{1,7},{12,8},{3,9},{... | collective-permute-start | bytes 196616 | tf_op jit(solution)/shard_map/ppermute | solution.py:492
  31.2 1.9 %collective-permute-start.13 = (bf16[8,4096]{1,0:T(8,128)(2,1)S(1)}, bf16[8,4096]{1,0:T(8,128)(2,1)S(1)}, u32[]{:S(2)}, u32[]{:S(2)}) collective-permute-start(bf16[8,4096]{1,0:T(8,128)(2,1)S(1)} %get-tuple-element.75), channel_id=1, source_target_pairs={{2,0},{13,1},{4,2},{15,3},{6,4},{1,5},{8,6},{3,7},{10,8},{5,9},{12... | collective-permute-start | bytes 196616 | tf_op jit(solution)/shard_map/ppermute | solution.py:492
  33.2 0.7 %collective-permute-start.14 = (bf16[8,4096]{1,0:T(8,128)(2,1)S(1)}, bf16[8,4096]{1,0:T(8,128)(2,1)S(1)}, u32[]{:S(2)}, u32[]{:S(2)}) collective-permute-start(bf16[8,4096]{1,0:T(8,128)(2,1)S(1)} %get-tuple-element.76), channel_id=1, source_target_pairs={{0,0},{15,1},{2,2},{1,3},{4,4},{3,5},{6,6},{5,7},{8,8},{7,9},{10,1... | collective-permute-start | bytes 196616 | tf_op jit(solution)/shard_map/ppermute | solution.py:492
  33.8 0.0 collective-permute-done.11.refs_0_
  33.8 0.2 collective-permute-start.15
  34.1 1.4 %collective-permute-done.12.refs_1_ = bf16[8,4096]{1,0:T(8,128)(2,1)S(1)} collective-permute-done((bf16[8,4096]{1,0:T(8,128)(2,1)S(1)}, bf16[8,4096]{1,0:T(8,128)(2,1)S(1)}, u32[]{:S(2)}, u32[]{:S(2)}) %collective-permute-start.12) | collective-permute-done | bytes 65568 | tf_op jit(solution)/shard_map/ppermute | solution.py:492
  35.4 0.4 collective-permute-start.16
  35.8 0.8 %collective-permute-done.13.refs_2_ = bf16[8,4096]{1,0:T(8,128)(2,1)S(1)} collective-permute-done((bf16[8,4096]{1,0:T(8,128)(2,1)S(1)}, bf16[8,4096]{1,0:T(8,128)(2,1)S(1)}, u32[]{:S(2)}, u32[]{:S(2)}) %collective-permute-start.13) | collective-permute-done | bytes 65568 | tf_op jit(solution)/shard_map/ppermute | solution.py:492
  36.6 0.1 collective-permute-start.17
  36.7 0.0 collective-permute-done.14.refs_3_
  36.7 2.7 %collective-permute-start.18 = (bf16[8,4096]{1,0:T(8,128)(2,1)S(1)}, bf16[8,4096]{1,0:T(8,128)(2,1)S(1)}, u32[]{:S(2)}, u32[]{:S(2)}) collective-permute-start(bf16[8,4096]{1,0:T(8,128)(2,1)S(1)} %collective-permute-done.14.refs_3_), channel_id=1, source_target_pairs={{0,1},{1,0},{2,3},{3,2},{4,5},{5,4},{6,7},{7,6},{8,9},{9,8},{10,11... | collective-permute-start | bytes 196616 | tf_op jit(solution)/shard_map/ppermute | solution.py:495
  39.4 0.0 collective-permute-done.15.refs_4_
  39.4 0.0 collective-permute-done.16.refs_5_
  39.4 0.0 collective-permute-done.17.refs_6_
  39.4 0.9 %collective-permute-done.18.refs_7_ = bf16[8,4096]{1,0:T(8,128)(2,1)S(1)} collective-permute-done((bf16[8,4096]{1,0:T(8,128)(2,1)S(1)}, bf16[8,4096]{1,0:T(8,128)(2,1)S(1)}, u32[]{:S(2)}, u32[]{:S(2)}) %collective-permute-start.18) | collective-permute-done | bytes 65568 | tf_op jit(solution)/shard_map/ppermute | solution.py:495
  40.3 0.8 %shard_map.160 = bf16[16,4096]{1,0:T(8,128)(2,1)} custom-call(bf16[16,64]{1,0:T(8,128)(2,1)S(1)} %get-tuple-element.57.place_ref, bf16[8,4096]{1,0:T(8,128)(2,1)S(1)} %collective-permute-done.11.refs_0_, bf16[8,4096]{1,0:T(8,128)(2,1)S(1)} %collective-permute-done.12.refs_1_, bf16[8,4096]{1,0:T(8,128)(2,1)S(1)} %collective-permute-done.13.refs_2_, ...), custom_call_target="tpu_custom_call" | custom-call | tf_op jit(solution)/shard_map/pallas_call | solution.py:346
  (3 shorter events, 0.0 us)
Async XLA Ops:
  1.8 22.8 %collective-permute-start.10 = (bf16[256,8192]{1,0:T(8,128)(2,1)}, bf16[256,8192]{1,0:T(8,128)(2,1)S(1)}, u32[]{:S(2)}, u32[]{:S(2)}) collective-permute-start(bf16[256,8192]{1,0:T(8,128)(2,1)} %wo_ref), channel_id=1, source_target_pairs={{0,1},{1,0},{2,3},{3,2},{4,5},{5,4},{6,7},{7,6},{8,9},{9,8},{10,11... | collective-permute-start | bytes 12582920 | tf_op jit(solution)/shard_map/ppermute | solution.py:466
  2.4 13.5 %collective-permute-start = (bf16[8,8320]{1,0:T(8,128)(2,1)S(1)}, bf16[8,8320]{1,0:T(8,128)(2,1)S(1)}, u32[]{:S(2)}, u32[]{:S(2)}) collective-permute-start(bf16[8,8320]{1,0:T(8,128)(2,1)S(1)} %get-tuple-element.45), channel_id=1, source_target_pairs={{0,6},{1,9},{2,8},{3,11},{4,10},{5,13},{6,12},{7,15},{8,14},{9,1},... | collective-permute-start | bytes 399368 | tf_op jit(solution)/shard_map/ppermute | solution.py:462
  5.9 10.4 %collective-permute-start.1 = (bf16[8,8320]{1,0:T(8,128)(2,1)S(1)}, bf16[8,8320]{1,0:T(8,128)(2,1)S(1)}, u32[]{:S(2)}, u32[]{:S(2)}) collective-permute-start(bf16[8,8320]{1,0:T(8,128)(2,1)S(1)} %get-tuple-element.54), channel_id=1, source_target_pairs={{0,4},{1,11},{2,6},{3,13},{4,8},{5,15},{6,10},{7,1},{8,12},{9,3},{... | collective-permute-start | bytes 399368 | tf_op jit(solution)/shard_map/ppermute | solution.py:462
  7.5 10.5 %collective-permute-start.2 = (bf16[8,8320]{1,0:T(8,128)(2,1)S(1)}, bf16[8,8320]{1,0:T(8,128)(2,1)S(1)}, u32[]{:S(2)}, u32[]{:S(2)}) collective-permute-start(bf16[8,8320]{1,0:T(8,128)(2,1)S(1)} %get-tuple-element.55), channel_id=1, source_target_pairs={{0,2},{1,13},{2,4},{3,15},{4,6},{5,1},{6,8},{7,3},{8,10},{9,5},{10... | collective-permute-start | bytes 399368 | tf_op jit(solution)/shard_map/ppermute | solution.py:462
  9.1 8.9 %collective-permute-start.3 = (bf16[8,8320]{1,0:T(8,128)(2,1)S(1)}, bf16[8,8320]{1,0:T(8,128)(2,1)S(1)}, u32[]{:S(2)}, u32[]{:S(2)}) collective-permute-start(bf16[8,8320]{1,0:T(8,128)(2,1)S(1)} %get-tuple-element.56), channel_id=1, source_target_pairs={{0,0},{1,15},{2,2},{3,1},{4,4},{5,3},{6,6},{7,5},{8,8},{9,7},{10,1... | collective-permute-start | bytes 399368 | tf_op jit(solution)/shard_map/ppermute | solution.py:462
  15.9 6.3 %copy-start.1 = (s32[16,1]{0,1:T(1,128)S(1)}, s32[16,1]{0,1:T(1,128)}, u32[]{:S(2)}) copy-start(s32[16,1]{0,1:T(1,128)} %param.24) | copy-start | bytes 196
  15.9 6.3 %copy-start.2 = (s32[8]{0:T(128)S(1)}, s32[8]{0:T(128)}, u32[]{:S(2)}) copy-start(s32[8]{0:T(128)} %param.25) | copy-start | bytes 100
  15.9 8.7 %copy-start = (bf16[256,8192]{1,0:T(8,128)(2,1)S(1)}, bf16[256,8192]{1,0:T(8,128)(2,1)}, u32[]{:S(2)}) copy-start(bf16[256,8192]{1,0:T(8,128)(2,1)} %wo_ref) | copy-start | bytes 12582916
  15.9 2.6 %collective-permute-start.4 = (bf16[8,8320]{1,0:T(8,128)(2,1)S(1)}, bf16[8,8320]{1,0:T(8,128)(2,1)S(1)}, u32[]{:S(2)}, u32[]{:S(2)}) collective-permute-start(bf16[8,8320]{1,0:T(8,128)(2,1)S(1)} %collective-permute-done.refs_0_), channel_id=1, source_target_pairs={{0,1},{1,0},{2,3},{3,2},{4,5},{5,4},{6,7},{7,6},{8,9},{9,8},{10,11... | collective-permute-start | bytes 399368 | tf_op jit(solution)/shard_map/ppermute | solution.py:465
  16.3 2.2 %collective-permute-start.5 = (bf16[8,8320]{1,0:T(8,128)(2,1)S(1)}, bf16[8,8320]{1,0:T(8,128)(2,1)S(1)}, u32[]{:S(2)}, u32[]{:S(2)}) collective-permute-start(bf16[8,8320]{1,0:T(8,128)(2,1)S(1)} %collective-permute-done.1.refs_1_), channel_id=1, source_target_pairs={{0,1},{1,0},{2,3},{3,2},{4,5},{5,4},{6,7},{7,6},{8,9},{9,8},{10,11... | collective-permute-start | bytes 399368 | tf_op jit(solution)/shard_map/ppermute | solution.py:465
  18.0 1.4 %collective-permute-start.6 = (bf16[8,8320]{1,0:T(8,128)(2,1)S(1)}, bf16[8,8320]{1,0:T(8,128)(2,1)S(1)}, u32[]{:S(2)}, u32[]{:S(2)}) collective-permute-start(bf16[8,8320]{1,0:T(8,128)(2,1)S(1)} %collective-permute-done.2.refs_2_), channel_id=1, source_target_pairs={{0,1},{1,0},{2,3},{3,2},{4,5},{5,4},{6,7},{7,6},{8,9},{9,8},{10,11... | collective-permute-start | bytes 399368 | tf_op jit(solution)/shard_map/ppermute | solution.py:465
  18.0 1.5 %collective-permute-start.7 = (bf16[8,8320]{1,0:T(8,128)(2,1)S(1)}, bf16[8,8320]{1,0:T(8,128)(2,1)S(1)}, u32[]{:S(2)}, u32[]{:S(2)}) collective-permute-start(bf16[8,8320]{1,0:T(8,128)(2,1)S(1)} %collective-permute-done.3.refs_3_), channel_id=1, source_target_pairs={{0,1},{1,0},{2,3},{3,2},{4,5},{5,4},{6,7},{7,6},{8,9},{9,8},{10,11... | collective-permute-start | bytes 399368 | tf_op jit(solution)/shard_map/ppermute | solution.py:465
  21.6 2.2 %collective-permute-start.9 = (bf16[64,4736]{1,0:T(8,128)(2,1)S(1)}, bf16[64,4736]{1,0:T(8,128)(2,1)S(1)}, u32[]{:S(2)}, u32[]{:S(2)}) collective-permute-start(bf16[64,4736]{1,0:T(8,128)(2,1)S(1)} %get-tuple-element.66.small_ref), channel_id=1, source_target_pairs={{0,1},{1,0},{2,3},{3,2},{4,5},{5,4},{6,7},{7,6},{8,9},{9,8},{10,11... | collective-permute-start | bytes 1818632 | tf_op jit(solution)/shard_map/ppermute | solution.py:476
  22.0 1.8 %collective-permute-start.8 = (f32[16,640]{1,0:T(8,128)S(1)}, f32[16,640]{1,0:T(8,128)S(1)}, u32[]{:S(2)}, u32[]{:S(2)}) collective-permute-start(f32[16,640]{1,0:T(8,128)S(1)} %get-tuple-element.65), channel_id=1, source_target_pairs={{0,1},{1,0},{2,3},{3,2},{4,5},{5,4},{6,7},{7,6},{8,9},{9,8},{10,11... | collective-permute-start | bytes 122888 | tf_op jit(solution)/shard_map/ppermute | solution.py:475
  26.4 7.5 %collective-permute-start.11 = (bf16[8,4096]{1,0:T(8,128)(2,1)S(1)}, bf16[8,4096]{1,0:T(8,128)(2,1)S(1)}, u32[]{:S(2)}, u32[]{:S(2)}) collective-permute-start(bf16[8,4096]{1,0:T(8,128)(2,1)S(1)} %get-tuple-element.73), channel_id=1, source_target_pairs={{6,0},{9,1},{8,2},{11,3},{10,4},{13,5},{12,6},{15,7},{14,8},{1,9},... | collective-permute-start | bytes 196616 | tf_op jit(solution)/shard_map/ppermute | solution.py:492
  29.7 5.7 %collective-permute-start.12 = (bf16[8,4096]{1,0:T(8,128)(2,1)S(1)}, bf16[8,4096]{1,0:T(8,128)(2,1)S(1)}, u32[]{:S(2)}, u32[]{:S(2)}) collective-permute-start(bf16[8,4096]{1,0:T(8,128)(2,1)S(1)} %get-tuple-element.74), channel_id=1, source_target_pairs={{4,0},{11,1},{6,2},{13,3},{8,4},{15,5},{10,6},{1,7},{12,8},{3,9},{... | collective-permute-start | bytes 196616 | tf_op jit(solution)/shard_map/ppermute | solution.py:492
  31.2 5.4 %collective-permute-start.13 = (bf16[8,4096]{1,0:T(8,128)(2,1)S(1)}, bf16[8,4096]{1,0:T(8,128)(2,1)S(1)}, u32[]{:S(2)}, u32[]{:S(2)}) collective-permute-start(bf16[8,4096]{1,0:T(8,128)(2,1)S(1)} %get-tuple-element.75), channel_id=1, source_target_pairs={{2,0},{13,1},{4,2},{15,3},{6,4},{1,5},{8,6},{3,7},{10,8},{5,9},{12... | collective-permute-start | bytes 196616 | tf_op jit(solution)/shard_map/ppermute | solution.py:492
  33.2 3.5 %collective-permute-start.14 = (bf16[8,4096]{1,0:T(8,128)(2,1)S(1)}, bf16[8,4096]{1,0:T(8,128)(2,1)S(1)}, u32[]{:S(2)}, u32[]{:S(2)}) collective-permute-start(bf16[8,4096]{1,0:T(8,128)(2,1)S(1)} %get-tuple-element.76), channel_id=1, source_target_pairs={{0,0},{15,1},{2,2},{1,3},{4,4},{3,5},{6,6},{5,7},{8,8},{7,9},{10,1... | collective-permute-start | bytes 196616 | tf_op jit(solution)/shard_map/ppermute | solution.py:492
  33.8 5.5 %collective-permute-start.15 = (bf16[8,4096]{1,0:T(8,128)(2,1)S(1)}, bf16[8,4096]{1,0:T(8,128)(2,1)S(1)}, u32[]{:S(2)}, u32[]{:S(2)}) collective-permute-start(bf16[8,4096]{1,0:T(8,128)(2,1)S(1)} %collective-permute-done.11.refs_0_), channel_id=1, source_target_pairs={{0,1},{1,0},{2,3},{3,2},{4,5},{5,4},{6,7},{7,6},{8,9},{9,8},{10,11... | collective-permute-start | bytes 196616 | tf_op jit(solution)/shard_map/ppermute | solution.py:495
  35.4 3.9 %collective-permute-start.16 = (bf16[8,4096]{1,0:T(8,128)(2,1)S(1)}, bf16[8,4096]{1,0:T(8,128)(2,1)S(1)}, u32[]{:S(2)}, u32[]{:S(2)}) collective-permute-start(bf16[8,4096]{1,0:T(8,128)(2,1)S(1)} %collective-permute-done.12.refs_1_), channel_id=1, source_target_pairs={{0,1},{1,0},{2,3},{3,2},{4,5},{5,4},{6,7},{7,6},{8,9},{9,8},{10,11... | collective-permute-start | bytes 196616 | tf_op jit(solution)/shard_map/ppermute | solution.py:495
  36.6 2.7 %collective-permute-start.17 = (bf16[8,4096]{1,0:T(8,128)(2,1)S(1)}, bf16[8,4096]{1,0:T(8,128)(2,1)S(1)}, u32[]{:S(2)}, u32[]{:S(2)}) collective-permute-start(bf16[8,4096]{1,0:T(8,128)(2,1)S(1)} %collective-permute-done.13.refs_2_), channel_id=1, source_target_pairs={{0,1},{1,0},{2,3},{3,2},{4,5},{5,4},{6,7},{7,6},{8,9},{9,8},{10,11... | collective-permute-start | bytes 196616 | tf_op jit(solution)/shard_map/ppermute | solution.py:495
  36.7 3.6 %collective-permute-start.18 = (bf16[8,4096]{1,0:T(8,128)(2,1)S(1)}, bf16[8,4096]{1,0:T(8,128)(2,1)S(1)}, u32[]{:S(2)}, u32[]{:S(2)}) collective-permute-start(bf16[8,4096]{1,0:T(8,128)(2,1)S(1)} %collective-permute-done.14.refs_3_), channel_id=1, source_target_pairs={{0,1},{1,0},{2,3},{3,2},{4,5},{5,4},{6,7},{7,6},{8,9},{9,8},{10,11... | collective-permute-start | bytes 196616 | tf_op jit(solution)/shard_map/ppermute | solution.py:495

commit v7 on v6

--- a/solution.py
+++ b/solution.py
@@ -130,7 +130,7 @@
     return jnp.concatenate([block[:, columns] for block in blocks], axis=0)
 
 
-def stage_kernel(wq_hbm, wk_hbm, wv_hbm, down_hbm, up_hbm, kv_up_hbm, out_down_hbm, out_up_hbm, wq_ref, kv_ref, down_ref, small_ref, up_ref, kv_up_ref, out_down_ref, sems):
+def stage_kernel(wq_hbm, wk_hbm, wv_hbm, down_hbm, up_hbm, kv_up_hbm, out_down_hbm, out_up_hbm, wq_ref, narrow_ref, small_ref, up_ref, kv_up_ref, out_down_ref, sems):
     width = wq_hbm.shape[0]
     hcols = wk_hbm.shape[0]
     ranks = down_hbm.shape[0]
@@ -139,8 +139,6 @@
         (up_hbm, up_ref),
         (kv_up_hbm, kv_up_ref),
         (out_down_hbm, out_down_ref),
-        (wk_hbm, kv_ref.at[0:hcols, :]),
-        (wv_hbm, kv_ref.at[hcols:, :]),
         (out_up_hbm, small_ref.at[:, 0 : out_up_hbm.shape[1]]),
     ]
     for n in range(pieces):
@@ -148,7 +146,11 @@
         pairs.append((wq_hbm.at[rows, :], wq_ref.at[rows, :]))
     for n in range(2):
         rows = pl.ds(n * (ranks // 2), ranks // 2)
-        pairs.append((down_hbm.at[rows, :], down_ref.at[rows, :]))
+        pairs.append((down_hbm.at[rows, :], narrow_ref.at[pl.ds(4 * hcols + n * (ranks // 2), ranks // 2), :]))
+        columns = pl.ds(n * (width // 2), width // 2)
+        for m, source in enumerate((wk_hbm, wv_hbm)):
+            target = narrow_ref.at[pl.ds((2 * n + m) * hcols, hcols), :]
+            pairs.append((source.at[:, columns], target))
     copies = copy_all(pairs, sems)
     for copy in copies[:3]:
         copy.wait()
@@ -161,17 +163,22 @@
 
 def project_kernel(count, *refs):
     blocks = refs[: 2 * count]
-    wq_ref, kv_ref, down_ref, mine_ref, theirs_ref, sums_ref = refs[2 * count :]
+    wq_ref, narrow_ref, mine_ref, theirs_ref, sums_ref = refs[2 * count :]
     width = wq_ref.shape[0]
-    half = down_ref.shape[1]
+    half = narrow_ref.shape[1]
     slots = mine_ref.shape[0]
     rows = sums_ref.shape[1]
+    kvcols = LANES
     x_all = stacked(blocks, slice(0, width))
-    halves = [x_all[:, :half], x_all[:, half:]]
-    x_half = jnp.where(lax.axis_index("tensor") == 0, halves[0], halves[1])
-    ranks = nt(x_half, down_ref[...])
+    narrow = nt(jnp.concatenate([x_all[:, :half], x_all[:, half:]], axis=0), narrow_ref[...])
+    early, late = narrow[:rows], narrow[rows:]
+    ranks = jnp.where(lax.axis_index("tensor") == 0, early[:, 2 * kvcols :], late[:, 2 * kvcols :])
     spare = jnp.zeros((rows, -ranks.shape[1] % LANES), F32)
-    sums = [nn(x_all, wq_ref[...]), nt(x_all, kv_ref[...]), jnp.concatenate([ranks, spare], axis=1)]
+    sums = [
+        nn(x_all, wq_ref[...]),
+        early[:, :kvcols] + late[:, kvcols : 2 * kvcols],
+        jnp.concatenate([ranks, spare], axis=1),
+    ]
     tile = 0
     for part in sums:
         for c in range(0, part.shape[1], LANES):
@@ -429,15 +436,14 @@
         stage_kernel,
         [
             shape(query_projection.shape, BF16),
-            shape((kvcols, width), BF16),
-            shape(down.shape, BF16),
+            shape((2 * kvcols + down.shape[0], half), BF16),
             shape((rank, half + qcols + 2 * hcols + hrows), BF16),
         ],
         [
             pltpu.VMEM((rank, qcols), BF16),
             pltpu.VMEM((2, rank, hcols), BF16),
             pltpu.VMEM((rank, hrows), BF16),
-            pltpu.SemaphoreType.DMA((12,)),
+            pltpu.SemaphoreType.DMA((14,)),
         ],
         outside=range(8),
         moved=2 * (query_projection.size + kvcols * width + down.size),
@@ -492,7 +498,10 @@
         lax.ppermute(one, ("adapter", "tensor"), [(b, a) for a, b in onward(n)])
         for n, one in enumerate(finished)
     ]
-    returned += [lax.ppermute(one, "tensor", SWAP) for one in returned]
+    waited = list(returned)
+    for n in reversed(range(count - 1)):
+        waited[n] = lax.optimization_barrier((returned[n], returned[n + 1]))[0]
+    returned += [lax.ppermute(one, "tensor", SWAP) for one in waited]
     return call(pick_kernel, shape((requests, half), BF16))(place, *returned)
 
 

time: 41.3 us -> 40.5 us (0.981)
  starting transfers between devices: 20.3 us -> 19.6 us
    ppermute x4, starting transfers between devices: 7.45 us -> 6.65 us  [body(): lax.ppermute(one, ('adapter', 'tensor'), [(b, a) for a, b in onward(n)])]
    ppermute x4, waiting for transfers between devices: 2.17 us -> 1.49 us  [body(): lax.ppermute(one, ('adapter', 'tensor'), [(b, a) for a, b in onward(n)])]
  transfers between devices with their start and end apart: 19 -> 19, of which waited for: 8 -> 10; matrix products, arithmetic and copies ran while one was open for 0% -> 0% of each run, Pallas kernels for 16% -> 16%
where the time goes in v7:
time: 40.5 us; the launch traced here: 39.9 us
  starting transfers between devices  19.6 us (48%)
  Pallas kernels  11 us (27%)
  waiting for transfers between devices  9.2 us (23%)
    pallas_call x7, Pallas kernels, call(): pl.pallas_call(kernel, out_shape=outs, in_specs=[OUTSIDE if i in outside...  11 us
    ppermute x4, starting transfers between devices, body(): lax.ppermute(one, ('adapter', 'tensor'), onward(n))  7.35 us
    ppermute x4, starting transfers between devices, body(): lax.ppermute(one, ('adapter', 'tensor'), [(b, a) for a, b in onward(n)])  6.65 us
    ppermute x4, waiting for transfers between devices, body(): lax.ppermute(one, ('adapter', 'tensor'), onward(n))  4.15 us
    ppermute x4, starting transfers between devices, body(): returned += [lax.ppermute(one, 'tensor', SWAP) for one in waited]  3.5 us
    ppermute x4, waiting for transfers between devices, body(): lax.ppermute(one, ('adapter', 'tensor'), [(b, a) for a, b in onward(n)])  1.49 us
    ppermute x1, waiting for transfers between devices, body(): theirs = lax.ppermute(theirs, 'tensor', SWAP)  1.29 us
    ppermute x4, waiting for transfers between devices, body(): returned += [lax.ppermute(one, 'tensor', SWAP) for one in waited]  1.25 us
  transfers between devices with their start and end apart: 19, of which 10 were waited for; matrix products, arithmetic and copies ran while one was open for 0% of the time, Pallas kernels for 16%

profile of v7, /device:TPU:0, one launch (start us, length us, event | category | flops | bytes accessed | tf_op | source)
XLA Modules:
  0.0 39.9 jit_solution(234082229651350405)
XLA Ops:
  0.0 1.8 %shard_map.154 = (bf16[8,8320]{1,0:T(8,128)(2,1)S(1)}, bf16[8,8320]{1,0:T(8,128)(2,1)S(1)}, bf16[8,8320]{1,0:T(8,128)(2,1)S(1)}, bf16[8,8320]{1,0:T(8,128)(2,1)S(1)}) custom-call(bf16[16,8192]{1,0:T(8,128)(2,1)} %x_hbm.1, f32[1,8192]{1,0:T(1,128)} %bitcast.30, bf16[512,128]{1,0:T(8,128)(2,1)} %bitcast.25, bf16[512,128]{1,0:T(8,128)(2,1)} %bitcast.26, ...), custom_call_target="tpu_custom_call" | custom-call | tf_op jit(solution)/shard_map/pallas_call | solution.py:353
  1.8 0.5 %collective-permute-start.10 = (bf16[256,8192]{1,0:T(8,128)(2,1)}, bf16[256,8192]{1,0:T(8,128)(2,1)S(1)}, u32[]{:S(2)}, u32[]{:S(2)}) collective-permute-start(bf16[256,8192]{1,0:T(8,128)(2,1)} %wo_ref), channel_id=1, source_target_pairs={{0,1},{1,0},{2,3},{3,2},{4,5},{5,4},{6,7},{7,6},{8,9},{9,8},{10,11... | collective-permute-start | bytes 12582920 | tf_op jit(solution)/shard_map/ppermute | solution.py:472
  2.4 3.6 %collective-permute-start = (bf16[8,8320]{1,0:T(8,128)(2,1)S(1)}, bf16[8,8320]{1,0:T(8,128)(2,1)S(1)}, u32[]{:S(2)}, u32[]{:S(2)}) collective-permute-start(bf16[8,8320]{1,0:T(8,128)(2,1)S(1)} %get-tuple-element.46), channel_id=1, source_target_pairs={{0,6},{1,9},{2,8},{3,11},{4,10},{5,13},{6,12},{7,15},{8,14},{9,1},... | collective-permute-start | bytes 399368 | tf_op jit(solution)/shard_map/ppermute | solution.py:468
  5.9 1.6 %collective-permute-start.1 = (bf16[8,8320]{1,0:T(8,128)(2,1)S(1)}, bf16[8,8320]{1,0:T(8,128)(2,1)S(1)}, u32[]{:S(2)}, u32[]{:S(2)}) collective-permute-start(bf16[8,8320]{1,0:T(8,128)(2,1)S(1)} %get-tuple-element.54), channel_id=1, source_target_pairs={{0,4},{1,11},{2,6},{3,13},{4,8},{5,15},{6,10},{7,1},{8,12},{9,3},{... | collective-permute-start | bytes 399368 | tf_op jit(solution)/shard_map/ppermute | solution.py:468
  7.5 1.5 %collective-permute-start.2 = (bf16[8,8320]{1,0:T(8,128)(2,1)S(1)}, bf16[8,8320]{1,0:T(8,128)(2,1)S(1)}, u32[]{:S(2)}, u32[]{:S(2)}) collective-permute-start(bf16[8,8320]{1,0:T(8,128)(2,1)S(1)} %get-tuple-element.55), channel_id=1, source_target_pairs={{0,2},{1,13},{2,4},{3,15},{4,6},{5,1},{6,8},{7,3},{8,10},{9,5},{10... | collective-permute-start | bytes 399368 | tf_op jit(solution)/shard_map/ppermute | solution.py:468
  9.1 0.7 %collective-permute-start.3 = (bf16[8,8320]{1,0:T(8,128)(2,1)S(1)}, bf16[8,8320]{1,0:T(8,128)(2,1)S(1)}, u32[]{:S(2)}, u32[]{:S(2)}) collective-permute-start(bf16[8,8320]{1,0:T(8,128)(2,1)S(1)} %get-tuple-element.56), channel_id=1, source_target_pairs={{0,0},{1,15},{2,2},{3,1},{4,4},{5,3},{6,6},{7,5},{8,8},{9,7},{10,1... | collective-permute-start | bytes 399368 | tf_op jit(solution)/shard_map/ppermute | solution.py:468
  9.7 3.6 %shard_map.155 = (bf16[8192,256]{1,0:T(8,128)(2,1)S(1)}, bf16[448,4096]{1,0:T(8,128)(2,1)S(1)}, bf16[64,4736]{1,0:T(8,128)(2,1)S(1)}) custom-call(bf16[8192,256]{1,0:T(8,128)(2,1)} %wq_hbm, bf16[64,8192]{1,0:T(8,128)(2,1)} %bitcast.22, bf16[64,8192]{1,0:T(8,128)(2,1)} %bitcast.23, bf16[192,4096]{1,0:T(8,128)(2,1)} %bitcast.21, bf16[64,256]{1,0:T(8,128)(2,1)} %bitcast.27, ...), custom_call_target="tpu_custom_call" | custom-call | bytes 7864320 | tf_op jit(solution)/shard_map/pallas_call | solution.py:353
  13.3 2.6 %collective-permute-done.refs_0_ = bf16[8,8320]{1,0:T(8,128)(2,1)S(1)} collective-permute-done((bf16[8,8320]{1,0:T(8,128)(2,1)S(1)}, bf16[8,8320]{1,0:T(8,128)(2,1)S(1)}, u32[]{:S(2)}, u32[]{:S(2)}) %collective-permute-start) | collective-permute-done | bytes 133152 | tf_op jit(solution)/shard_map/ppermute | solution.py:468
  15.9 0.4 %collective-permute-start.4 = (bf16[8,8320]{1,0:T(8,128)(2,1)S(1)}, bf16[8,8320]{1,0:T(8,128)(2,1)S(1)}, u32[]{:S(2)}, u32[]{:S(2)}) collective-permute-start(bf16[8,8320]{1,0:T(8,128)(2,1)S(1)} %collective-permute-done.refs_0_), channel_id=1, source_target_pairs={{0,1},{1,0},{2,3},{3,2},{4,5},{5,4},{6,7},{7,6},{8,9},{9,8},{10,11... | collective-permute-start | bytes 399368 | tf_op jit(solution)/shard_map/ppermute | solution.py:471
  16.3 0.0 collective-permute-done.1.refs_1_
  16.3 0.1 collective-permute-start.5
  16.4 1.6 %collective-permute-done.2.refs_2_ = bf16[8,8320]{1,0:T(8,128)(2,1)S(1)} collective-permute-done((bf16[8,8320]{1,0:T(8,128)(2,1)S(1)}, bf16[8,8320]{1,0:T(8,128)(2,1)S(1)}, u32[]{:S(2)}, u32[]{:S(2)}) %collective-permute-start.2) | collective-permute-done | bytes 133152 | tf_op jit(solution)/shard_map/ppermute | solution.py:468
  18.0 0.0 collective-permute-start.6
  18.0 0.0 collective-permute-done.3.refs_3_
  18.0 0.5 %collective-permute-start.7 = (bf16[8,8320]{1,0:T(8,128)(2,1)S(1)}, bf16[8,8320]{1,0:T(8,128)(2,1)S(1)}, u32[]{:S(2)}, u32[]{:S(2)}) collective-permute-start(bf16[8,8320]{1,0:T(8,128)(2,1)S(1)} %collective-permute-done.3.refs_3_), channel_id=1, source_target_pairs={{0,1},{1,0},{2,3},{3,2},{4,5},{5,4},{6,7},{7,6},{8,9},{9,8},{10,11... | collective-permute-start | bytes 399368 | tf_op jit(solution)/shard_map/ppermute | solution.py:471
  18.5 0.0 collective-permute-done.4.refs_4_
  18.5 0.0 collective-permute-done.5.refs_5_
  18.5 0.8 %collective-permute-done.6.refs_6_ = bf16[8,8320]{1,0:T(8,128)(2,1)S(1)} collective-permute-done((bf16[8,8320]{1,0:T(8,128)(2,1)S(1)}, bf16[8,8320]{1,0:T(8,128)(2,1)S(1)}, u32[]{:S(2)}, u32[]{:S(2)}) %collective-permute-start.6) | collective-permute-done | bytes 133152 | tf_op jit(solution)/shard_map/ppermute | solution.py:471
  19.3 0.2 collective-permute-done.7.refs_7_
  19.5 1.9 %shard_map.157 = (f32[16,640]{1,0:T(8,128)S(1)}, f32[16,640]{1,0:T(8,128)S(1)}) custom-call(bf16[8,8320]{1,0:T(8,128)(2,1)S(1)} %collective-permute-done.refs_0_, bf16[8,8320]{1,0:T(8,128)(2,1)S(1)} %collective-permute-done.1.refs_1_, bf16[8,8320]{1,0:T(8,128)(2,1)S(1)} %collective-permute-done.2.refs_2_, ...), custom_call_target="tpu_custom_call" | custom-call | tf_op jit(solution)/shard_map/pallas_call | solution.py:353
  21.4 0.4 collective-permute-start.9
  21.8 0.2 collective-permute-start.8
  21.9 0.0 copy-done.1
  21.9 0.0 copy-done.2
  22.0 0.3 shard_map.156
  22.2 1.3 %collective-permute-done.8.theirs_ref = f32[16,640]{1,0:T(8,128)S(1)} collective-permute-done((f32[16,640]{1,0:T(8,128)S(1)}, f32[16,640]{1,0:T(8,128)S(1)}, u32[]{:S(2)}, u32[]{:S(2)}) %collective-permute-start.8) | collective-permute-done | bytes 40992 | tf_op jit(solution)/shard_map/ppermute | solution.py:481
  23.5 0.0 collective-permute-done.9.small_other_ref
  23.5 0.9 %shard_map.158.attended_ref = bf16[16,512]{1,0:T(8,128)(2,1)S(1)} custom-call(f32[16,640]{1,0:T(8,128)S(1)} %get-tuple-element.63.mine_ref, f32[16,640]{1,0:T(8,128)S(1)} %collective-permute-done.8.theirs_ref, bf16[64,4736]{1,0:T(8,128)(2,1)S(1)} %get-tuple-element.65.small_ref, bf16[64,4736]{1,0:T(8,128)(2,1)S(1)} %collective-permute-done.9.small_other_ref, ...), custom_call_target="tpu_custom_call" | custom-call | tf_op jit(solution)/shard_map/pallas_call | solution.py:353
  24.4 0.0 collective-permute-done.10.wo_other_ref
  24.4 0.0 copy-done
  24.4 1.7 %shard_map.159 = (bf16[8,4096]{1,0:T(8,128)(2,1)S(1)}, bf16[8,4096]{1,0:T(8,128)(2,1)S(1)}, bf16[8,4096]{1,0:T(8,128)(2,1)S(1)}, bf16[8,4096]{1,0:T(8,128)(2,1)S(1)}) custom-call(bf16[16,512]{1,0:T(8,128)(2,1)S(1)} %shard_map.158.attended_ref, bf16[256,8192]{1,0:T(8,128)(2,1)S(1)} %copy-done, bf16[256,8192]{1,0:T(8,128)(2,1)S(1)} %collective-permute-done.10.wo_other_ref, ...), custom_call_target="tpu_custom_call" | custom-call | tf_op jit(solution)/shard_map/pallas_call | solution.py:353
  26.2 5.0 %collective-permute-start.13 = (bf16[8,4096]{1,0:T(8,128)(2,1)S(1)}, bf16[8,4096]{1,0:T(8,128)(2,1)S(1)}, u32[]{:S(2)}, u32[]{:S(2)}) collective-permute-start(bf16[8,4096]{1,0:T(8,128)(2,1)S(1)} %get-tuple-element.74), channel_id=1, source_target_pairs={{2,0},{13,1},{4,2},{15,3},{6,4},{1,5},{8,6},{3,7},{10,8},{5,9},{12... | collective-permute-start | bytes 196616 | tf_op jit(solution)/shard_map/ppermute | solution.py:498
  31.1 0.7 %collective-permute-start.14 = (bf16[8,4096]{1,0:T(8,128)(2,1)S(1)}, bf16[8,4096]{1,0:T(8,128)(2,1)S(1)}, u32[]{:S(2)}, u32[]{:S(2)}) collective-permute-start(bf16[8,4096]{1,0:T(8,128)(2,1)S(1)} %get-tuple-element.75), channel_id=1, source_target_pairs={{0,0},{15,1},{2,2},{1,3},{4,4},{3,5},{6,6},{5,7},{8,8},{7,9},{10,1... | collective-permute-start | bytes 196616 | tf_op jit(solution)/shard_map/ppermute | solution.py:498
  31.8 0.1 collective-permute-start.12
  31.9 1.0 %collective-permute-start.11 = (bf16[8,4096]{1,0:T(8,128)(2,1)S(1)}, bf16[8,4096]{1,0:T(8,128)(2,1)S(1)}, u32[]{:S(2)}, u32[]{:S(2)}) collective-permute-start(bf16[8,4096]{1,0:T(8,128)(2,1)S(1)} %get-tuple-element.72), channel_id=1, source_target_pairs={{6,0},{9,1},{8,2},{11,3},{10,4},{13,5},{12,6},{15,7},{14,8},{1,9},... | collective-permute-start | bytes 196616 | tf_op jit(solution)/shard_map/ppermute | solution.py:498
  32.8 0.2 collective-permute-done.13.refs_2_
  33.1 0.0 collective-permute-done.14.refs_3_
  33.1 2.7 %collective-permute-start.17 = (bf16[8,4096]{1,0:T(8,128)(2,1)S(1)}, bf16[8,4096]{1,0:T(8,128)(2,1)S(1)}, u32[]{:S(2)}, u32[]{:S(2)}) collective-permute-start(bf16[8,4096]{1,0:T(8,128)(2,1)S(1)} %collective-permute-done.13.refs_2_), channel_id=1, source_target_pairs={{0,1},{1,0},{2,3},{3,2},{4,5},{5,4},{6,7},{7,6},{8,9},{9,8},{10,11... | collective-permute-start | bytes 196616 | tf_op jit(solution)/shard_map/ppermute | solution.py:504
  35.7 0.4 %collective-permute-done.12.refs_1_ = bf16[8,4096]{1,0:T(8,128)(2,1)S(1)} collective-permute-done((bf16[8,4096]{1,0:T(8,128)(2,1)S(1)}, bf16[8,4096]{1,0:T(8,128)(2,1)S(1)}, u32[]{:S(2)}, u32[]{:S(2)}) %collective-permute-start.12) | collective-permute-done | bytes 65568 | tf_op jit(solution)/shard_map/ppermute | solution.py:498
  36.1 0.2 collective-permute-start.16
  36.4 0.9 %collective-permute-done.11.refs_0_ = bf16[8,4096]{1,0:T(8,128)(2,1)S(1)} collective-permute-done((bf16[8,4096]{1,0:T(8,128)(2,1)S(1)}, bf16[8,4096]{1,0:T(8,128)(2,1)S(1)}, u32[]{:S(2)}, u32[]{:S(2)}) %collective-permute-start.11) | collective-permute-done | bytes 65568 | tf_op jit(solution)/shard_map/ppermute | solution.py:498
  37.2 0.6 %collective-permute-start.15 = (bf16[8,4096]{1,0:T(8,128)(2,1)S(1)}, bf16[8,4096]{1,0:T(8,128)(2,1)S(1)}, u32[]{:S(2)}, u32[]{:S(2)}) collective-permute-start(bf16[8,4096]{1,0:T(8,128)(2,1)S(1)} %collective-permute-done.11.refs_0_), channel_id=1, source_target_pairs={{0,1},{1,0},{2,3},{3,2},{4,5},{5,4},{6,7},{7,6},{8,9},{9,8},{10,11... | collective-permute-start | bytes 196616 | tf_op jit(solution)/shard_map/ppermute | solution.py:504
  37.8 0.0 collective-permute-start.18
  37.8 0.0 collective-permute-done.17.refs_6_
  37.8 0.0 collective-permute-done.16.refs_5_
  37.8 0.9 %collective-permute-done.15.refs_4_ = bf16[8,4096]{1,0:T(8,128)(2,1)S(1)} collective-permute-done((bf16[8,4096]{1,0:T(8,128)(2,1)S(1)}, bf16[8,4096]{1,0:T(8,128)(2,1)S(1)}, u32[]{:S(2)}, u32[]{:S(2)}) %collective-permute-start.15) | collective-permute-done | bytes 65568 | tf_op jit(solution)/shard_map/ppermute | solution.py:504
  38.7 0.4 collective-permute-done.18.refs_7_
  39.1 0.9 %shard_map.160 = bf16[16,4096]{1,0:T(8,128)(2,1)} custom-call(bf16[16,64]{1,0:T(8,128)(2,1)S(1)} %get-tuple-element.57.place_ref, bf16[8,4096]{1,0:T(8,128)(2,1)S(1)} %collective-permute-done.11.refs_0_, bf16[8,4096]{1,0:T(8,128)(2,1)S(1)} %collective-permute-done.12.refs_1_, bf16[8,4096]{1,0:T(8,128)(2,1)S(1)} %collective-permute-done.13.refs_2_, ...), custom_call_target="tpu_custom_call" | custom-call | tf_op jit(solution)/shard_map/pallas_call | solution.py:353
  (3 shorter events, 0.0 us)
Async XLA Ops:
  1.8 22.6 %collective-permute-start.10 = (bf16[256,8192]{1,0:T(8,128)(2,1)}, bf16[256,8192]{1,0:T(8,128)(2,1)S(1)}, u32[]{:S(2)}, u32[]{:S(2)}) collective-permute-start(bf16[256,8192]{1,0:T(8,128)(2,1)} %wo_ref), channel_id=1, source_target_pairs={{0,1},{1,0},{2,3},{3,2},{4,5},{5,4},{6,7},{7,6},{8,9},{9,8},{10,11... | collective-permute-start | bytes 12582920 | tf_op jit(solution)/shard_map/ppermute | solution.py:472
  2.4 13.5 %collective-permute-start = (bf16[8,8320]{1,0:T(8,128)(2,1)S(1)}, bf16[8,8320]{1,0:T(8,128)(2,1)S(1)}, u32[]{:S(2)}, u32[]{:S(2)}) collective-permute-start(bf16[8,8320]{1,0:T(8,128)(2,1)S(1)} %get-tuple-element.46), channel_id=1, source_target_pairs={{0,6},{1,9},{2,8},{3,11},{4,10},{5,13},{6,12},{7,15},{8,14},{9,1},... | collective-permute-start | bytes 399368 | tf_op jit(solution)/shard_map/ppermute | solution.py:468
  5.9 10.4 %collective-permute-start.1 = (bf16[8,8320]{1,0:T(8,128)(2,1)S(1)}, bf16[8,8320]{1,0:T(8,128)(2,1)S(1)}, u32[]{:S(2)}, u32[]{:S(2)}) collective-permute-start(bf16[8,8320]{1,0:T(8,128)(2,1)S(1)} %get-tuple-element.54), channel_id=1, source_target_pairs={{0,4},{1,11},{2,6},{3,13},{4,8},{5,15},{6,10},{7,1},{8,12},{9,3},{... | collective-permute-start | bytes 399368 | tf_op jit(solution)/shard_map/ppermute | solution.py:468
  7.5 10.5 %collective-permute-start.2 = (bf16[8,8320]{1,0:T(8,128)(2,1)S(1)}, bf16[8,8320]{1,0:T(8,128)(2,1)S(1)}, u32[]{:S(2)}, u32[]{:S(2)}) collective-permute-start(bf16[8,8320]{1,0:T(8,128)(2,1)S(1)} %get-tuple-element.55), channel_id=1, source_target_pairs={{0,2},{1,13},{2,4},{3,15},{4,6},{5,1},{6,8},{7,3},{8,10},{9,5},{10... | collective-permute-start | bytes 399368 | tf_op jit(solution)/shard_map/ppermute | solution.py:468
  9.1 8.9 %collective-permute-start.3 = (bf16[8,8320]{1,0:T(8,128)(2,1)S(1)}, bf16[8,8320]{1,0:T(8,128)(2,1)S(1)}, u32[]{:S(2)}, u32[]{:S(2)}) collective-permute-start(bf16[8,8320]{1,0:T(8,128)(2,1)S(1)} %get-tuple-element.56), channel_id=1, source_target_pairs={{0,0},{1,15},{2,2},{3,1},{4,4},{5,3},{6,6},{7,5},{8,8},{9,7},{10,1... | collective-permute-start | bytes 399368 | tf_op jit(solution)/shard_map/ppermute | solution.py:468
  15.9 6.1 %copy-start.1 = (s32[16,1]{0,1:T(1,128)S(1)}, s32[16,1]{0,1:T(1,128)}, u32[]{:S(2)}) copy-start(s32[16,1]{0,1:T(1,128)} %param.24) | copy-start | bytes 196
  15.9 6.1 %copy-start.2 = (s32[8]{0:T(128)S(1)}, s32[8]{0:T(128)}, u32[]{:S(2)}) copy-start(s32[8]{0:T(128)} %param.25) | copy-start | bytes 100
  15.9 8.6 %copy-start = (bf16[256,8192]{1,0:T(8,128)(2,1)S(1)}, bf16[256,8192]{1,0:T(8,128)(2,1)}, u32[]{:S(2)}) copy-start(bf16[256,8192]{1,0:T(8,128)(2,1)} %wo_ref) | copy-start | bytes 12582916
  15.9 2.6 %collective-permute-start.4 = (bf16[8,8320]{1,0:T(8,128)(2,1)S(1)}, bf16[8,8320]{1,0:T(8,128)(2,1)S(1)}, u32[]{:S(2)}, u32[]{:S(2)}) collective-permute-start(bf16[8,8320]{1,0:T(8,128)(2,1)S(1)} %collective-permute-done.refs_0_), channel_id=1, source_target_pairs={{0,1},{1,0},{2,3},{3,2},{4,5},{5,4},{6,7},{7,6},{8,9},{9,8},{10,11... | collective-permute-start | bytes 399368 | tf_op jit(solution)/shard_map/ppermute | solution.py:471
  16.3 2.2 %collective-permute-start.5 = (bf16[8,8320]{1,0:T(8,128)(2,1)S(1)}, bf16[8,8320]{1,0:T(8,128)(2,1)S(1)}, u32[]{:S(2)}, u32[]{:S(2)}) collective-permute-start(bf16[8,8320]{1,0:T(8,128)(2,1)S(1)} %collective-permute-done.1.refs_1_), channel_id=1, source_target_pairs={{0,1},{1,0},{2,3},{3,2},{4,5},{5,4},{6,7},{7,6},{8,9},{9,8},{10,11... | collective-permute-start | bytes 399368 | tf_op jit(solution)/shard_map/ppermute | solution.py:471
  18.0 1.4 %collective-permute-start.6 = (bf16[8,8320]{1,0:T(8,128)(2,1)S(1)}, bf16[8,8320]{1,0:T(8,128)(2,1)S(1)}, u32[]{:S(2)}, u32[]{:S(2)}) collective-permute-start(bf16[8,8320]{1,0:T(8,128)(2,1)S(1)} %collective-permute-done.2.refs_2_), channel_id=1, source_target_pairs={{0,1},{1,0},{2,3},{3,2},{4,5},{5,4},{6,7},{7,6},{8,9},{9,8},{10,11... | collective-permute-start | bytes 399368 | tf_op jit(solution)/shard_map/ppermute | solution.py:471
  18.0 1.5 %collective-permute-start.7 = (bf16[8,8320]{1,0:T(8,128)(2,1)S(1)}, bf16[8,8320]{1,0:T(8,128)(2,1)S(1)}, u32[]{:S(2)}, u32[]{:S(2)}) collective-permute-start(bf16[8,8320]{1,0:T(8,128)(2,1)S(1)} %collective-permute-done.3.refs_3_), channel_id=1, source_target_pairs={{0,1},{1,0},{2,3},{3,2},{4,5},{5,4},{6,7},{7,6},{8,9},{9,8},{10,11... | collective-permute-start | bytes 399368 | tf_op jit(solution)/shard_map/ppermute | solution.py:471
  21.4 2.2 %collective-permute-start.9 = (bf16[64,4736]{1,0:T(8,128)(2,1)S(1)}, bf16[64,4736]{1,0:T(8,128)(2,1)S(1)}, u32[]{:S(2)}, u32[]{:S(2)}) collective-permute-start(bf16[64,4736]{1,0:T(8,128)(2,1)S(1)} %get-tuple-element.65.small_ref), channel_id=1, source_target_pairs={{0,1},{1,0},{2,3},{3,2},{4,5},{5,4},{6,7},{7,6},{8,9},{9,8},{10,11... | collective-permute-start | bytes 1818632 | tf_op jit(solution)/shard_map/ppermute | solution.py:482
  21.8 1.8 %collective-permute-start.8 = (f32[16,640]{1,0:T(8,128)S(1)}, f32[16,640]{1,0:T(8,128)S(1)}, u32[]{:S(2)}, u32[]{:S(2)}) collective-permute-start(f32[16,640]{1,0:T(8,128)S(1)} %get-tuple-element.64), channel_id=1, source_target_pairs={{0,1},{1,0},{2,3},{3,2},{4,5},{5,4},{6,7},{7,6},{8,9},{9,8},{10,11... | collective-permute-start | bytes 122888 | tf_op jit(solution)/shard_map/ppermute | solution.py:481
  26.2 6.9 %collective-permute-start.13 = (bf16[8,4096]{1,0:T(8,128)(2,1)S(1)}, bf16[8,4096]{1,0:T(8,128)(2,1)S(1)}, u32[]{:S(2)}, u32[]{:S(2)}) collective-permute-start(bf16[8,4096]{1,0:T(8,128)(2,1)S(1)} %get-tuple-element.74), channel_id=1, source_target_pairs={{2,0},{13,1},{4,2},{15,3},{6,4},{1,5},{8,6},{3,7},{10,8},{5,9},{12... | collective-permute-start | bytes 196616 | tf_op jit(solution)/shard_map/ppermute | solution.py:498
  31.1 1.9 %collective-permute-start.14 = (bf16[8,4096]{1,0:T(8,128)(2,1)S(1)}, bf16[8,4096]{1,0:T(8,128)(2,1)S(1)}, u32[]{:S(2)}, u32[]{:S(2)}) collective-permute-start(bf16[8,4096]{1,0:T(8,128)(2,1)S(1)} %get-tuple-element.75), channel_id=1, source_target_pairs={{0,0},{15,1},{2,2},{1,3},{4,4},{3,5},{6,6},{5,7},{8,8},{7,9},{10,1... | collective-permute-start | bytes 196616 | tf_op jit(solution)/shard_map/ppermute | solution.py:498
  31.8 4.3 %collective-permute-start.12 = (bf16[8,4096]{1,0:T(8,128)(2,1)S(1)}, bf16[8,4096]{1,0:T(8,128)(2,1)S(1)}, u32[]{:S(2)}, u32[]{:S(2)}) collective-permute-start(bf16[8,4096]{1,0:T(8,128)(2,1)S(1)} %get-tuple-element.73), channel_id=1, source_target_pairs={{4,0},{11,1},{6,2},{13,3},{8,4},{15,5},{10,6},{1,7},{12,8},{3,9},{... | collective-permute-start | bytes 196616 | tf_op jit(solution)/shard_map/ppermute | solution.py:498
  31.9 5.3 %collective-permute-start.11 = (bf16[8,4096]{1,0:T(8,128)(2,1)S(1)}, bf16[8,4096]{1,0:T(8,128)(2,1)S(1)}, u32[]{:S(2)}, u32[]{:S(2)}) collective-permute-start(bf16[8,4096]{1,0:T(8,128)(2,1)S(1)} %get-tuple-element.72), channel_id=1, source_target_pairs={{6,0},{9,1},{8,2},{11,3},{10,4},{13,5},{12,6},{15,7},{14,8},{1,9},... | collective-permute-start | bytes 196616 | tf_op jit(solution)/shard_map/ppermute | solution.py:498
  33.1 4.8 %collective-permute-start.17 = (bf16[8,4096]{1,0:T(8,128)(2,1)S(1)}, bf16[8,4096]{1,0:T(8,128)(2,1)S(1)}, u32[]{:S(2)}, u32[]{:S(2)}) collective-permute-start(bf16[8,4096]{1,0:T(8,128)(2,1)S(1)} %collective-permute-done.13.refs_2_), channel_id=1, source_target_pairs={{0,1},{1,0},{2,3},{3,2},{4,5},{5,4},{6,7},{7,6},{8,9},{9,8},{10,11... | collective-permute-start | bytes 196616 | tf_op jit(solution)/shard_map/ppermute | solution.py:504
  36.1 1.7 %collective-permute-start.16 = (bf16[8,4096]{1,0:T(8,128)(2,1)S(1)}, bf16[8,4096]{1,0:T(8,128)(2,1)S(1)}, u32[]{:S(2)}, u32[]{:S(2)}) collective-permute-start(bf16[8,4096]{1,0:T(8,128)(2,1)S(1)} %collective-permute-done.12.refs_1_), channel_id=1, source_target_pairs={{0,1},{1,0},{2,3},{3,2},{4,5},{5,4},{6,7},{7,6},{8,9},{9,8},{10,11... | collective-permute-start | bytes 196616 | tf_op jit(solution)/shard_map/ppermute | solution.py:504
  37.2 1.5 %collective-permute-start.15 = (bf16[8,4096]{1,0:T(8,128)(2,1)S(1)}, bf16[8,4096]{1,0:T(8,128)(2,1)S(1)}, u32[]{:S(2)}, u32[]{:S(2)}) collective-permute-start(bf16[8,4096]{1,0:T(8,128)(2,1)S(1)} %collective-permute-done.11.refs_0_), channel_id=1, source_target_pairs={{0,1},{1,0},{2,3},{3,2},{4,5},{5,4},{6,7},{7,6},{8,9},{9,8},{10,11... | collective-permute-start | bytes 196616 | tf_op jit(solution)/shard_map/ppermute | solution.py:504
  37.8 1.3 %collective-permute-start.18 = (bf16[8,4096]{1,0:T(8,128)(2,1)S(1)}, bf16[8,4096]{1,0:T(8,128)(2,1)S(1)}, u32[]{:S(2)}, u32[]{:S(2)}) collective-permute-start(bf16[8,4096]{1,0:T(8,128)(2,1)S(1)} %collective-permute-done.14.refs_3_), channel_id=1, source_target_pairs={{0,1},{1,0},{2,3},{3,2},{4,5},{5,4},{6,7},{7,6},{8,9},{9,8},{10,11... | collective-permute-start | bytes 196616 | tf_op jit(solution)/shard_map/ppermute | solution.py:504
